TPU v7x, 128 devices: a whole 4x4x4 slice. The times are simulated.
128 devices in a mesh: ctx: 16 (over z_hi, x, core), fsdp: 8 (over z_lo, y).
Axes of the slice: x: 4, y: 4, z: 4 (z_hi: 2, z_lo: 2; z = z_hi * 2 + z_lo), core: 2. Of those that a mesh axis runs over, the one named last changes fastest.
Arguments:
- layer_input: bfloat16 [8, 2048, 1536], P('fsdp', 'ctx'), may hold values from -6 to 6
- segments: int32 [8, 2048], P('fsdp', 'ctx'), may hold values from 0 to 3, as said below
- positions: int32 [8, 2048], P('fsdp', 'ctx'), may hold values from 0 to 4094, as said below
- attn_norm: bfloat16 [1536], P('fsdp'), may hold values from 0.099609375 to 1.8984375
- q_weight: bfloat16 [1536, 1536], P('fsdp'), may hold values from -0.15625 to 0.15625
- q_bias: bfloat16 [1536], P('fsdp'), may hold values from -3 to 3
- k_weight: bfloat16 [1536, 256], P('fsdp'), may hold values from -0.15625 to 0.15625
- k_bias: bfloat16 [256], P('fsdp'), may hold values from -3 to 3
- v_weight: bfloat16 [1536, 256], P('fsdp'), may hold values from -0.15625 to 0.15625
- v_bias: bfloat16 [256], P('fsdp'), may hold values from -3 to 3
- o_weight: bfloat16 [1536, 1536], P('fsdp'), may hold values from -1.25 to 1.25
- mlp_norm: bfloat16 [1536], P('fsdp'), may hold values from 0.099609375 to 1.8984375
- gate_weight: bfloat16 [1536, 8960], P('fsdp'), may hold values from -0.15625 to 0.15625
- up_weight: bfloat16 [1536, 8960], P('fsdp'), may hold values from -0.15625 to 0.15625
- down_weight: bfloat16 [8960, 1536], P('fsdp'), may hold values from -0.0625 to 0.0625
- out_cotangent: bfloat16 [8, 2048, 1536], P('fsdp', 'ctx'), may hold values from -6 to 6
Outputs:
- layer_output: bfloat16 [8, 2048, 1536], P('fsdp', 'ctx')
- input_grad: float32 [8, 2048, 1536], P('fsdp', 'ctx')
- attn_norm_grad: float32 [1536], P('fsdp')
- q_weight_grad: float32 [1536, 1536], P('fsdp')
- q_bias_grad: float32 [1536], P('fsdp')
- k_weight_grad: float32 [1536, 256], P('fsdp')
- k_bias_grad: float32 [256], P('fsdp')
- v_weight_grad: float32 [1536, 256], P('fsdp')
- v_bias_grad: float32 [256], P('fsdp')
- o_weight_grad: float32 [1536, 1536], P('fsdp')
- mlp_norm_grad: float32 [1536], P('fsdp')
- gate_weight_grad: float32 [1536, 8960], P('fsdp')
- up_weight_grad: float32 [1536, 8960], P('fsdp')
- down_weight_grad: float32 [8960, 1536], P('fsdp')
Inputs may be any that keep to these rules, and one draw needn't show every extreme that they name: `segments`: in order of place, each sequence holds documents 1, 2 and 3, then at least one padding token (0) at its end; document 1 ends and document 2 begins within the first 64 places, document 2 ends within the last 64 places, padding takes at most 32 places. Within each document positions rise by one from place to place; document 1 starts at 0, documents 2 and 3 anywhere from 0 to 2047; a padding token's position is its place plus 2047.
All inputs are finite; a program needn't handle non-finite values.
Results may differ from a plain program's by a relative error of at most 0.025.
Values may be sent and summed in bfloat16 or wider, within the bound.
A program may use at most 320 MiB of HBM per device.

v0:
```python
import jax
import jax.numpy as jnp
from jax import lax
from jax.sharding import PartitionSpec as P

HEADS = 12
KV_HEADS = 2
HD = 128


EPSILON = 1e-06
THETA = 1000000.0


def rope_tables(position, head_dim):
    freqs = THETA ** (-jnp.arange(0, head_dim, 2).astype(jnp.float32) / head_dim)
    angles = position.astype(jnp.float32)[:, None] * freqs[None, :]
    return (jnp.cos(angles), jnp.sin(angles))


def rotate(values, cosine, sine):
    middle = values.shape[-1] // 2
    front = values[..., :middle]
    behind = values[..., middle:]
    cos_head = cosine[:, None, :]
    sin_head = sine[:, None, :]
    return jnp.concatenate(
        [front * cos_head - behind * sin_head, behind * cos_head + front * sin_head], axis=-1
    )


def rotate_back(gradient, cosine, sine):
    middle = gradient.shape[-1] // 2
    front = gradient[..., :middle]
    behind = gradient[..., middle:]
    cos_head = cosine[:, None, :]
    sin_head = sine[:, None, :]
    return jnp.concatenate(
        [front * cos_head + behind * sin_head, behind * cos_head - front * sin_head], axis=-1
    )


def contract_rows(left, right):
    return lax.dot_general(
        left, right, (((0,), (0,)), ((), ())), preferred_element_type=jnp.float32
    )


def contract_cols(left, right):
    return lax.dot_general(
        left, right, (((1,), (1,)), ((), ())), preferred_element_type=jnp.float32
    )


def body(
    layer_input,
    segments,
    positions,
    attn_norm,
    q_weight,
    q_bias,
    k_weight,
    k_bias,
    v_weight,
    v_bias,
    o_weight,
    mlp_norm,
    gate_weight,
    up_weight,
    down_weight,
    out_cotangent,
):
    tokens = layer_input.shape[1]
    units = gate_weight.shape[1]
    group_size = HEADS // KV_HEADS
    q_width = HEADS * HD
    kv_width = KV_HEADS * HD
    ctx_count = lax.axis_size("ctx")
    half_block = tokens // 2
    score_scale = HD ** (-0.5)
    inputs = layer_input[0].astype(jnp.float32)
    segment = segments[0]
    position = positions[0]

    def dealt_place(device, within):
        return jnp.where(
            within < half_block,
            device * half_block + within,
            (2 * ctx_count - 1 - device) * half_block + within - half_block,
        )

    query_index = dealt_place(lax.axis_index("ctx"), jnp.arange(tokens, dtype=jnp.int32))
    gathered = (
        lax.all_gather(attn_norm, "fsdp", axis=0, tiled=True),
        lax.all_gather(mlp_norm, "fsdp", axis=0, tiled=True),
        lax.all_gather(q_bias, "fsdp", axis=0, tiled=True),
        lax.all_gather(k_bias, "fsdp", axis=0, tiled=True),
        lax.all_gather(v_bias, "fsdp", axis=0, tiled=True),
        lax.all_gather(q_weight, "fsdp", axis=0, tiled=True),
        lax.all_gather(k_weight, "fsdp", axis=0, tiled=True),
        lax.all_gather(v_weight, "fsdp", axis=0, tiled=True),
        lax.all_gather(o_weight, "fsdp", axis=0, tiled=True),
    )
    gain_one = gathered[0].astype(jnp.float32)
    gain_two = gathered[1].astype(jnp.float32)
    bias_q = gathered[2].astype(jnp.float32)
    bias_k = gathered[3].astype(jnp.float32)
    bias_v = gathered[4].astype(jnp.float32)
    full_q, full_k, full_v, full_o = (gathered[5], gathered[6], gathered[7], gathered[8])
    scale_one = lax.rsqrt(jnp.mean(inputs * inputs, axis=-1, keepdims=True) + EPSILON)
    norm_first = inputs * scale_one
    normed_in = (norm_first * gain_one).astype(jnp.bfloat16)
    query = jnp.dot(normed_in, full_q, preferred_element_type=jnp.float32) + bias_q
    keyproj = jnp.dot(normed_in, full_k, preferred_element_type=jnp.float32) + bias_k
    valproj = jnp.dot(normed_in, full_v, preferred_element_type=jnp.float32) + bias_v
    cosine, sine = rope_tables(position, HD)
    query_rot = rotate(query.reshape(tokens, HEADS, HD), cosine, sine).astype(jnp.bfloat16)
    key_rot = (
        rotate(keyproj.reshape(tokens, KV_HEADS, HD), cosine, sine)
        .astype(jnp.bfloat16)
        .reshape(tokens, kv_width)
    )
    value_low = valproj.astype(jnp.bfloat16)
    keys_all, values_all, segment_all = (
        lax.all_gather(key_rot, "ctx", axis=0, tiled=True),
        lax.all_gather(value_low, "ctx", axis=0, tiled=True),
        lax.all_gather(segment.astype(jnp.bfloat16), "ctx", axis=0, tiled=True),
    )
    length = keys_all.shape[0]
    key_segment = segment_all.astype(jnp.int32)
    stored_index = jnp.arange(length, dtype=jnp.int32)
    key_index = dealt_place(stored_index // tokens, stored_index % tokens)
    allowed = (
        (key_index[None, :] <= query_index[:, None])
        & (key_segment[None, :] == segment[:, None])
        & (segment[:, None] > 0)
    )
    query_group = query_rot.reshape(tokens, KV_HEADS, group_size, HD)
    key_group = keys_all.reshape(length, KV_HEADS, HD)
    value_group = values_all.reshape(length, KV_HEADS, HD)
    scores = (
        jnp.einsum("qcgd,kcd->cgqk", query_group, key_group, preferred_element_type=jnp.float32)
        * score_scale
    )
    masked = jnp.where(allowed, scores, -1e30)
    highest = jnp.max(masked, axis=-1, keepdims=True)
    exponent = jnp.where(allowed, jnp.exp(masked - highest), 0.0)
    totals = jnp.sum(exponent, axis=-1, keepdims=True)
    totals = jnp.where(totals > 0.5, totals, 1.0)
    probability = (exponent / totals).astype(jnp.bfloat16)
    attended = jnp.einsum(
        "cgqk,kcd->qcgd", probability, value_group, preferred_element_type=jnp.float32
    )
    attended_low = attended.reshape(tokens, q_width).astype(jnp.bfloat16)
    middle_state = inputs + jnp.dot(attended_low, full_o, preferred_element_type=jnp.float32)
    scale_two = lax.rsqrt(jnp.mean(middle_state * middle_state, axis=-1, keepdims=True) + EPSILON)
    norm_second = middle_state * scale_two
    normed_mid = (norm_second * gain_two).astype(jnp.bfloat16)
    cotangent = out_cotangent[0].astype(jnp.float32) * (segment > 0).astype(jnp.float32)[:, None]
    cot_low = cotangent.astype(jnp.bfloat16)
    pieces = (
        lax.all_gather(gate_weight, "fsdp", axis=0, tiled=True),
        lax.all_gather(up_weight, "fsdp", axis=0, tiled=True),
    )
    columns = normed_mid
    gate_pre = jnp.dot(columns, pieces[0], preferred_element_type=jnp.float32)
    up_pre = jnp.dot(columns, pieces[1], preferred_element_type=jnp.float32)
    sigma = jax.nn.sigmoid(gate_pre)
    swish = gate_pre * sigma
    activation = (swish * up_pre).astype(jnp.bfloat16)
    piece = lax.all_gather(down_weight, "fsdp", axis=0, tiled=True)
    columns = activation
    out_part = jnp.dot(columns, piece, preferred_element_type=jnp.float32)
    grad_part = contract_cols(cot_low, piece)
    output_rows = (middle_state + out_part).astype(jnp.bfloat16)
    down_share = lax.psum_scatter(
        contract_rows(activation, cot_low).astype(jnp.bfloat16),
        "fsdp",
        scatter_dimension=0,
        tiled=True,
    )
    gate_grad = grad_part * up_pre * sigma * (1.0 + gate_pre * (1.0 - sigma))
    up_grad = grad_part * swish
    both_grad = jnp.concatenate([gate_grad, up_grad], axis=1).astype(jnp.bfloat16)
    gate_low = both_grad[:, :units]
    up_low = both_grad[:, units:]
    pieces = (
        lax.all_gather(gate_weight, "fsdp", axis=0, tiled=True),
        lax.all_gather(up_weight, "fsdp", axis=0, tiled=True),
    )
    part_sum = contract_cols(gate_low, pieces[0]) + contract_cols(up_low, pieces[1])
    gate_up_share = lax.psum_scatter(
        contract_rows(normed_mid, both_grad).astype(jnp.bfloat16),
        "fsdp",
        scatter_dimension=0,
        tiled=True,
    ).astype(jnp.float32)
    gain_two_grad = jnp.sum(part_sum * norm_second, axis=0)
    scaled_two = part_sum * gain_two
    mid_grad = cotangent + scale_two * (
        scaled_two - norm_second * jnp.mean(scaled_two * norm_second, axis=-1, keepdims=True)
    )
    branch_low = mid_grad.astype(jnp.bfloat16)
    attended_grad = contract_cols(branch_low, full_o).astype(jnp.bfloat16)
    out_share = lax.psum_scatter(
        contract_rows(attended_low, branch_low).astype(jnp.bfloat16),
        "fsdp",
        scatter_dimension=0,
        tiled=True,
    )
    grad_group = attended_grad.reshape(tokens, KV_HEADS, group_size, HD)
    prob_float = exponent / totals
    prob_grad = jnp.einsum(
        "qcgd,kcd->cgqk", grad_group, value_group, preferred_element_type=jnp.float32
    )
    row_dot = jnp.sum(prob_float * prob_grad, axis=-1, keepdims=True)
    score_grad = (prob_float * (prob_grad - row_dot) * score_scale).astype(jnp.bfloat16)
    value_grad_all = jnp.einsum(
        "cgqk,qcgd->kcd", probability, grad_group, preferred_element_type=jnp.float32
    )
    query_rot_grad = jnp.einsum(
        "cgqk,kcd->qcgd", score_grad, key_group, preferred_element_type=jnp.float32
    )
    key_grad_all = jnp.einsum(
        "cgqk,qcgd->kcd", score_grad, query_group, preferred_element_type=jnp.float32
    )
    key_grad_own, value_grad_own = (
        lax.psum_scatter(
            key_grad_all.reshape(length, kv_width), "ctx", scatter_dimension=0, tiled=True
        ),
        lax.psum_scatter(
            value_grad_all.reshape(length, kv_width), "ctx", scatter_dimension=0, tiled=True
        ),
    )
    query_grad = rotate_back(query_rot_grad.reshape(tokens, HEADS, HD), cosine, sine).reshape(
        tokens, q_width
    )
    key_grad = rotate_back(key_grad_own.reshape(tokens, KV_HEADS, HD), cosine, sine).reshape(
        tokens, kv_width
    )
    proj_grad = jnp.concatenate([query_grad, key_grad, value_grad_own], axis=1).astype(jnp.bfloat16)
    bias_grads = jnp.sum(proj_grad.astype(jnp.float32), axis=0)
    proj_share = lax.psum_scatter(
        contract_rows(normed_in, proj_grad).astype(jnp.bfloat16),
        "fsdp",
        scatter_dimension=0,
        tiled=True,
    ).astype(jnp.float32)
    in_norm_grad = contract_cols(proj_grad, jnp.concatenate([full_q, full_k, full_v], axis=1))
    gain_one_grad = jnp.sum(in_norm_grad * norm_first, axis=0)
    scaled_one = in_norm_grad * gain_one
    input_rows = mid_grad + scale_one * (
        scaled_one - norm_first * jnp.mean(scaled_one * norm_first, axis=-1, keepdims=True)
    )
    small_shares = (
        lax.psum_scatter(gain_one_grad, "fsdp", scatter_dimension=0, tiled=True),
        lax.psum_scatter(gain_two_grad, "fsdp", scatter_dimension=0, tiled=True),
        lax.psum_scatter(bias_grads[:q_width], "fsdp", scatter_dimension=0, tiled=True),
        lax.psum_scatter(
            bias_grads[q_width : q_width + kv_width], "fsdp", scatter_dimension=0, tiled=True
        ),
        lax.psum_scatter(bias_grads[q_width + kv_width :], "fsdp", scatter_dimension=0, tiled=True),
    )
    summed = (
        lax.psum(small_shares[0].astype(jnp.bfloat16), "ctx").astype(jnp.float32),
        lax.psum(proj_share[:, :q_width].astype(jnp.bfloat16), "ctx").astype(jnp.float32),
        lax.psum(small_shares[2].astype(jnp.bfloat16), "ctx").astype(jnp.float32),
        lax.psum(proj_share[:, q_width : q_width + kv_width].astype(jnp.bfloat16), "ctx").astype(
            jnp.float32
        ),
        lax.psum(small_shares[3].astype(jnp.bfloat16), "ctx").astype(jnp.float32),
        lax.psum(proj_share[:, q_width + kv_width :].astype(jnp.bfloat16), "ctx").astype(
            jnp.float32
        ),
        lax.psum(small_shares[4].astype(jnp.bfloat16), "ctx").astype(jnp.float32),
        lax.psum(out_share, "ctx").astype(jnp.float32),
        lax.psum(small_shares[1].astype(jnp.bfloat16), "ctx").astype(jnp.float32),
        lax.psum(gate_up_share[:, :units].astype(jnp.bfloat16), "ctx").astype(jnp.float32),
        lax.psum(gate_up_share[:, units:].astype(jnp.bfloat16), "ctx").astype(jnp.float32),
        lax.psum(down_share, "ctx").astype(jnp.float32),
    )
    return (
        output_rows[None],
        input_rows[None],
        summed[0],
        summed[1],
        summed[2],
        summed[3],
        summed[4],
        summed[5],
        summed[6],
        summed[7],
        summed[8],
        summed[9],
        summed[10],
        summed[11],
    )


def solution(mesh):
    placed = (
        P("fsdp", "ctx", None),
        P("fsdp", "ctx"),
        P("fsdp", "ctx"),
        P("fsdp"),
        P("fsdp", None),
        P("fsdp"),
        P("fsdp", None),
        P("fsdp"),
        P("fsdp", None),
        P("fsdp"),
        P("fsdp", None),
        P("fsdp"),
        P("fsdp", None),
        P("fsdp", None),
        P("fsdp", None),
        P("fsdp", "ctx", None),
    )
    return jax.shard_map(
        body,
        mesh=mesh,
        in_specs=placed,
        out_specs=(
            P("fsdp", "ctx", None),
            P("fsdp", "ctx", None),
            P("fsdp"),
            P("fsdp", None),
            P("fsdp"),
            P("fsdp", None),
            P("fsdp"),
            P("fsdp", None),
            P("fsdp"),
            P("fsdp", None),
            P("fsdp"),
            P("fsdp", None),
            P("fsdp", None),
            P("fsdp", None),
        ),
        check_vma=False,
    )
```

profile of v0, /device:TPU:35, one launch (start us, length us, event | category | flops | bytes accessed | tf_op | source)
XLA Modules:
  0.0 2474.6 jit_solution(11323667917891524827)
XLA Ops:
  7.2 24.5 all_gather.48
  38.6 25.7 %all-reduce.13 = (bf16[256]{0:T(256)(128)(2,1)S(1)}, bf16[1536]{0:T(1024)(128)(2,1)S(1)}, bf16[256]{0:T(256)(128)(2,1)S(1)}, bf16[1536]{0:T(1024)(128)(2,1)S(1)}, bf16[1536]{0:T(1024)(128)(2,1)S(1)}) all-reduce(bf16[256]{0:T(256)(128)(2,1)S(1)} %dynamic-update-slice.1, ...), channel_id=1, replica_groups=mesh['ctx'=16,'fsdp'=8] {'fsdp'}, use_global_device_ids=true, to_apply=%add.1 | all-reduce | flops 5120 | bytes 20480
  68.3 23.1 all_gather.52
  98.7 39.6 %all-gather = bf16[16,1,128]{2,1,0:T(2,128)(2,1)S(1)} all-gather(bf16[1,1,128]{2,1,0:T(2,128)(2,1)S(1)} %convert_bitcast_fusion.1), channel_id=1, replica_groups=mesh['ctx'=16,'fsdp'=8] {'ctx'}, dimensions={0}, use_global_device_ids=true | all-gather | bytes 4352 | tf_op jit(solution)/shard_map/all_gather | solution.py:127
  142.4 40.5 %all-gather.13.cloned.1.call-done = bf16[1536,1536]{1,0:T(8,128)(2,1)} async-done(((bf16[192,1536]{1,0:T(8,128)(2,1)}), bf16[1536,1536]{1,0:T(8,128)(2,1)}) %all-gather.13.cloned.1.call-update) | async-done | bytes 4718608 | tf_op jit(solution)/shard_map/all_gather | solution.py:99
  187.0 43.2 %all-gather.11.cloned.1.call-done = bf16[2048,256]{0,1:T(8,128)(2,1)} async-done(((bf16[128,256]{0,1:T(8,128)(2,1)}), bf16[2048,256]{0,1:T(8,128)(2,1)}) %all-gather.11.cloned.1.call-update) | async-done | bytes 1048592 | tf_op jit(solution)/shard_map/all_gather | solution.py:125
  247.3 40.5 %all-gather.15.cloned.1.call-done = bf16[1536,1536]{1,0:T(8,128)(2,1)} async-done(((bf16[192,1536]{1,0:T(8,128)(2,1)}), bf16[1536,1536]{1,0:T(8,128)(2,1)}) %all-gather.15.cloned.1.call-update) | async-done | bytes 4718608 | tf_op jit(solution)/shard_map/all_gather | solution.py:102
  291.1 268.2 %all-gather.17.cloned.1.call-done = bf16[1536,8960]{1,0:T(8,128)(2,1)} async-done(((bf16[192,8960]{1,0:T(8,128)(2,1)}), bf16[1536,8960]{1,0:T(8,128)(2,1)}) %all-gather.17.cloned.1.call-update) | async-done | bytes 27525136 | tf_op jit(solution)/shard_map/all_gather | solution.py:162
  574.2 256.7 %all-gather.19.cloned.1.call-done = bf16[1536,8960]{1,0:T(8,128)(2,1)} async-done(((bf16[192,8960]{1,0:T(8,128)(2,1)}), bf16[1536,8960]{1,0:T(8,128)(2,1)}) %all-gather.19.cloned.1.call-update) | async-done | bytes 27525136 | tf_op jit(solution)/shard_map/all_gather | solution.py:163
  845.7 257.1 %all-gather.21.cloned.1.call-done = bf16[8960,1536]{1,0:T(8,128)(2,1)} async-done(((bf16[1120,1536]{1,0:T(8,128)(2,1)}), bf16[8960,1536]{1,0:T(8,128)(2,1)}) %all-gather.21.cloned.1.call-update) | async-done | bytes 27525136 | tf_op jit(solution)/shard_map/all_gather | solution.py:171
  1102.7 17.7 multiply_convert_fusion
  1135.4 15.7 multiply_reduce_fusion
  1167.8 19.4 fusion.16
  1195.6 20.4 fusion.17
  1218.0 37.1 %reduce-scatter.7.cloned.1.call-done = f32[128,256]{0,1:T(8,128)} async-done(((f32[2048,256]{0,1:T(8,128)}), f32[128,256]{0,1:T(8,128)}) %reduce-scatter.7.cloned.1.call-update) | async-done | bytes 131088 | tf_op jit(solution)/shard_map/reduce_scatter | solution.py:228
  1261.9 67.7 %reduce-scatter.9.cloned.1.call-done = f32[128,256]{0,1:T(8,128)} async-done(((f32[2048,256]{0,1:T(8,128)}), f32[128,256]{0,1:T(8,128)}) %reduce-scatter.9.cloned.1.call-update) | async-done | bytes 131088 | tf_op jit(solution)/shard_map/reduce_scatter | solution.py:231
  1336.2 23.7 convolution_convert_fusion
  1379.2 31.0 %reduce-scatter.11.cloned.1.call-done = bf16[192,2048]{1,0:T(8,128)(2,1)} async-done(((bf16[1536,2048]{1,0:T(8,128)(2,1)}), bf16[192,2048]{1,0:T(8,128)(2,1)}) %reduce-scatter.11.cloned.1.call-update) | async-done | bytes 786448 | tf_op jit(solution)/shard_map/reduce_scatter | solution.py:243
  1413.7 528.3 %reduce-scatter.15.cloned.1.call-done = bf16[192,17920]{1,0:T(8,128)(2,1)} async-done(((bf16[1536,17920]{1,0:T(8,128)(2,1)}), bf16[192,17920]{1,0:T(8,128)(2,1)}) %reduce-scatter.15.cloned.1.call-update) | async-done | bytes 6881296 | tf_op jit(solution)/shard_map/reduce_scatter | solution.py:192
  1948.4 53.5 %reduce-scatter.13.cloned.1.call-done = bf16[192,1536]{1,0:T(8,128)(2,1)} async-done(((bf16[1536,1536]{1,0:T(8,128)(2,1)}), bf16[192,1536]{1,0:T(8,128)(2,1)}) %reduce-scatter.13.cloned.1.call-update) | async-done | bytes 589840 | tf_op jit(solution)/shard_map/reduce_scatter | solution.py:205
  2001.9 273.9 %reduce-scatter.17.cloned.1.call-done = bf16[1120,1536]{1,0:T(8,128)(2,1)} async-done(((bf16[8960,1536]{1,0:T(8,128)(2,1)}), bf16[1120,1536]{1,0:T(8,128)(2,1)}) %reduce-scatter.17.cloned.1.call-update) | async-done | bytes 3440656 | tf_op jit(solution)/shard_map/reduce_scatter | solution.py:176
  2293.8 25.3 %all-reduce.10 = (bf16[1536]{0:T(1024)(128)(2,1)S(1)}, bf16[1536]{0:T(1024)(128)(2,1)S(1)}, bf16[256]{0:T(256)(128)(2,1)S(1)}, bf16[256]{0:T(256)(128)(2,1)S(1)}, bf16[1536]{0:T(1024)(128)(2,1)S(1)}) all-reduce(f32[1536]{0:T(1024)S(1)} %get-tuple-element.16, ...), channel_id=4, replica_groups=mesh['ctx'=16,'fsdp'=8] {'fsdp'}, use_global_device_ids=true, to_apply=%region_10.11.clone | all-reduce | flops 5120 | bytes 30720
  2319.5 35.1 %all-reduce.11 = (bf16[192]{0:T(256)(128)(2,1)S(1)}, bf16[192]{0:T(256)(128)(2,1)S(1)}, bf16[32]{0:T(256)(128)(2,1)S(1)}, bf16[32]{0:T(256)(128)(2,1)S(1)}, bf16[192]{0:T(256)(128)(2,1)S(1)}) all-reduce(bf16[192]{0:T(256)(128)(2,1)S(1)} %dynamic-slice.22, ...), channel_id=1, replica_groups=mesh['ctx'=16,'fsdp'=8] {'ctx'}, use_global_device_ids=true, to_apply=%region_11.12 | all-reduce | flops 640 | bytes 2560 | tf_op jit(solution)/shard_map/psum | solution.py:265
  2358.5 89.0 %all-reduce.16.cloned.1.call-done = (bf16[192,1536]{1,0:T(8,128)(2,1)}, bf16[192,256]{1,0:T(8,128)(2,1)}, bf16[192,256]{1,0:T(8,128)(2,1)}, bf16[192,1536]{1,0:T...) async-done(((bf16[192,1536]{1,0:T(8,128)(2,1)}, bf16[192,256]{1,0:T(8,128)(2,1)}, bf16[192,256]{1,0:T(8,128)(2,1)}, ...) | async-done | bytes 11698192 | tf_op jit(solution)/shard_map/psum | solution.py:266
  (179 shorter events, 200.4 us)
Async XLA Ops:
  7.2 133.3 %all-gather.9.cloned.1.call-start = ((), (), s32[]{:S(2)}) async-start(), calls=%async_computation.6 | async-start | bytes 1114112 | tf_op jit(solution)/shard_map/all_gather | solution.py:126
  65.5 117.4 %copy-start.23 = (f32[128]{0:T(128)}, f32[128]{0:T(128)S(1)}, u32[]{:S(2)}) copy-start(f32[128]{0:T(128)S(1)} %add_rsqrt_fusion.1) | copy-start | bytes 1540
  67.5 115.4 %all-gather.13.cloned.1.call-start = ((), (), s32[]{:S(2)}) async-start(), calls=%async_computation.8 | async-start | bytes 5308416 | tf_op jit(solution)/shard_map/all_gather | solution.py:99
  68.3 162.0 %all-gather.11.cloned.1.call-start = ((), (), s32[]{:S(2)}) async-start(), calls=%async_computation.7 | async-start | bytes 1114112 | tf_op jit(solution)/shard_map/all_gather | solution.py:125
  94.6 91.8 %copy-start.18 = (f32[128,64]{0,1:T(8,128)}, f32[128,64]{0,1:T(8,128)S(1)}, u32[]{:S(2)}) copy-start(f32[128,64]{0,1:T(8,128)S(1)} %get-tuple-element.59) | copy-start | bytes 98308
  94.7 91.8 %copy-start.19 = (f32[128,64]{0,1:T(8,128)}, f32[128,64]{0,1:T(8,128)S(1)}, u32[]{:S(2)}) copy-start(f32[128,64]{0,1:T(8,128)S(1)} %get-tuple-element.60) | copy-start | bytes 98308
  95.2 87.8 %copy-start.3 = (bf16[1,128,1536]{2,1,0:T(8,128)(2,1)S(1)}, bf16[1,128,1536]{2,1,0:T(8,128)(2,1)}, u32[]{:S(2)}) copy-start(bf16[1,128,1536]{2,1,0:T(8,128)(2,1)} %param.16) | copy-start | bytes 1179652
  96.1 191.6 %all-gather.15.cloned.1.call-start = ((), (), s32[]{:S(2)}) async-start(), calls=%async_computation.9 | async-start | bytes 5308416 | tf_op jit(solution)/shard_map/all_gather | solution.py:102
  96.7 462.6 %all-gather.17.cloned.1.call-start = ((), (), s32[]{:S(2)}) async-start(), calls=%async_computation.10 | async-start | bytes 30965760 | tf_op jit(solution)/shard_map/all_gather | solution.py:162
  97.3 733.6 %all-gather.19.cloned.1.call-start = ((), (), s32[]{:S(2)}) async-start(), calls=%async_computation.11 | async-start | bytes 30965760 | tf_op jit(solution)/shard_map/all_gather | solution.py:163
  97.9 1004.9 %all-gather.21.cloned.1.call-start = ((), (), s32[]{:S(2)}) async-start(), calls=%async_computation.12 | async-start | bytes 30965760 | tf_op jit(solution)/shard_map/all_gather | solution.py:171
  98.6 1156.5 %reduce-scatter.7.cloned.1.call-start = ((), (), s32[]{:S(2)}) async-start(), calls=%async_computation.13 | async-start | bytes 2228224 | tf_op jit(solution)/shard_map/reduce_scatter | solution.py:228
  138.4 1012.8 %copy-start.26 = (f32[128]{0:T(128)}, f32[128]{0:T(128)S(1)}, u32[]{:S(2)}) copy-start(f32[128]{0:T(128)S(1)} %get-tuple-element.63) | copy-start | bytes 1540
  142.4 99.1 %copy-start.5 = (bf16[2048,2,128]{2,1,0:T(2,128)(2,1)}, bf16[2048,2,128]{2,1,0:T(2,128)(2,1)S(1)}, u32[]{:S(2)}) copy-start(bf16[2048,2,128]{2,1,0:T(2,128)(2,1)S(1)} %reshape.226) | copy-start | bytes 3145732
  241.5 945.7 %copy-start.22 = (f32[2,6,128]{2,1,0:T(8,128)}, f32[2,6,128]{2,1,0:T(8,128)S(1)}, u32[]{:S(2)}) copy-start(f32[2,6,128]{2,1,0:T(8,128)S(1)} %compare_select_fusion) | copy-start | bytes 18436
  291.1 539.8 %copy-start.4 = (bf16[128,1536]{1,0:T(8,128)(2,1)}, bf16[128,1536]{1,0:T(8,128)(2,1)S(1)}, u32[]{:S(2)}) copy-start(bf16[128,1536]{1,0:T(8,128)(2,1)S(1)} %multiply_convert_fusion.3) | copy-start | bytes 1179652
  1187.2 142.4 %reduce-scatter.9.cloned.1.call-start = ((), (), s32[]{:S(2)}) async-start(), calls=%async_computation.14 | async-start | bytes 2228224 | tf_op jit(solution)/shard_map/reduce_scatter | solution.py:231
  1195.5 214.7 %reduce-scatter.11.cloned.1.call-start = ((), (), s32[]{:S(2)}) async-start(), calls=%async_computation.15 | async-start | bytes 7077888 | tf_op jit(solution)/shard_map/reduce_scatter | solution.py:243
  1336.2 605.9 %reduce-scatter.15.cloned.1.call-start = ((), (), s32[]{:S(2)}) async-start(), calls=%async_computation.17 | async-start | bytes 61931520 | tf_op jit(solution)/shard_map/reduce_scatter | solution.py:192
  1360.0 641.9 %reduce-scatter.13.cloned.1.call-start = ((), (), s32[]{:S(2)}) async-start(), calls=%async_computation.16 | async-start | bytes 5308416 | tf_op jit(solution)/shard_map/reduce_scatter | solution.py:205
  1365.0 910.8 %reduce-scatter.17.cloned.1.call-start = ((), (), s32[]{:S(2)}) async-start(), calls=%async_computation.18 | async-start | bytes 30965760 | tf_op jit(solution)/shard_map/reduce_scatter | solution.py:176
  1379.2 1068.4 %all-reduce.16.cloned.1.call-start = ((), (), s32[]{:S(2)}) async-start(), calls=%async_computation.19 | async-start | bytes 23396352 | tf_op jit(solution)/shard_map/psum | solution.py:266
  2289.4 67.9 %copy-start.2 = (f32[128,1536]{1,0:T(8,128)S(1)}, f32[128,1536]{1,0:T(8,128)}, u32[]{:S(2)}) copy-start(f32[128,1536]{1,0:T(8,128)} %copy-done.1) | copy-start | bytes 2359300
  2289.4 67.9 %copy-start.25 = (f32[128]{0:T(128)S(1)}, f32[128]{0:T(128)}, u32[]{:S(2)}) copy-start(f32[128]{0:T(128)} %copy-done.23) | copy-start | bytes 1540
  (18 other events, 459.1 us)
Sparse Core Ops, SparseCore 0:
  67.6 57.8 all-gather.8
  127.1 55.7 all-gather.12
  185.8 44.4 all-gather.10
  231.8 55.8 all-gather.14
  289.2 270.0 all-gather.16
  560.8 270.0 all-gather.18
  832.6 270.0 all-gather.20
  1187.3 67.7 reduce-scatter.6
  1259.7 69.8 reduce-scatter.8
  1336.3 73.8 reduce-scatter.10
  1412.7 529.3 reduce-scatter.14
  1945.0 56.8 reduce-scatter.12
  2004.5 271.2 reduce-scatter.16
  2279.9 167.5 all-reduce.15
where the time goes:
time: 2490 us; the launch traced here: 2470 us
  waiting for transfers between devices  1990 us (80%)
  matrix products  230 us (9%)
  blocking collectives  173 us (7%)
  other arithmetic  35.1 us (1%)
  local copies, waits for them, and re-layouts  28.7 us (1%)
    reduce_scatter x1, waiting for transfers between devices, body(): lax.psum_scatter(contract_rows(normed_mid, both_grad).astype(jnp.bfloat16...  528 us
    reduce_scatter x1, waiting for transfers between devices, body(): lax.psum_scatter(contract_rows(activation, cot_low).astype(jnp.bfloat16),...  274 us
    all_gather x1, waiting for transfers between devices, body(): lax.all_gather(gate_weight, 'fsdp', axis=0, tiled=True)  268 us
    all_gather x1, waiting for transfers between devices, body(): piece = lax.all_gather(down_weight, 'fsdp', axis=0, tiled=True)  257 us
    all_gather x1, waiting for transfers between devices, body(): lax.all_gather(up_weight, 'fsdp', axis=0, tiled=True)  257 us
    psum x1, waiting for transfers between devices, body(): lax.psum(proj_share[:, :q_width].astype(jnp.bfloat16), 'ctx')  89 us
    reduce_scatter x1, waiting for transfers between devices, body(): lax.psum_scatter(value_grad_all.reshape(length, kv_width), 'ctx', scatter...  67.7 us
    dot_general x5, matrix products, contract_cols(): lax.dot_general(left, right, (((1,), (1,)), ((), ())), preferred_element_...  57.4 us
  transfers between devices with their start and end apart: 14, of which 13 were waited for; matrix products, arithmetic and copies ran while one was open for 7% of the time, Pallas kernels for 0%

commit v1 on v0

v1 whole, which is shorter than its diff:
```python
import functools

import jax
import jax.numpy as jnp
from jax import lax
from jax.experimental import pallas as pl
from jax.experimental.pallas import tpu as pltpu
from jax.sharding import PartitionSpec as P

HEADS = 12
KV_HEADS = 2
HD = 128
GROUP = HEADS // KV_HEADS
N_CTX = 16
N_FS = 8
EPSILON = 1e-06
THETA = 1000000.0
MESH = pl.DeviceIdType.MESH
BF = jnp.bfloat16
F32 = jnp.float32


def rope_tables(position, head_dim):
    freqs = THETA ** (-jnp.arange(0, head_dim, 2).astype(F32) / head_dim)
    angles = position.astype(F32)[:, None] * freqs[None, :]
    return (jnp.cos(angles), jnp.sin(angles))


def rotate(values, cosine, sine):
    middle = values.shape[-1] // 2
    front = values[..., :middle]
    behind = values[..., middle:]
    cos_head = cosine[:, None, :]
    sin_head = sine[:, None, :]
    return jnp.concatenate(
        [front * cos_head - behind * sin_head, behind * cos_head + front * sin_head], axis=-1
    )


def contract_rows(left, right):
    return lax.dot_general(
        left, right, (((0,), (0,)), ((), ())), preferred_element_type=F32
    )


def contract_cols(left, right):
    return lax.dot_general(
        left, right, (((1,), (1,)), ((), ())), preferred_element_type=F32
    )


def flip(value, mask):
    out = value
    bit = 1
    while bit <= mask:
        if mask & bit:
            out = out + bit * (1 - 2 * lax.rem(lax.div(value, bit), 2))
        bit *= 2
    return out


class Copies:
    def __init__(self, send, recv):
        self.send, self.recv, self.count, self.all = send, recv, 0, []

    def start(self, src, dst, device):
        copy = pltpu.make_async_remote_copy(
            src_ref=src,
            dst_ref=dst,
            send_sem=self.send.at[self.count],
            recv_sem=self.recv.at[self.count],
            device_id=device,
            device_id_type=MESH,
        )
        self.count += 1
        copy.start()
        self.all.append(copy)
        return copy


def greet(devices):
    barrier = pltpu.get_barrier_semaphore()
    for device in devices:
        pl.semaphore_signal(barrier, inc=1, device_id=device, device_id_type=MESH)
    pl.semaphore_wait(barrier, len(devices))


def exchange(kernel, name, cid, ins, outs, copies, locals_):
    return pl.pallas_call(
        kernel,
        name=name,
        out_shape=[jax.ShapeDtypeStruct(s, d) for s, d in outs],
        in_specs=[pl.BlockSpec(memory_space=pl.ANY)] * len(ins),
        out_specs=[pl.BlockSpec(memory_space=pl.ANY)] * len(outs),
        scratch_shapes=[
            pltpu.SemaphoreType.DMA((copies,)),
            pltpu.SemaphoreType.DMA((copies,)),
            pltpu.SemaphoreType.DMA((locals_,)),
        ],
        compiler_params=pltpu.CompilerParams(collective_id=cid, has_side_effects=True),
    )(*ins)


def first_kernel(w_ref, s_ref, g_ref, w_out, s_out, g_out, send, recv, local):
    c, f = lax.axis_index("ctx"), lax.axis_index("fsdp")
    core = lax.rem(c, 2)
    sibling = (flip(c, 1), f)
    peers = [(c, flip(f, i)) for i in range(1, N_FS)]
    greet(peers + [sibling])
    copies = Copies(send, recv)
    own = [
        pltpu.make_async_copy(w_ref, w_out.at[f], local.at[0]),
        pltpu.make_async_copy(s_ref, s_out.at[f], local.at[1]),
        pltpu.make_async_copy(g_ref.at[f], g_out.at[f], local.at[2]),
    ]
    for copy in own:
        copy.start()
    rest = [copies.start(s_ref, s_out.at[f], peer) for peer in peers]
    halves = [copies.start(w_ref.at[core], w_out.at[f, core], peer) for peer in peers]
    rest += [copies.start(g_ref.at[peer[1]], g_out.at[f], peer) for peer in peers]
    for half, peer in zip(halves, peers):
        half.wait_recv()
        place = w_out.at[peer[1], core]
        rest.append(copies.start(place, place, sibling))
    for half in halves:
        half.wait_send()
    for copy in rest + own:
        copy.wait()


def second_kernel(kv_ref, w_ref, kv_out, w_out, send, recv, local):
    c, f = lax.axis_index("ctx"), lax.axis_index("fsdp")
    core = lax.rem(c, 2)
    sibling = (flip(c, 1), f)
    ring = [(flip(c, 2 * i), f) for i in range(1, N_CTX // 2)]
    peers = [(c, flip(f, i)) for i in range(1, N_FS)]
    greet(ring + peers + [sibling])
    copies = Copies(send, recv)
    own = [
        pltpu.make_async_copy(kv_ref, kv_out.at[c], local.at[0]),
        pltpu.make_async_copy(w_ref, w_out.at[f], local.at[1]),
    ]
    for copy in own:
        copy.start()
    keys = [copies.start(kv_ref, kv_out.at[c], device) for device in ring]
    rest = [copies.start(kv_ref, kv_out.at[c], sibling)]
    halves = [copies.start(w_ref.at[core], w_out.at[f, core], peer) for peer in peers]
    for key, device in zip(keys, ring):
        key.wait_recv()
        place = kv_out.at[device[0]]
        rest.append(copies.start(place, place, sibling))
    for half, peer in zip(halves, peers):
        half.wait_recv()
        place = w_out.at[peer[1], core]
        rest.append(copies.start(place, place, sibling))
    for copy in keys + halves:
        copy.wait_send()
    for copy in rest + own:
        copy.wait()


def scatter_kernel(count, *refs):
    ins, outs = refs[:count], refs[count : 2 * count]
    send, recv, local = refs[2 * count :]
    c, f = lax.axis_index("ctx"), lax.axis_index("fsdp")
    ring = [(flip(c, 2 * i), f) for i in range(1, N_CTX // 2)]
    greet(ring)
    copies = Copies(send, recv)
    for i, device in enumerate(ring):
        for src, dst in zip(ins, outs):
            piece = lax.div(device[0], 2)
            if len(src.shape) == 4:
                copies.start(src.at[:, piece], dst.at[i], device)
            else:
                copies.start(src.at[piece], dst.at[i], device)
    for copy in copies.all:
        copy.wait()


def owner_kernel(count, *refs):
    ins, outs = refs[:count], refs[count : 2 * count]
    send, recv, local = refs[2 * count :]
    c, f = lax.axis_index("ctx"), lax.axis_index("fsdp")
    peers = [(c, flip(f, i)) for i in range(1, N_FS)]
    greet(peers)
    copies = Copies(send, recv)
    own = [
        pltpu.make_async_copy(src.at[f], dst.at[f], local.at[n])
        for n, (src, dst) in enumerate(zip(ins, outs))
    ]
    for copy in own:
        copy.start()
    for peer in peers:
        for src, dst in zip(ins, outs):
            copies.start(src.at[peer[1]], dst.at[f], peer)
    for copy in copies.all + own:
        copy.wait()


def gather_kernel(count, *refs):
    ins, outs = refs[:count], refs[count : 2 * count]
    send, recv, local = refs[2 * count :]
    c, f = lax.axis_index("ctx"), lax.axis_index("fsdp")
    sibling = (flip(c, 1), f)
    ring = [(flip(c, 2 * i), f) for i in range(1, N_CTX // 2)]
    greet(ring + [sibling])
    copies = Copies(send, recv)
    own = [
        pltpu.make_async_copy(src, dst.at[c], local.at[n])
        for n, (src, dst) in enumerate(zip(ins, outs))
    ]
    for copy in own:
        copy.start()
    near = [
        [copies.start(src, dst.at[c], device) for src, dst in zip(ins, outs)] for device in ring
    ]
    rest = [copies.start(src, dst.at[c], sibling) for src, dst in zip(ins, outs)]
    for group, device in zip(near, ring):
        for copy, dst in zip(group, outs):
            copy.wait_recv()
            place = dst.at[device[0]]
            rest.append(copies.start(place, place, sibling))
    for group in near:
        for copy in group:
            copy.wait_send()
    for copy in rest + own:
        copy.wait()


def gather_ctx(name, cid, arrays):
    count = len(arrays)
    return exchange(
        functools.partial(gather_kernel, count),
        name,
        cid,
        arrays,
        [((N_CTX,) + a.shape, a.dtype) for a in arrays],
        15 * count,
        count,
    )


def scatter_ctx(name, cid, arrays):
    count = len(arrays)
    outs = [
        ((7, a.shape[0]) + a.shape[2:] if a.ndim == 4 else (7,) + a.shape[1:], a.dtype)
        for a in arrays
    ]
    return exchange(
        functools.partial(scatter_kernel, count), name, cid, arrays, outs, 7 * count, 1
    )


def to_owner(name, cid, arrays):
    count = len(arrays)
    return exchange(
        functools.partial(owner_kernel, count),
        name,
        cid,
        arrays,
        [(a.shape, a.dtype) for a in arrays],
        7 * count,
        count,
    )


def swap_fs(value, mask):
    return lax.ppermute(value, "fsdp", [(s, s ^ mask) for s in range(N_FS)])


def swap_ctx(value, mask):
    return lax.ppermute(value, "ctx", [(s, s ^ mask) for s in range(N_CTX)])


CHUNK = 256


def attend_kernel(q_ref, k_ref, v_ref, row_ref, e_ref, o_ref, inv_ref, s_ref):
    tokens = k_ref.shape[1] - 16
    length = N_CTX * tokens
    half = tokens // 2
    scale = HD ** (-0.5)
    query = q_ref[0]
    row_place, row_seg = row_ref[0:1, :], row_ref[1:2, :]
    key_seg = k_ref[:, tokens : tokens + 16, :][:, 0, :].astype(F32).T
    within = lax.broadcasted_iota(jnp.int32, (tokens, tokens), 0)
    top = jnp.full((8, GROUP * tokens), -1e30, F32)
    for b in range(N_CTX):
        place = jnp.where(
            within < half, b * half + within, (2 * N_CTX - 1 - b) * half + within - half
        ).astype(F32)
        allowed = (place <= row_place) & (key_seg[:, b : b + 1] == row_seg) & (row_seg > 0.5)
        bias = jnp.where(allowed, 0.0, -1e30).astype(F32)
        scores = (
            lax.dot_general(
                k_ref[b, :tokens, :],
                query,
                (((1,), (1,)), ((), ())),
                preferred_element_type=F32,
            )
            * scale
            + jnp.concatenate([bias] * GROUP, axis=1)
        )
        s_ref[b * tokens : (b + 1) * tokens, :] = scores
        top = jnp.maximum(top, jnp.max(scores.reshape(tokens // 8, 8, -1), axis=0))
    highest = jnp.maximum(jnp.max(top, axis=0, keepdims=True), -1e29)
    total = jnp.zeros((8, GROUP * tokens), F32)
    mixed = jnp.zeros((HD, GROUP * tokens), F32)
    for j in range(length // CHUNK):
        part = jnp.exp(s_ref[j * CHUNK : (j + 1) * CHUNK, :] - highest)
        total = total + jnp.sum(part.reshape(CHUNK // 8, 8, -1), axis=0)
        low = part.astype(BF)
        e_ref[0, j * CHUNK : (j + 1) * CHUNK, :] = low
        values = v_ref[2 * j : 2 * j + 2, :tokens, :].reshape(CHUNK, HD)
        mixed = mixed + contract_rows(values, low)
    total = jnp.sum(total, axis=0, keepdims=True)
    inverse = 1.0 / jnp.where(total > 0.5, total, 1.0)
    o_ref[0] = mixed * inverse
    inv_ref[0] = jnp.broadcast_to(inverse, (8, GROUP * tokens))


def attend(query, keys_values, rows):
    tokens = rows.shape[1]
    wide = GROUP * tokens
    length = N_CTX * tokens
    return pl.pallas_call(
        attend_kernel,
        name="attend",
        grid=(KV_HEADS,),
        in_specs=[
            pl.BlockSpec((1, wide, HD), lambda h: (h, 0, 0)),
            pl.BlockSpec((N_CTX, tokens + 16, HD), lambda h: (0, 0, h)),
            pl.BlockSpec((N_CTX, tokens + 16, HD), lambda h: (0, 0, KV_HEADS + h)),
            pl.BlockSpec((2, tokens), lambda h: (0, 0)),
        ],
        out_specs=[
            pl.BlockSpec((1, length, wide), lambda h: (h, 0, 0)),
            pl.BlockSpec((1, HD, wide), lambda h: (h, 0, 0)),
            pl.BlockSpec((1, 8, wide), lambda h: (h, 0, 0)),
        ],
        out_shape=[
            jax.ShapeDtypeStruct((KV_HEADS, length, wide), BF),
            jax.ShapeDtypeStruct((KV_HEADS, HD, wide), F32),
            jax.ShapeDtypeStruct((KV_HEADS, 8, wide), F32),
        ],
        scratch_shapes=[pltpu.VMEM((length, wide), F32)],
        compiler_params=pltpu.CompilerParams(vmem_limit_bytes=48 * 2**20),
        cost_estimate=pl.CostEstimate(
            flops=4 * KV_HEADS * length * wide * HD,
            bytes_accessed=2 * KV_HEADS * length * wide + 4 * 2**20,
            transcendentals=KV_HEADS * length * wide,
        ),
    )(query, keys_values, keys_values, rows)


def attend_back_kernel(
    e_ref, q_ref, k_ref, v_ref, g_ref, o_ref, inv_ref, dq_ref, dk_ref, dv_ref
):
    tokens = k_ref.shape[1] - 16
    length = N_CTX * tokens
    scale = HD ** (-0.5)
    query, grad = q_ref[0], g_ref[0]
    inverse = inv_ref[0, 0:1, :]
    grad_turned = grad.astype(F32).T
    weighted = jnp.sum(grad_turned * o_ref[0], axis=0, keepdims=True)
    factor = inverse * scale
    shift = weighted * factor
    grad_scaled = (grad_turned * inverse).T.astype(BF)
    turned = jnp.zeros((HD, GROUP * tokens), F32)
    for j in range(length // CHUNK):
        part = e_ref[0, j * CHUNK : (j + 1) * CHUNK, :]
        keys = k_ref[2 * j : 2 * j + 2, :tokens, :].reshape(CHUNK, HD)
        values = v_ref[2 * j : 2 * j + 2, :tokens, :].reshape(CHUNK, HD)
        prob_grad = contract_cols(values, grad)
        score_grad = (part.astype(F32) * (prob_grad * factor - shift)).astype(BF)
        dk = jnp.dot(score_grad, query, preferred_element_type=F32)
        dv = jnp.dot(part, grad_scaled, preferred_element_type=F32)
        dk_ref[2 * j : 2 * j + 2] = dk.reshape(2, tokens, HD).astype(dk_ref.dtype)
        dv_ref[2 * j : 2 * j + 2] = dv.reshape(2, tokens, HD).astype(dv_ref.dtype)
        turned = turned + contract_rows(keys, score_grad)
    dq_ref[0] = turned


def attend_back(expo, query, keys_values, grad, mixed, inverse):
    wide = query.shape[1]
    tokens = wide // GROUP
    length = N_CTX * tokens
    return pl.pallas_call(
        attend_back_kernel,
        name="attend_back",
        grid=(KV_HEADS,),
        in_specs=[
            pl.BlockSpec((1, length, wide), lambda h: (h, 0, 0)),
            pl.BlockSpec((1, wide, HD), lambda h: (h, 0, 0)),
            pl.BlockSpec((N_CTX, tokens + 16, HD), lambda h: (0, 0, h)),
            pl.BlockSpec((N_CTX, tokens + 16, HD), lambda h: (0, 0, KV_HEADS + h)),
            pl.BlockSpec((1, wide, HD), lambda h: (h, 0, 0)),
            pl.BlockSpec((1, HD, wide), lambda h: (h, 0, 0)),
            pl.BlockSpec((1, 8, wide), lambda h: (h, 0, 0)),
        ],
        out_specs=[
            pl.BlockSpec((1, HD, wide), lambda h: (h, 0, 0)),
            pl.BlockSpec((N_CTX, tokens, HD), lambda h: (0, 0, h)),
            pl.BlockSpec((N_CTX, tokens, HD), lambda h: (0, 0, h)),
        ],
        out_shape=[
            jax.ShapeDtypeStruct((KV_HEADS, HD, wide), F32),
            jax.ShapeDtypeStruct((N_CTX, tokens, KV_HEADS * HD), BF),
            jax.ShapeDtypeStruct((N_CTX, tokens, KV_HEADS * HD), BF),
        ],
        compiler_params=pltpu.CompilerParams(vmem_limit_bytes=48 * 2**20),
        cost_estimate=pl.CostEstimate(
            flops=8 * KV_HEADS * length * wide * HD,
            bytes_accessed=2 * KV_HEADS * length * wide + 6 * 2**20,
            transcendentals=0,
        ),
    )(expo, query, keys_values, keys_values, grad, mixed, inverse)


def body(
    layer_input,
    segments,
    positions,
    attn_norm,
    q_weight,
    q_bias,
    k_weight,
    k_bias,
    v_weight,
    v_bias,
    o_weight,
    mlp_norm,
    gate_weight,
    up_weight,
    down_weight,
    out_cotangent,
):
    tokens, width = layer_input.shape[1:]
    rows = gate_weight.shape[0]
    units = gate_weight.shape[1] // N_FS
    q_width = HEADS * HD
    kv_width = KV_HEADS * HD
    half_block = tokens // 2
    ctx = lax.axis_index("ctx")
    core = lax.rem(ctx, 2)
    pair = lax.div(ctx, 2)
    x_part = lax.rem(ctx, N_FS)
    inputs = layer_input[0].astype(F32)
    segment = segments[0]
    position = positions[0]
    keep = (segment > 0).astype(F32)[:, None]
    cotangent = out_cotangent[0].astype(F32) * keep
    cot_low = cotangent.astype(BF)

    cot_all = jnp.concatenate([cot_low] + [swap_fs(cot_low, i) for i in range(1, N_FS)], axis=0)

    qkv = jnp.concatenate([q_weight, k_weight, v_weight], axis=1).reshape(2, rows // 2, -1)
    small = jnp.concatenate([attn_norm, mlp_norm, q_bias, k_bias, v_bias]).reshape(-1, 128)
    small = jnp.pad(small, ((0, 16 - small.shape[0]), (0, 0)))
    cut = rows // 4
    start = lax.rem(x_part, 4) * cut
    gate_cut = lax.dynamic_slice_in_dim(gate_weight, start, cut, 0)
    up_cut = lax.dynamic_slice_in_dim(up_weight, start, cut, 0)
    blocks = (
        jnp.where(x_part < 4, gate_cut, up_cut).reshape(cut, N_FS, units).transpose(1, 0, 2)
    )
    full_qkv, small_all, blocks_here = exchange(
        first_kernel,
        "gather_qkv",
        1,
        (qkv, small, blocks),
        [
            ((N_FS,) + qkv.shape, BF),
            ((N_FS,) + small.shape, BF),
            (blocks.shape, BF),
        ],
        28,
        3,
    )
    along = [blocks_here] + [swap_ctx(blocks_here, 2 * i) for i in range(1, 4)]
    along = jnp.stack(along)
    other = swap_ctx(along, 1)
    x_here = lax.div(x_part, 2)
    both = jnp.where(core == 0, jnp.stack([along, other]), jnp.stack([other, along]))
    order = jnp.bitwise_xor(jnp.arange(4), x_here)
    both = jnp.take(both, order, axis=1)
    both = both.transpose(1, 0, 2, 3, 4).reshape(2, 4, N_FS, cut, units)
    both = both.transpose(0, 2, 1, 3, 4).reshape(2, width, units)
    gate_cols, up_cols = both[0], both[1]

    flat = small_all[:, :5].reshape(N_FS, -1)
    marks = [0, rows, 2 * rows, 2 * rows + q_width // N_FS]
    marks += [marks[-1] + kv_width // N_FS, marks[-1] + 2 * kv_width // N_FS]
    gain_one, gain_two, bias_q, bias_k, bias_v = (
        flat[:, lo:hi].reshape(-1).astype(F32) for lo, hi in zip(marks[:-1], marks[1:])
    )
    bias_all = jnp.concatenate([bias_q, bias_k, bias_v])
    full_qkv = full_qkv.reshape(width, q_width + 2 * kv_width)

    scale_one = lax.rsqrt(jnp.mean(inputs * inputs, axis=-1, keepdims=True) + EPSILON)
    norm_first = inputs * scale_one
    normed_in = (norm_first * gain_one).astype(BF)
    projected = jnp.dot(normed_in, full_qkv, preferred_element_type=F32) + bias_all
    cosine, sine = rope_tables(position, HD)
    turned = rotate(
        projected[:, : q_width + kv_width].reshape(tokens, HEADS + KV_HEADS, HD), cosine, sine
    ).astype(BF)
    value_low = projected[:, q_width + kv_width :].astype(BF)
    query = (
        turned[:, :HEADS]
        .reshape(tokens, KV_HEADS, GROUP, HD)
        .transpose(1, 2, 0, 3)
        .reshape(KV_HEADS, GROUP * tokens, HD)
    )
    keys_values = jnp.concatenate([turned[:, HEADS:].reshape(tokens, kv_width), value_low], axis=1)
    segment_rows = jnp.broadcast_to(
        jnp.tile(segment.astype(BF)[None, :], (1, 2 * KV_HEADS)), (16, 2 * kv_width)
    )
    keys_values = jnp.concatenate([keys_values, segment_rows], axis=0)
    kv_all, full_o = exchange(
        second_kernel,
        "gather_kv_o",
        2,
        (keys_values, o_weight.reshape(2, rows // 2, width)),
        [((N_CTX,) + keys_values.shape, BF), ((N_FS, 2, rows // 2, width), BF)],
        29,
        2,
    )
    full_o = full_o.reshape(q_width, width)
    within = jnp.arange(tokens, dtype=jnp.int32)
    row_place = jnp.where(
        within < half_block,
        ctx * half_block + within,
        (2 * N_CTX - 1 - ctx) * half_block + within - half_block,
    )
    row_info = jnp.stack([row_place.astype(F32), segment.astype(F32)])
    expo, mixed, inverse = attend(query, kv_all, row_info)
    attended = (
        mixed.reshape(KV_HEADS, HD, GROUP, tokens).transpose(3, 0, 2, 1).reshape(tokens, q_width)
    ).astype(BF)
    middle = inputs + jnp.dot(attended, full_o, preferred_element_type=F32)
    scale_two = lax.rsqrt(jnp.mean(middle * middle, axis=-1, keepdims=True) + EPSILON)
    norm_second = middle * scale_two
    normed_mid = (norm_second * gain_two).astype(BF)

    nm_all = jnp.concatenate(
        [normed_mid] + [swap_fs(normed_mid, i) for i in range(1, N_FS)], axis=0
    )
    act_grad = contract_cols(cot_all, down_weight)
    gate_pre = jnp.dot(nm_all, gate_cols, preferred_element_type=F32)
    up_pre = jnp.dot(nm_all, up_cols, preferred_element_type=F32)
    sigma = jax.nn.sigmoid(gate_pre)
    swish = gate_pre * sigma
    activation = (swish * up_pre).astype(BF)
    gate_grad = (act_grad * up_pre * sigma * (1.0 + gate_pre * (1.0 - sigma))).astype(BF)
    up_grad = (act_grad * swish).astype(BF)
    part_sum = (contract_cols(gate_grad, gate_cols) + contract_cols(up_grad, up_cols)).astype(BF)
    part_sum = part_sum.reshape(N_FS, tokens, width)
    mid_norm_grad = part_sum[0].astype(F32)
    for i in range(1, N_FS):
        mid_norm_grad = mid_norm_grad + swap_fs(part_sum[i], i).astype(F32)
    out_part = jnp.dot(activation, down_weight, preferred_element_type=F32).astype(BF)
    out_part = out_part.reshape(N_FS, tokens, width)
    output_rows = middle + out_part[0].astype(F32)
    for i in range(1, N_FS):
        output_rows = output_rows + swap_fs(out_part[i], i).astype(F32)
    output_rows = output_rows.astype(BF)

    piece = rows // 8
    gate_part = contract_rows(nm_all, gate_grad).astype(BF)
    up_part = contract_rows(nm_all, up_grad).astype(BF)
    down_part = contract_rows(activation, cot_all).astype(BF).reshape(2, units // 2, width)
    keep_gu = jnp.where(core == 0, gate_part, up_part)
    send_gu = jnp.where(core == 0, up_part, gate_part)
    keep_down = jnp.where(core == 0, down_part[0], down_part[1])
    send_down = jnp.where(core == 0, down_part[1], down_part[0])
    sum_gu = (keep_gu.astype(F32) + swap_ctx(send_gu, 1).astype(F32)).astype(BF)
    sum_down = (keep_down.astype(F32) + swap_ctx(send_down, 1).astype(F32)).astype(BF)
    sum_gu = sum_gu.reshape(N_FS, 8, piece, units)
    sum_down = sum_down.reshape(8, units // 16, width)
    far_gu, far_down = scatter_ctx("scatter_mlp", 3, (sum_gu, sum_down))
    done_gu = (
        lax.dynamic_index_in_dim(sum_gu, pair, 1, False).astype(F32)
        + jnp.sum(far_gu.astype(F32), axis=0)
    ).astype(BF)
    done_down = (
        lax.dynamic_index_in_dim(sum_down, pair, 0, False).astype(F32)
        + jnp.sum(far_down.astype(F32), axis=0)
    ).astype(BF)

    gain_two_grad = jnp.sum(mid_norm_grad * norm_second, axis=0)
    scaled_two = mid_norm_grad * gain_two
    mid_grad = cotangent + scale_two * (
        scaled_two - norm_second * jnp.mean(scaled_two * norm_second, axis=-1, keepdims=True)
    )
    branch_low = mid_grad.astype(BF)
    attended_grad = contract_cols(branch_low, full_o).astype(BF)
    grad_rows = (
        attended_grad.reshape(tokens, KV_HEADS, GROUP, HD)
        .transpose(1, 2, 0, 3)
        .reshape(KV_HEADS, GROUP * tokens, HD)
    )
    turned_grad, key_part, value_part = attend_back(
        expo, query, kv_all, grad_rows, mixed, inverse
    )
    kv_part = jnp.concatenate([key_part, value_part], axis=2)
    kv_part = kv_part.reshape(N_CTX // 2, 2, tokens, 2 * kv_width)
    keep_kv = jnp.where(core == 0, kv_part[:, 0], kv_part[:, 1])
    send_kv = jnp.where(core == 0, kv_part[:, 1], kv_part[:, 0])
    sum_kv = (keep_kv.astype(F32) + swap_ctx(send_kv, 1).astype(F32)).astype(BF)
    (far_kv,) = scatter_ctx("scatter_kv", 4, (sum_kv,))
    own_kv = lax.dynamic_index_in_dim(sum_kv, pair, 0, False).astype(F32) + jnp.sum(
        far_kv.astype(F32), axis=0
    )
    query_rot_grad = (
        turned_grad.reshape(KV_HEADS, HD, GROUP, tokens)
        .transpose(3, 0, 2, 1)
        .reshape(tokens, HEADS, HD)
    )
    turned_back = rotate(
        jnp.concatenate(
            [query_rot_grad, own_kv[:, :kv_width].reshape(tokens, KV_HEADS, HD)], axis=1
        ),
        cosine,
        -sine,
    ).reshape(tokens, q_width + kv_width)
    proj_grad = jnp.concatenate([turned_back, own_kv[:, kv_width:]], axis=1).astype(BF)
    bias_grads = jnp.sum(proj_grad.astype(F32), axis=0)
    in_norm_grad = contract_cols(proj_grad, full_qkv)
    gain_one_grad = jnp.sum(in_norm_grad * norm_first, axis=0)
    scaled_one = in_norm_grad * gain_one
    input_rows = mid_grad + scale_one * (
        scaled_one - norm_first * jnp.mean(scaled_one * norm_first, axis=-1, keepdims=True)
    )

    q_part = contract_rows(normed_in, proj_grad).astype(BF)
    o_part = contract_rows(attended, branch_low).astype(BF)
    side = q_width // 2
    low_side = jnp.concatenate(
        [o_part[:, :side], q_part[:, :side], q_part[:, q_width : q_width + kv_width]], axis=1
    )
    high_side = jnp.concatenate(
        [o_part[:, side:], q_part[:, side:q_width], q_part[:, q_width + kv_width :]], axis=1
    )
    keep_at = jnp.where(core == 0, low_side, high_side)
    send_at = jnp.where(core == 0, high_side, low_side)
    sum_at = (keep_at.astype(F32) + swap_ctx(send_at, 1).astype(F32)).astype(BF)
    sum_at = sum_at.reshape(N_FS, 8, piece, -1)
    (far_at,) = scatter_ctx("scatter_attn", 5, (sum_at,))
    done_at = (
        lax.dynamic_index_in_dim(sum_at, pair, 1, False).astype(F32)
        + jnp.sum(far_at.astype(F32), axis=0)
    ).astype(BF)

    vectors = jnp.concatenate(
        [
            v.reshape(N_FS, -1)
            for v in (
                gain_one_grad,
                gain_two_grad,
                bias_grads[:q_width],
                bias_grads[q_width : q_width + kv_width],
                bias_grads[q_width + kv_width :],
            )
        ],
        axis=1,
    ).reshape(N_FS, 5, 128)
    vectors = jnp.pad(vectors, ((0, 0), (0, 3), (0, 0)))
    own_gu, own_at, own_vec = to_owner("to_owner", 6, (done_gu, done_at, vectors))
    own_at = jnp.sum(own_at.astype(F32), axis=0).astype(BF)
    own_vec = jnp.sum(own_vec, axis=0)
    all_gu, all_at, all_down, all_vec = gather_ctx(
        "gather_grads", 7, (own_gu, own_at, done_down, own_vec)
    )
    all_vec = jnp.sum(all_vec, axis=0)[:5].reshape(-1)
    sum_vec = [all_vec[lo:hi] for lo, hi in zip(marks[:-1], marks[1:])]
    all_gu = all_gu.reshape(8, 2, N_FS, piece, units).transpose(1, 0, 3, 2, 4)
    all_gu = all_gu.reshape(2, rows, N_FS * units)
    all_at = all_at.reshape(8, 2, piece, -1).transpose(1, 0, 2, 3).reshape(2, rows, -1)
    all_down = all_down.reshape(8, 2, units // 16, width).transpose(1, 0, 2, 3)
    o_grad = jnp.concatenate([all_at[0, :, :side], all_at[1, :, :side]], axis=1).astype(F32)
    q_grad = jnp.concatenate(
        [all_at[0, :, side:q_width], all_at[1, :, side:q_width]], axis=1
    ).astype(F32)
    return (
        output_rows[None],
        input_rows[None],
        sum_vec[0],
        q_grad,
        sum_vec[2],
        all_at[0, :, q_width:].astype(F32),
        sum_vec[3],
        all_at[1, :, q_width:].astype(F32),
        sum_vec[4],
        o_grad,
        sum_vec[1],
        all_gu[0].astype(F32),
        all_gu[1].astype(F32),
        all_down.reshape(units, width).astype(F32),
    )


def solution(mesh):
    placed = (
        P("fsdp", "ctx", None),
        P("fsdp", "ctx"),
        P("fsdp", "ctx"),
        P("fsdp"),
        P("fsdp", None),
        P("fsdp"),
        P("fsdp", None),
        P("fsdp"),
        P("fsdp", None),
        P("fsdp"),
        P("fsdp", None),
        P("fsdp"),
        P("fsdp", None),
        P("fsdp", None),
        P("fsdp", None),
        P("fsdp", "ctx", None),
    )
    return jax.shard_map(
        body,
        mesh=mesh,
        in_specs=placed,
        out_specs=(
            P("fsdp", "ctx", None),
            P("fsdp", "ctx", None),
            P("fsdp"),
            P("fsdp", None),
            P("fsdp"),
            P("fsdp", None),
            P("fsdp"),
            P("fsdp", None),
            P("fsdp"),
            P("fsdp", None),
            P("fsdp"),
            P("fsdp", None),
            P("fsdp", None),
            P("fsdp", None),
        ),
        check_vma=False,
    )
```

time: 2490 us -> 864 us (0.35)
  waiting for transfers between devices: 1990 us -> 103 us
  Pallas kernels: 0 us -> 407 us
  blocking collectives: 173 us -> 0 us
  matrix products: 230 us -> 74.9 us
  local copies, waits for them, and re-layouts: 28.7 us -> 109 us
  other arithmetic: 35.1 us -> 107 us
  starting transfers between devices: 0.56 us -> 47 us
    reduce_scatter x6 -> x0, waiting for transfers between devices: 991 us -> none  [the longest x1 528 us: body(): lax.psum_scatter(contract_rows(normed_mid, both_grad).astype(jnp.bfloat16...]
    all_gather x7 -> x0, waiting for transfers between devices: 906 us -> none  [the longest x1 268 us: body(): lax.all_gather(gate_weight, 'fsdp', axis=0, tiled=True)]
    pallas_call x0 -> x9, Pallas kernels: none -> 407 us  [the longest x7 390 us: exchange(): pl.pallas_call(kernel, name=name, out_shape=[jax.ShapeDtypeStruct(s, d) f...]
    ppermute x0 -> x36, waiting for transfers between devices: none -> 103 us  [the longest x28 103 us: swap_fs(): return lax.ppermute(value, 'fsdp', [(s, s ^ mask) for s in range(N_FS)])]
    psum x1 -> x0, waiting for transfers between devices: 89 us -> none  [body(): lax.psum(proj_share[:, :q_width].astype(jnp.bfloat16), 'ctx')]
    dot_general x12 -> x5, matrix products: 113 us -> 24.6 us  [the longest x1 5.81 us: body(): up_pre = jnp.dot(nm_all, up_cols, preferred_element_type=F32)]
    all_gather x3 -> x0, blocking collectives: 87.2 us -> none  [the longest x1 39.6 us: body(): lax.all_gather(segment.astype(jnp.bfloat16), 'ctx', axis=0, tiled=True)]
    unnamed x2 -> x0, blocking collectives: 51 us -> none
  transfers between devices with their start and end apart: 14 -> 36, of which waited for: 13 -> 15; matrix products, arithmetic and copies ran while one was open for 7% -> 15% of each run, Pallas kernels for 0% -> 26%
where the time goes in v1:
time: 864 us; the launch traced here: 850 us
  Pallas kernels  407 us (47%)
  local copies, waits for them, and re-layouts  109 us (13%)
  other arithmetic  107 us (12%)
  waiting for transfers between devices  103 us (12%)
  matrix products  74.9 us (9%)
  starting transfers between devices  47 us (5%)
    pallas_call x7, Pallas kernels, exchange(): pl.pallas_call(kernel, name=name, out_shape=[jax.ShapeDtypeStruct(s, d) f...  390 us
    ppermute x28, waiting for transfers between devices, swap_fs(): return lax.ppermute(value, 'fsdp', [(s, s ^ mask) for s in range(N_FS)])  103 us
    ppermute x28, starting transfers between devices, swap_fs(): return lax.ppermute(value, 'fsdp', [(s, s ^ mask) for s in range(N_FS)])  32.2 us
    dot_general x5, matrix products, contract_cols(): lax.dot_general(left, right, (((1,), (1,)), ((), ())), preferred_element_...  26.9 us
    dot_general x5, matrix products, contract_rows(): lax.dot_general(left, right, (((0,), (0,)), ((), ())), preferred_element_...  23.4 us
    unnamed x120, local copies, waits for them, and re-layouts  17.4 us
  transfers between devices with their start and end apart: 36, of which 15 were waited for; matrix products, arithmetic and copies ran while one was open for 15% of the time, Pallas kernels for 26%

profile of v1, /device:TPU:35, one launch (start us, length us, event | category | flops | bytes accessed | tf_op | source)
XLA Modules:
  0.0 850.1 jit_solution(4357333852302132534)
XLA Ops:
  20.4 54.4 %gather_qkv.1 = (bf16[8,2,96,2048]{3,2,1,0:T(8,128)(2,1)}, bf16[8,16,128]{2,1,0:T(8,128)(2,1)}, bf16[8,48,1120]{2,1,0:T(8,128)(2,1)}) custom-call(bf16[2,96,2048]{2,1,0:T(8,128)(2,1)} %bitcast.235, bf16[16,128]{1,0:T(8,128)(2,1)} %pad.8.s_ref, bf16[8,48,1120]{2,1,0:T(8,128)(2,1)} %bitcast.233), custom_call_target="tpu_custom_call" | custom-call | tf_op jit(solution)/shard_map/gather_qkv/pallas_call | solution.py:89
  97.9 52.1 %gather_kv_o.1 = (bf16[16,144,512]{2,1,0:T(8,128)(2,1)}, bf16[8,2,96,1536]{3,2,1,0:T(8,128)(2,1)}) custom-call(bf16[144,512]{1,0:T(8,128)(2,1)} %pad_maximum_fusion.10.kv_ref, bf16[2,96,1536]{2,1,0:T(8,128)(2,1)} %bitcast.242), custom_call_target="tpu_custom_call" | custom-call | tf_op jit(solution)/shard_map/gather_kv_o/pallas_call | solution.py:89
  152.6 8.2 attend.1
  181.3 11.9 %collective-permute-done.18 = bf16[128,1536]{1,0:T(8,128)(2,1)} collective-permute-done((bf16[128,1536]{1,0:T(8,128)(2,1)}, bf16[128,1536]{1,0:T(8,128)(2,1)}, u32[]{:S(2)}, u32[]{:S(2)}) %collective-permute-start.18) | collective-permute-done | bytes 393248 | tf_op jit(solution)/shard_map/ppermute | solution.py:268
  209.1 8.7 %collective-permute-done.22 = bf16[128,1536]{1,0:T(8,128)(2,1)S(1)} collective-permute-done((bf16[128,1536]{1,0:T(8,128)(2,1)}, bf16[128,1536]{1,0:T(8,128)(2,1)S(1)}, u32[]{:S(2)}, u32[]{:S(2)}) %collective-permute-start.22) | collective-permute-done | bytes 393248 | tf_op jit(solution)/shard_map/ppermute | solution.py:268
  227.4 7.7 collective-permute-done
  235.2 7.8 collective-permute-done.1
  250.2 7.5 collective-permute-done.4
  259.5 7.4 maximum_select_fusion
  296.7 8.5 multiply_convert_fusion
  339.9 10.6 %collective-permute-done.31 = bf16[128,1536]{1,0:T(8,128)(2,1)S(1)} collective-permute-done((bf16[128,1536]{1,0:T(8,128)(2,1)S(1)}, bf16[128,1536]{1,0:T(8,128)(2,1)S(1)}, u32[]{:S(2)}, u32[]{:S(2)}) %collective-permute-start.31) | collective-permute-done | bytes 393248 | tf_op jit(solution)/shard_map/ppermute | solution.py:268
  355.3 18.6 %collective-permute-done.28 = bf16[128,1536]{1,0:T(8,128)(2,1)S(1)} collective-permute-done((bf16[128,1536]{1,0:T(8,128)(2,1)S(1)}, bf16[128,1536]{1,0:T(8,128)(2,1)S(1)}, u32[]{:S(2)}, u32[]{:S(2)}) %collective-permute-start.28) | collective-permute-done | bytes 393248 | tf_op jit(solution)/shard_map/ppermute | solution.py:268
  386.5 9.0 %collective-permute-start.34 = (bf16[560,1536]{1,0:T(8,128)(2,1)}, bf16[560,1536]{1,0:T(8,128)(2,1)}, u32[]{:S(2)}, u32[]{:S(2)}) collective-permute-start(bf16[560,1536]{1,0:T(8,128)(2,1)} %broadcast_select_fusion.3), channel_id=1, source_target_pairs={{0,8},{8,0},{16,24},{24,16},{32,40},{40,32},{48,56},{56,48},{64,72... | collective-permute-start | bytes 5160968 | tf_op jit(solution)/shard_map/ppermute | solution.py:272
  397.9 9.2 %collective-permute-done.14 = bf16[128,1536]{1,0:T(8,128)(2,1)S(1)} collective-permute-done((bf16[128,1536]{1,0:T(8,128)(2,1)S(1)}, bf16[128,1536]{1,0:T(8,128)(2,1)S(1)}, u32[]{:S(2)}, u32[]{:S(2)}) %collective-permute-start.14) | collective-permute-done | bytes 393248 | tf_op jit(solution)/shard_map/ppermute | solution.py:268
  410.9 9.5 %attend_back.1 = (f32[2,128,768]{2,1,0:T(8,128)S(1)}, bf16[16,128,256]{2,1,0:T(8,128)(2,1)S(1)}, bf16[16,128,256]{2,1,0:T(8,128)(2,1)S(1)}) custom-call(bf16[2,2048,768]{2,1,0:T(8,128)(2,1)} %get-tuple-element.40.e_ref, bf16[2,768,128]{2,1,0:T(8,128)(2,1)S(1)} %bitcast.203, bf16[16,144,512]{2,1,0:T(8,128)(2,1)} %get-tuple-element.36.k_ref.v_ref, ...), custom_call_target="tpu_custom_call" | custom-call | flops 3221225472 | bytes 12582912 | tf_op jit(solution)/shard_map/attend_back/pallas_call | solution.py:388
  438.6 20.8 %scatter_kv.1 = bf16[7,128,512]{2,1,0:T(8,128)(2,1)} custom-call(bf16[8,128,512]{2,1,0:T(8,128)(2,1)} %fusion.1.refs_0_), custom_call_target="tpu_custom_call" | custom-call | tf_op jit(solution)/shard_map/scatter_kv/pallas_call | solution.py:89
  500.6 76.0 %scatter_mlp.1 = (bf16[7,8,24,1120]{3,2,1,0:T(8,128)(2,1)}, bf16[7,70,1536]{2,1,0:T(8,128)(2,1)}) custom-call(bf16[8,8,24,1120]{3,2,1,0:T(8,128)(2,1)} %bitcast.218, bf16[8,70,1536]{2,1,0:T(8,128)(2,1)} %reshape.466.refs_1_), custom_call_target="tpu_custom_call" | custom-call | tf_op jit(solution)/shard_map/scatter_mlp/pallas_call | solution.py:89
  591.8 8.3 copy.57
  600.1 78.3 %scatter_attn.1 = bf16[7,8,24,1792]{3,2,1,0:T(8,128)(2,1)} custom-call(bf16[8,8,24,1792]{3,2,1,0:T(8,128)(2,1)} %bitcast.210), custom_call_target="tpu_custom_call" | custom-call | tf_op jit(solution)/shard_map/scatter_attn/pallas_call | solution.py:89
  683.7 18.4 %to_owner.1 = (bf16[8,24,1120]{2,1,0:T(8,128)(2,1)}, bf16[8,24,1792]{2,1,0:T(8,128)(2,1)}, f32[8,8,128]{2,1,0:T(8,128)}) custom-call(bf16[8,24,1120]{2,1,0:T(8,128)(2,1)} %fusion.9.refs_0_, bf16[8,24,1792]{2,1,0:T(8,128)(2,1)} %fusion.2.refs_1_, f32[8,8,128]{2,1,0:T(8,128)} %pad.9.refs_2_), custom_call_target="tpu_custom_call" | custom-call | tf_op jit(solution)/shard_map/to_owner/pallas_call | solution.py:89
  705.3 89.6 %gather_grads.1 = (bf16[16,8,24,1120]{3,2,1,0:T(8,128)(2,1)}, bf16[16,24,1792]{2,1,0:T(8,128)(2,1)}, bf16[16,70,1536]{2,1,0:T(8,128)(2,1)}, f32[16,8,128]{2,1,0:T(8,128)}) custom-call(bf16[8,24,1120]{2,1,0:T(8,128)(2,1)} %get-tuple-element.46.refs_0_, bf16[24,1792]{1,0:T(8,128)(2,1)} %reduce_sum.139.refs_1_, bf16[70,1536]{1,0:T(8,128)(2,1)} %fusion.23.refs_2_, ...), custom_call_target="tpu_custom_call" | custom-call | tf_op jit(solution)/shard_map/gather_grads/pallas_call | solution.py:89
  810.6 7.5 slice_convert_fusion
  822.2 7.9 reshape.491
  837.2 8.1 reshape.490
  (311 shorter events, 302.0 us)
Async XLA Ops:
  4.1 220.5 %collective-permute-start.24 = (bf16[128,1536]{1,0:T(8,128)(2,1)}, bf16[128,1536]{1,0:T(8,128)(2,1)}, u32[]{:S(2)}, u32[]{:S(2)}) collective-permute-start(bf16[128,1536]{1,0:T(8,128)(2,1)} %get-tuple-element.60), channel_id=1, source_target_pairs={{0,7},{1,6},{2,5},{3,4},{4,3},{5,2},{6,1},{7,0},{8,15},{9,14},{10,... | collective-permute-start | bytes 1179656 | tf_op jit(solution)/shard_map/ppermute | solution.py:268
  6.4 214.8 %collective-permute-start.23 = (bf16[128,1536]{1,0:T(8,128)(2,1)}, bf16[128,1536]{1,0:T(8,128)(2,1)}, u32[]{:S(2)}, u32[]{:S(2)}) collective-permute-start(bf16[128,1536]{1,0:T(8,128)(2,1)} %get-tuple-element.60), channel_id=1, source_target_pairs={{0,6},{1,7},{2,4},{3,5},{4,2},{5,3},{6,0},{7,1},{8,14},{9,15},{10,... | collective-permute-start | bytes 1179656 | tf_op jit(solution)/shard_map/ppermute | solution.py:268
  74.8 99.2 %collective-permute-start.9 = (bf16[8,48,1120]{2,1,0:T(8,128)(2,1)}, bf16[8,48,1120]{2,1,0:T(8,128)(2,1)}, u32[]{:S(2)}, u32[]{:S(2)}) collective-permute-start(bf16[8,48,1120]{2,1,0:T(8,128)(2,1)} %get-tuple-element.39), channel_id=1, source_target_pairs={{0,48},{8,56},{16,32},{24,40},{32,16},{40,24},{48,0},{56,8},{64,11... | collective-permute-start | bytes 2580488 | tf_op jit(solution)/shard_map/ppermute | solution.py:272
  76.1 100.1 %collective-permute-start.8 = (bf16[8,48,1120]{2,1,0:T(8,128)(2,1)}, bf16[8,48,1120]{2,1,0:T(8,128)(2,1)}, u32[]{:S(2)}, u32[]{:S(2)}) collective-permute-start(bf16[8,48,1120]{2,1,0:T(8,128)(2,1)} %get-tuple-element.39), channel_id=1, source_target_pairs={{0,32},{8,40},{16,48},{24,56},{32,0},{40,8},{48,16},{56,24},{64,96... | collective-permute-start | bytes 2580488 | tf_op jit(solution)/shard_map/ppermute | solution.py:272
  76.9 99.2 %collective-permute-start.7 = (bf16[8,48,1120]{2,1,0:T(8,128)(2,1)}, bf16[8,48,1120]{2,1,0:T(8,128)(2,1)}, u32[]{:S(2)}, u32[]{:S(2)}) collective-permute-start(bf16[8,48,1120]{2,1,0:T(8,128)(2,1)} %get-tuple-element.39), channel_id=1, source_target_pairs={{0,16},{8,24},{16,0},{24,8},{32,48},{40,56},{48,32},{56,40},{64,80... | collective-permute-start | bytes 2580488 | tf_op jit(solution)/shard_map/ppermute | solution.py:272
  174.0 23.0 %collective-permute-start.19 = (bf16[128,1536]{1,0:T(8,128)(2,1)}, bf16[128,1536]{1,0:T(8,128)(2,1)}, u32[]{:S(2)}, u32[]{:S(2)}) collective-permute-start(bf16[128,1536]{1,0:T(8,128)(2,1)} %get-tuple-element.60), channel_id=1, source_target_pairs={{0,2},{1,3},{2,0},{3,1},{4,6},{5,7},{6,4},{7,5},{8,10},{9,11},{10,... | collective-permute-start | bytes 1179656 | tf_op jit(solution)/shard_map/ppermute | solution.py:268
  176.2 17.1 %collective-permute-start.18 = (bf16[128,1536]{1,0:T(8,128)(2,1)}, bf16[128,1536]{1,0:T(8,128)(2,1)}, u32[]{:S(2)}, u32[]{:S(2)}) collective-permute-start(bf16[128,1536]{1,0:T(8,128)(2,1)} %get-tuple-element.60), channel_id=1, source_target_pairs={{0,1},{1,0},{2,3},{3,2},{4,5},{5,4},{6,7},{7,6},{8,9},{9,8},{10,11... | collective-permute-start | bytes 1179656 | tf_op jit(solution)/shard_map/ppermute | solution.py:268
  180.9 78.6 %collective-permute-start.10 = (bf16[4,8,48,1120]{3,2,1,0:T(8,128)(2,1)}, bf16[4,8,48,1120]{3,2,1,0:T(8,128)(2,1)}, u32[]{:S(2)}, u32[]{:S(2)}) collective-permute-start(bf16[4,8,48,1120]{3,2,1,0:T(8,128)(2,1)} %get-tuple-element.77), channel_id=1, source_target_pairs={{0,8},{8,0},{16,24},{24,16},{32,40},{40,32},{48,56},{56,48},{64,72... | collective-permute-start | bytes 10321928 | tf_op jit(solution)/shard_map/ppermute | solution.py:272
  206.6 51.2 %collective-permute-start.6 = (bf16[128,1536]{1,0:T(8,128)(2,1)}, bf16[128,1536]{1,0:T(8,128)(2,1)S(1)}, u32[]{:S(2)}, u32[]{:S(2)}) collective-permute-start(bf16[128,1536]{1,0:T(8,128)(2,1)} %get-tuple-element.62), channel_id=1, source_target_pairs={{0,7},{1,6},{2,5},{3,4},{4,3},{5,2},{6,1},{7,0},{8,15},{9,14},{10,... | collective-permute-start | bytes 1179656 | tf_op jit(solution)/shard_map/ppermute | solution.py:268
  217.8 40.0 %collective-permute-start.5 = (bf16[128,1536]{1,0:T(8,128)(2,1)}, bf16[128,1536]{1,0:T(8,128)(2,1)S(1)}, u32[]{:S(2)}, u32[]{:S(2)}) collective-permute-start(bf16[128,1536]{1,0:T(8,128)(2,1)} %get-tuple-element.62), channel_id=1, source_target_pairs={{0,6},{1,7},{2,4},{3,5},{4,2},{5,3},{6,0},{7,1},{8,14},{9,15},{10,... | collective-permute-start | bytes 1179656 | tf_op jit(solution)/shard_map/ppermute | solution.py:268
  224.6 18.5 %collective-permute-start.1 = (bf16[128,1536]{1,0:T(8,128)(2,1)S(1)}, bf16[128,1536]{1,0:T(8,128)(2,1)S(1)}, u32[]{:S(2)}, u32[]{:S(2)}) collective-permute-start(bf16[128,1536]{1,0:T(8,128)(2,1)S(1)} %copy-done.28), channel_id=1, source_target_pairs={{0,2},{1,3},{2,0},{3,1},{4,6},{5,7},{6,4},{7,5},{8,10},{9,11},{10,... | collective-permute-start | bytes 1179656 | tf_op jit(solution)/shard_map/ppermute | solution.py:268
  333.3 17.2 %collective-permute-start.31 = (bf16[128,1536]{1,0:T(8,128)(2,1)S(1)}, bf16[128,1536]{1,0:T(8,128)(2,1)S(1)}, u32[]{:S(2)}, u32[]{:S(2)}) collective-permute-start(bf16[128,1536]{1,0:T(8,128)(2,1)S(1)} %get-tuple-element.79), channel_id=1, source_target_pairs={{0,7},{1,6},{2,5},{3,4},{4,3},{5,2},{6,1},{7,0},{8,15},{9,14},{10,... | collective-permute-start | bytes 1179656 | tf_op jit(solution)/shard_map/ppermute | solution.py:268
  337.4 36.4 %collective-permute-start.28 = (bf16[128,1536]{1,0:T(8,128)(2,1)S(1)}, bf16[128,1536]{1,0:T(8,128)(2,1)S(1)}, u32[]{:S(2)}, u32[]{:S(2)}) collective-permute-start(bf16[128,1536]{1,0:T(8,128)(2,1)S(1)} %get-tuple-element.82), channel_id=1, source_target_pairs={{0,4},{1,5},{2,6},{3,7},{4,0},{5,1},{6,2},{7,3},{8,12},{9,13},{10,... | collective-permute-start | bytes 1179656 | tf_op jit(solution)/shard_map/ppermute | solution.py:268
  339.9 36.6 %collective-permute-start.27 = (bf16[128,1536]{1,0:T(8,128)(2,1)S(1)}, bf16[128,1536]{1,0:T(8,128)(2,1)S(1)}, u32[]{:S(2)}, u32[]{:S(2)}) collective-permute-start(bf16[128,1536]{1,0:T(8,128)(2,1)S(1)} %get-tuple-element.83), channel_id=1, source_target_pairs={{0,3},{1,2},{2,1},{3,0},{4,7},{5,6},{6,5},{7,4},{8,11},{9,10},{10,... | collective-permute-start | bytes 1179656 | tf_op jit(solution)/shard_map/ppermute | solution.py:268
  350.4 26.6 %collective-permute-start.26 = (bf16[128,1536]{1,0:T(8,128)(2,1)S(1)}, bf16[128,1536]{1,0:T(8,128)(2,1)S(1)}, u32[]{:S(2)}, u32[]{:S(2)}) collective-permute-start(bf16[128,1536]{1,0:T(8,128)(2,1)S(1)} %get-tuple-element.84), channel_id=1, source_target_pairs={{0,2},{1,3},{2,0},{3,1},{4,6},{5,7},{6,4},{7,5},{8,10},{9,11},{10,... | collective-permute-start | bytes 1179656 | tf_op jit(solution)/shard_map/ppermute | solution.py:268
  350.4 26.6 %collective-permute-start.11 = (bf16[128,1536]{1,0:T(8,128)(2,1)S(1)}, bf16[128,1536]{1,0:T(8,128)(2,1)S(1)}, u32[]{:S(2)}, u32[]{:S(2)}) collective-permute-start(bf16[128,1536]{1,0:T(8,128)(2,1)S(1)} %get-tuple-element.85), channel_id=1, source_target_pairs={{0,1},{1,0},{2,3},{3,2},{4,5},{5,4},{6,7},{7,6},{8,9},{9,8},{10,11... | collective-permute-start | bytes 1179656 | tf_op jit(solution)/shard_map/ppermute | solution.py:268
  352.8 27.5 %collective-permute-start.17 = (bf16[128,1536]{1,0:T(8,128)(2,1)S(1)}, bf16[128,1536]{1,0:T(8,128)(2,1)S(1)}, u32[]{:S(2)}, u32[]{:S(2)}) collective-permute-start(bf16[128,1536]{1,0:T(8,128)(2,1)S(1)} %get-tuple-element.86), channel_id=1, source_target_pairs={{0,7},{1,6},{2,5},{3,4},{4,3},{5,2},{6,1},{7,0},{8,15},{9,14},{10,... | collective-permute-start | bytes 1179656 | tf_op jit(solution)/shard_map/ppermute | solution.py:268
  376.5 21.5 %collective-permute-start.15 = (bf16[128,1536]{1,0:T(8,128)(2,1)S(1)}, bf16[128,1536]{1,0:T(8,128)(2,1)S(1)}, u32[]{:S(2)}, u32[]{:S(2)}) collective-permute-start(bf16[128,1536]{1,0:T(8,128)(2,1)S(1)} %get-tuple-element.88), channel_id=1, source_target_pairs={{0,5},{1,4},{2,7},{3,6},{4,1},{5,0},{6,3},{7,2},{8,13},{9,12},{10,... | collective-permute-start | bytes 1179656 | tf_op jit(solution)/shard_map/ppermute | solution.py:268
  377.0 30.1 %collective-permute-start.14 = (bf16[128,1536]{1,0:T(8,128)(2,1)S(1)}, bf16[128,1536]{1,0:T(8,128)(2,1)S(1)}, u32[]{:S(2)}, u32[]{:S(2)}) collective-permute-start(bf16[128,1536]{1,0:T(8,128)(2,1)S(1)} %get-tuple-element.89), channel_id=1, source_target_pairs={{0,4},{1,5},{2,6},{3,7},{4,0},{5,1},{6,2},{7,3},{8,12},{9,13},{10,... | collective-permute-start | bytes 1179656 | tf_op jit(solution)/shard_map/ppermute | solution.py:268
  377.0 30.1 %collective-permute-start.13 = (bf16[128,1536]{1,0:T(8,128)(2,1)S(1)}, bf16[128,1536]{1,0:T(8,128)(2,1)S(1)}, u32[]{:S(2)}, u32[]{:S(2)}) collective-permute-start(bf16[128,1536]{1,0:T(8,128)(2,1)S(1)} %get-tuple-element.90), channel_id=1, source_target_pairs={{0,3},{1,2},{2,1},{3,0},{4,7},{5,6},{6,5},{7,4},{8,11},{9,10},{10,... | collective-permute-start | bytes 1179656 | tf_op jit(solution)/shard_map/ppermute | solution.py:268
  380.3 26.8 %collective-permute-start.12 = (bf16[128,1536]{1,0:T(8,128)(2,1)S(1)}, bf16[128,1536]{1,0:T(8,128)(2,1)S(1)}, u32[]{:S(2)}, u32[]{:S(2)}) collective-permute-start(bf16[128,1536]{1,0:T(8,128)(2,1)S(1)} %get-tuple-element.91), channel_id=1, source_target_pairs={{0,2},{1,3},{2,0},{3,1},{4,6},{5,7},{6,4},{7,5},{8,10},{9,11},{10,... | collective-permute-start | bytes 1179656 | tf_op jit(solution)/shard_map/ppermute | solution.py:268
  386.5 95.2 %collective-permute-start.34 = (bf16[560,1536]{1,0:T(8,128)(2,1)}, bf16[560,1536]{1,0:T(8,128)(2,1)}, u32[]{:S(2)}, u32[]{:S(2)}) collective-permute-start(bf16[560,1536]{1,0:T(8,128)(2,1)} %broadcast_select_fusion.3), channel_id=1, source_target_pairs={{0,8},{8,0},{16,24},{24,16},{32,40},{40,32},{48,56},{56,48},{64,72... | collective-permute-start | bytes 5160968 | tf_op jit(solution)/shard_map/ppermute | solution.py:272
  430.2 58.6 %collective-permute-start.33 = (bf16[1536,1120]{0,1:T(8,128)(2,1)}, bf16[1536,1120]{0,1:T(8,128)(2,1)}, u32[]{:S(2)}, u32[]{:S(2)}) collective-permute-start(bf16[1536,1120]{0,1:T(8,128)(2,1)} %get-tuple-element.124), channel_id=1, source_target_pairs={{0,8},{8,0},{16,24},{24,16},{32,40},{40,32},{48,56},{56,48},{64,72... | collective-permute-start | bytes 10321928 | tf_op jit(solution)/shard_map/ppermute | solution.py:272
  471.0 113.6 %collective-permute-start.35 = (bf16[1536,1792]{0,1:T(8,128)(2,1)}, bf16[1536,1792]{0,1:T(8,128)(2,1)}, u32[]{:S(2)}, u32[]{:S(2)}) collective-permute-start(bf16[1536,1792]{0,1:T(8,128)(2,1)} %broadcast_select_fusion.1), channel_id=1, source_target_pairs={{0,8},{8,0},{16,24},{24,16},{32,40},{40,32},{48,56},{56,48},{64,72... | collective-permute-start | bytes 16515080 | tf_op jit(solution)/shard_map/ppermute | solution.py:272
  (65 other events, 1164.2 us)

commit v2 on v1

--- a/solution.py
+++ b/solution.py
@@ -106,29 +106,50 @@
     core = lax.rem(c, 2)
     sibling = (flip(c, 1), f)
     peers = [(c, flip(f, i)) for i in range(1, N_FS)]
-    greet(peers + [sibling])
+    along = [(flip(c, 2 * i), f) for i in range(1, 4)]
+    greet(peers + along + [sibling])
     copies = Copies(send, recv)
+
+    def columns(device):
+        part = lax.rem(device[0], N_FS)
+        return g_out.at[lax.div(part, 4), :, lax.rem(part, 4)]
+
+    def block(device, source):
+        part = lax.rem(device[0], N_FS)
+        return g_out.at[lax.div(part, 4), source, lax.rem(part, 4)]
+
+    here = (c, f)
     own = [
+        pltpu.make_async_copy(g_ref.at[f], block(here, f), local.at[2]),
         pltpu.make_async_copy(w_ref, w_out.at[f], local.at[0]),
         pltpu.make_async_copy(s_ref, s_out.at[f], local.at[1]),
-        pltpu.make_async_copy(g_ref.at[f], g_out.at[f], local.at[2]),
     ]
     for copy in own:
         copy.start()
     rest = [copies.start(s_ref, s_out.at[f], peer) for peer in peers]
+    blocks = [copies.start(g_ref.at[peer[1]], block(here, f), peer) for peer in peers]
     halves = [copies.start(w_ref.at[core], w_out.at[f, core], peer) for peer in peers]
-    rest += [copies.start(g_ref.at[peer[1]], g_out.at[f], peer) for peer in peers]
+    own[0].wait()
+    for copy in blocks:
+        copy.wait_recv()
+    mine = columns(here)
+    near = [copies.start(mine, mine, device) for device in along]
+    rest.append(copies.start(mine, mine, sibling))
     for half, peer in zip(halves, peers):
         half.wait_recv()
         place = w_out.at[peer[1], core]
         rest.append(copies.start(place, place, sibling))
-    for half in halves:
-        half.wait_send()
-    for copy in rest + own:
+    for copy, device in zip(near, along):
+        copy.wait_recv()
+        place = columns(device)
+        rest.append(copies.start(place, place, sibling))
+    for copy in halves + blocks + near:
+        copy.wait_send()
+    for copy in rest + own[1:]:
         copy.wait()
 
 
-def second_kernel(kv_ref, w_ref, kv_out, w_out, send, recv, local):
+def second_kernel(kv_ref, w_ref, t_ref, kv_out, w_out, t_out, send, recv, local):
     c, f = lax.axis_index("ctx"), lax.axis_index("fsdp")
     core = lax.rem(c, 2)
     sibling = (flip(c, 1), f)
@@ -139,12 +160,14 @@
     own = [
         pltpu.make_async_copy(kv_ref, kv_out.at[c], local.at[0]),
         pltpu.make_async_copy(w_ref, w_out.at[f], local.at[1]),
+        pltpu.make_async_copy(t_ref, t_out.at[0], local.at[2]),
     ]
     for copy in own:
         copy.start()
     keys = [copies.start(kv_ref, kv_out.at[c], device) for device in ring]
     rest = [copies.start(kv_ref, kv_out.at[c], sibling)]
     halves = [copies.start(w_ref.at[core], w_out.at[f, core], peer) for peer in peers]
+    rest += [copies.start(t_ref, t_out.at[i + 1], peer) for i, peer in enumerate(peers)]
     for key, device in zip(keys, ring):
         key.wait_recv()
         place = kv_out.at[device[0]]
@@ -417,6 +440,249 @@
     )(expo, query, keys_values, keys_values, grad, mixed, inverse)
 
 
+def apart(value, mask):
+    out = 0
+    for bit in (1, 2, 4):
+        out = out + bit * lax.rem(lax.div(value, bit) + lax.div(mask, bit), 2)
+    return out
+
+
+def mlp_kernel(
+    nm_ref,
+    cot_ref,
+    gu_ref,
+    down_ref,
+    grad_ref,
+    out_ref,
+    sum_gu_ref,
+    sum_dn_ref,
+    nm,
+    cot,
+    gu,
+    down,
+    act,
+    gate_low,
+    up_low,
+    part,
+    part_in,
+    outs,
+    gu_in,
+    dn_in,
+    nm_send,
+    nm_recv,
+    part_send,
+    part_recv,
+    swap_send,
+    swap_recv,
+    local,
+):
+    c, f = lax.axis_index("ctx"), lax.axis_index("fsdp")
+    core = lax.rem(c, 2)
+    sibling = (flip(c, 1), f)
+    tokens, width = nm_ref.shape
+    units = down_ref.shape[0]
+    rows = 2 * tokens
+    greet([(c, flip(f, i)) for i in range(1, N_FS)] + [sibling])
+
+    def normed_copy(i):
+        return pltpu.make_async_remote_copy(
+            src_ref=nm_ref,
+            dst_ref=nm.at[i],
+            send_sem=nm_send.at[i],
+            recv_sem=nm_recv.at[i],
+            device_id=(c, apart(f, i)),
+            device_id_type=MESH,
+        )
+
+    def part_copy(i):
+        return pltpu.make_async_remote_copy(
+            src_ref=part.at[i],
+            dst_ref=part_in.at[i],
+            send_sem=part_send.at[i],
+            recv_sem=part_recv.at[i],
+            device_id=(c, apart(f, i)),
+            device_id_type=MESH,
+        )
+
+    for i in range(1, N_FS):
+        normed_copy(i).start()
+    loads = [
+        pltpu.make_async_copy(nm_ref, nm.at[0], local.at[0]),
+        pltpu.make_async_copy(gu_ref, gu, local.at[1]),
+        pltpu.make_async_copy(cot_ref, cot, local.at[2]),
+        pltpu.make_async_copy(down_ref, down, local.at[3]),
+    ]
+    for load in loads:
+        load.start()
+    for load in loads:
+        load.wait()
+
+    def out_copy(s):
+        return pltpu.make_async_copy(
+            outs.at[lax.rem(s, 2)], out_ref.at[pl.ds(2 * s, 2)], local.at[4 + lax.rem(s, 2)]
+        )
+
+    def pair(s, carry):
+        @pl.when(s > 0)
+        def _():
+            normed_copy(2 * s).wait_recv()
+
+        normed_copy(2 * s + 1).wait_recv()
+        at = pl.multiple_of(s * rows, rows)
+        x = nm[pl.ds(2 * s, 2)].reshape(rows, width)
+        gate = jnp.dot(x, gu[0], preferred_element_type=F32)
+        up = jnp.dot(x, gu[1], preferred_element_type=F32)
+        grad = contract_cols(cot[pl.ds(2 * s, 2)].reshape(rows, width), down[...])
+        sigma = jax.nn.sigmoid(gate)
+        swish = gate * sigma
+        act[pl.ds(at, rows), :] = (swish * up).astype(BF)
+        gate_low[pl.ds(at, rows), :] = (
+            grad * up * sigma * (1.0 + gate * (1.0 - sigma))
+        ).astype(BF)
+        up_low[pl.ds(at, rows), :] = (grad * swish).astype(BF)
+        summed = contract_cols(gate_low[pl.ds(at, rows), :], gu[0])
+        summed = summed + contract_cols(up_low[pl.ds(at, rows), :], gu[1])
+        part[pl.ds(2 * s, 2)] = summed.astype(BF).reshape(2, tokens, width)
+
+        @pl.when(s > 0)
+        def _():
+            part_copy(2 * s).start()
+
+        part_copy(2 * s + 1).start()
+
+        @pl.when(s > 1)
+        def _():
+            out_copy(s - 2).wait()
+
+        result = jnp.dot(act[pl.ds(at, rows), :], down[...], preferred_element_type=F32)
+        outs[lax.rem(s, 2)] = result.astype(BF).reshape(2, tokens, width)
+        out_copy(s).start()
+        return carry
+
+    lax.fori_loop(0, N_FS // 2, pair, 0)
+
+    every = N_FS * tokens
+
+    def gate_up(m, carry):
+        at = pl.multiple_of(m * 256, 256)
+        x = nm[:, :, pl.ds(at, 256)].reshape(every, 256)
+        gu[0, pl.ds(at, 256), :] = contract_rows(x, gate_low[...]).astype(BF)
+        gu[1, pl.ds(at, 256), :] = contract_rows(x, up_low[...]).astype(BF)
+        return carry
+
+    lax.fori_loop(0, width // 256, gate_up, 0)
+    swap_gu = pltpu.make_async_remote_copy(
+        src_ref=gu.at[1 - core],
+        dst_ref=gu_in,
+        send_sem=swap_send.at[0],
+        recv_sem=swap_recv.at[0],
+        device_id=sibling,
+        device_id_type=MESH,
+    )
+    swap_gu.start()
+    turned = cot[...].reshape(every, width)
+
+    def down_rows(m, carry):
+        at = pl.multiple_of(m * 256, 256)
+        down[pl.ds(at, 256), :] = contract_rows(act[:, pl.ds(at, 256)], turned).astype(BF)
+        return carry
+
+    whole = units // 256
+    lax.fori_loop(0, whole, down_rows, 0)
+    if units % 256:
+        down[whole * 256 :, :] = contract_rows(act[:, whole * 256 :], turned).astype(BF)
+    half = units // 2
+    swap_dn = pltpu.make_async_remote_copy(
+        src_ref=down.at[pl.ds(pl.multiple_of((1 - core) * half, 16), half)],
+        dst_ref=dn_in,
+        send_sem=swap_send.at[1],
+        recv_sem=swap_recv.at[1],
+        device_id=sibling,
+        device_id_type=MESH,
+    )
+    swap_dn.start()
+    swap_gu.wait_recv()
+
+    def add_gu(m, carry):
+        at = pl.multiple_of(m * 256, 256)
+        gu_in[pl.ds(at, 256), :] = (
+            gu[core, pl.ds(at, 256), :].astype(F32) + gu_in[pl.ds(at, 256), :].astype(F32)
+        ).astype(BF)
+        return carry
+
+    lax.fori_loop(0, width // 256, add_gu, 0)
+    save_gu = pltpu.make_async_copy(gu_in, sum_gu_ref, local.at[6])
+    save_gu.start()
+    swap_dn.wait_recv()
+
+    def add_dn(m, carry):
+        at = pl.multiple_of(m * 112, 16)
+        own = down[pl.ds(pl.multiple_of(core * half + m * 112, 16), 112), :]
+        dn_in[pl.ds(at, 112), :] = (
+            own.astype(F32) + dn_in[pl.ds(at, 112), :].astype(F32)
+        ).astype(BF)
+        return carry
+
+    lax.fori_loop(0, half // 112, add_dn, 0)
+    save_dn = pltpu.make_async_copy(dn_in, sum_dn_ref, local.at[7])
+    save_dn.start()
+    total = part[0].astype(F32)
+    for i in range(1, N_FS):
+        part_copy(i).wait_recv()
+        total = total + part_in[i].astype(F32)
+    grad_ref[...] = total
+    for i in range(1, N_FS):
+        normed_copy(i).wait_send()
+        part_copy(i).wait_send()
+    swap_gu.wait_send()
+    swap_dn.wait_send()
+    for copy in (out_copy(2), out_copy(3), save_gu, save_dn):
+        copy.wait()
+
+
+def feed_forward(cid, normed, cot_all, columns, down_weight):
+    tokens, width = normed.shape
+    units = down_weight.shape[0]
+    every = N_FS * tokens
+    return pl.pallas_call(
+        mlp_kernel,
+        name="feed_forward",
+        out_shape=[
+            jax.ShapeDtypeStruct((tokens, width), F32),
+            jax.ShapeDtypeStruct((N_FS, tokens, width), BF),
+            jax.ShapeDtypeStruct((width, units), BF),
+            jax.ShapeDtypeStruct((units // 2, width), BF),
+        ],
+        in_specs=[pl.BlockSpec(memory_space=pl.ANY)] * 4,
+        out_specs=[pl.BlockSpec(memory_space=pltpu.VMEM)]
+        + [pl.BlockSpec(memory_space=pl.ANY)] * 3,
+        scratch_shapes=[
+            pltpu.VMEM((N_FS, tokens, width), BF),
+            pltpu.VMEM((N_FS, tokens, width), BF),
+            pltpu.VMEM((2, width, units), BF),
+            pltpu.VMEM((units, width), BF),
+            pltpu.VMEM((every, units), BF),
+            pltpu.VMEM((every, units), BF),
+            pltpu.VMEM((every, units), BF),
+            pltpu.VMEM((N_FS, tokens, width), BF),
+            pltpu.VMEM((N_FS, tokens, width), BF),
+            pltpu.VMEM((2, 2, tokens, width), BF),
+            pltpu.VMEM((width, units), BF),
+            pltpu.VMEM((units // 2, width), BF),
+            pltpu.SemaphoreType.DMA((N_FS,)),
+            pltpu.SemaphoreType.DMA((N_FS,)),
+            pltpu.SemaphoreType.DMA((N_FS,)),
+            pltpu.SemaphoreType.DMA((N_FS,)),
+            pltpu.SemaphoreType.DMA((2,)),
+            pltpu.SemaphoreType.DMA((2,)),
+            pltpu.SemaphoreType.DMA((8,)),
+        ],
+        compiler_params=pltpu.CompilerParams(
+            collective_id=cid, has_side_effects=True, vmem_limit_bytes=60 * 2**20
+        ),
+    )(normed, cot_all, columns, down_weight)
+
+
 def body(
     layer_input,
     segments,
@@ -452,8 +718,6 @@
     cotangent = out_cotangent[0].astype(F32) * keep
     cot_low = cotangent.astype(BF)
 
-    cot_all = jnp.concatenate([cot_low] + [swap_fs(cot_low, i) for i in range(1, N_FS)], axis=0)
-
     qkv = jnp.concatenate([q_weight, k_weight, v_weight], axis=1).reshape(2, rows // 2, -1)
     small = jnp.concatenate([attn_norm, mlp_norm, q_bias, k_bias, v_bias]).reshape(-1, 128)
     small = jnp.pad(small, ((0, 16 - small.shape[0]), (0, 0)))
@@ -464,7 +728,7 @@
     blocks = (
         jnp.where(x_part < 4, gate_cut, up_cut).reshape(cut, N_FS, units).transpose(1, 0, 2)
     )
-    full_qkv, small_all, blocks_here = exchange(
+    full_qkv, small_all, columns = exchange(
         first_kernel,
         "gather_qkv",
         1,
@@ -472,21 +736,12 @@
         [
             ((N_FS,) + qkv.shape, BF),
             ((N_FS,) + small.shape, BF),
-            (blocks.shape, BF),
-        ],
-        28,
+            ((2, N_FS, 4, cut, units), BF),
+        ],
+        35,
         3,
     )
-    along = [blocks_here] + [swap_ctx(blocks_here, 2 * i) for i in range(1, 4)]
-    along = jnp.stack(along)
-    other = swap_ctx(along, 1)
-    x_here = lax.div(x_part, 2)
-    both = jnp.where(core == 0, jnp.stack([along, other]), jnp.stack([other, along]))
-    order = jnp.bitwise_xor(jnp.arange(4), x_here)
-    both = jnp.take(both, order, axis=1)
-    both = both.transpose(1, 0, 2, 3, 4).reshape(2, 4, N_FS, cut, units)
-    both = both.transpose(0, 2, 1, 3, 4).reshape(2, width, units)
-    gate_cols, up_cols = both[0], both[1]
+    columns = columns.reshape(2, width, units)
 
     flat = small_all[:, :5].reshape(N_FS, -1)
     marks = [0, rows, 2 * rows, 2 * rows + q_width // N_FS]
@@ -517,14 +772,18 @@
         jnp.tile(segment.astype(BF)[None, :], (1, 2 * KV_HEADS)), (16, 2 * kv_width)
     )
     keys_values = jnp.concatenate([keys_values, segment_rows], axis=0)
-    kv_all, full_o = exchange(
+    kv_all, full_o, cot_all = exchange(
         second_kernel,
         "gather_kv_o",
         2,
-        (keys_values, o_weight.reshape(2, rows // 2, width)),
-        [((N_CTX,) + keys_values.shape, BF), ((N_FS, 2, rows // 2, width), BF)],
-        29,
-        2,
+        (keys_values, o_weight.reshape(2, rows // 2, width), cot_low),
+        [
+            ((N_CTX,) + keys_values.shape, BF),
+            ((N_FS, 2, rows // 2, width), BF),
+            ((N_FS, tokens, width), BF),
+        ],
+        36,
+        3,
     )
     full_o = full_o.reshape(q_width, width)
     within = jnp.arange(tokens, dtype=jnp.int32)
@@ -543,39 +802,14 @@
     norm_second = middle * scale_two
     normed_mid = (norm_second * gain_two).astype(BF)
 
-    nm_all = jnp.concatenate(
-        [normed_mid] + [swap_fs(normed_mid, i) for i in range(1, N_FS)], axis=0
-    )
-    act_grad = contract_cols(cot_all, down_weight)
-    gate_pre = jnp.dot(nm_all, gate_cols, preferred_element_type=F32)
-    up_pre = jnp.dot(nm_all, up_cols, preferred_element_type=F32)
-    sigma = jax.nn.sigmoid(gate_pre)
-    swish = gate_pre * sigma
-    activation = (swish * up_pre).astype(BF)
-    gate_grad = (act_grad * up_pre * sigma * (1.0 + gate_pre * (1.0 - sigma))).astype(BF)
-    up_grad = (act_grad * swish).astype(BF)
-    part_sum = (contract_cols(gate_grad, gate_cols) + contract_cols(up_grad, up_cols)).astype(BF)
-    part_sum = part_sum.reshape(N_FS, tokens, width)
-    mid_norm_grad = part_sum[0].astype(F32)
-    for i in range(1, N_FS):
-        mid_norm_grad = mid_norm_grad + swap_fs(part_sum[i], i).astype(F32)
-    out_part = jnp.dot(activation, down_weight, preferred_element_type=F32).astype(BF)
-    out_part = out_part.reshape(N_FS, tokens, width)
+    piece = rows // 8
+    mid_norm_grad, out_part, sum_gu, sum_down = feed_forward(
+        8, normed_mid, cot_all, columns, down_weight
+    )
     output_rows = middle + out_part[0].astype(F32)
     for i in range(1, N_FS):
         output_rows = output_rows + swap_fs(out_part[i], i).astype(F32)
     output_rows = output_rows.astype(BF)
-
-    piece = rows // 8
-    gate_part = contract_rows(nm_all, gate_grad).astype(BF)
-    up_part = contract_rows(nm_all, up_grad).astype(BF)
-    down_part = contract_rows(activation, cot_all).astype(BF).reshape(2, units // 2, width)
-    keep_gu = jnp.where(core == 0, gate_part, up_part)
-    send_gu = jnp.where(core == 0, up_part, gate_part)
-    keep_down = jnp.where(core == 0, down_part[0], down_part[1])
-    send_down = jnp.where(core == 0, down_part[1], down_part[0])
-    sum_gu = (keep_gu.astype(F32) + swap_ctx(send_gu, 1).astype(F32)).astype(BF)
-    sum_down = (keep_down.astype(F32) + swap_ctx(send_down, 1).astype(F32)).astype(BF)
     sum_gu = sum_gu.reshape(N_FS, 8, piece, units)
     sum_down = sum_down.reshape(8, units // 16, width)
     far_gu, far_down = scatter_ctx("scatter_mlp", 3, (sum_gu, sum_down))

time: 864 us -> 745 us (0.86)
  Pallas kernels: 407 us -> 527 us
  waiting for transfers between devices: 103 us -> 31.7 us
  matrix products: 74.9 us -> 19.1 us
  other arithmetic: 107 us -> 65.4 us
  starting transfers between devices: 47 us -> 8.96 us
  local copies, waits for them, and re-layouts: 109 us -> 81 us
    pallas_call x0 -> x1, Pallas kernels: none -> 85 us  [feed_forward(): pl.pallas_call(mlp_kernel, name='feed_forward', out_shape=[jax.ShapeDtype...]
    ppermute x28 -> x7, waiting for transfers between devices: 103 us -> 31.7 us  [swap_fs(): return lax.ppermute(value, 'fsdp', [(s, s ^ mask) for s in range(N_FS)])]
    pallas_call x7, Pallas kernels: 390 us -> 424 us  [exchange(): pl.pallas_call(kernel, name=name, out_shape=[jax.ShapeDtypeStruct(s, d) f...]
    ppermute x28 -> x7, starting transfers between devices: 32.2 us -> 6.77 us  [swap_fs(): return lax.ppermute(value, 'fsdp', [(s, s ^ mask) for s in range(N_FS)])]
    dot_general x5 -> x2, matrix products: 26.9 us -> 7.65 us  [contract_cols(): lax.dot_general(left, right, (((1,), (1,)), ((), ())), preferred_element_...]
    dot_general x5 -> x2, matrix products: 23.4 us -> 4.25 us  [contract_rows(): lax.dot_general(left, right, (((0,), (0,)), ((), ())), preferred_element_...]
    dot_general x3 -> x0, matrix products: 15.8 us -> none  [the longest x1 5.81 us: body(): up_pre = jnp.dot(nm_all, up_cols, preferred_element_type=F32)]
    select_n x4 -> x0, other arithmetic: 15.5 us -> none  [the longest x1 7.44 us: body(): jnp.where(core == 0, jnp.stack([along, other]), jnp.stack([other, along]))]
  transfers between devices with their start and end apart: 36 -> 9, of which waited for: 15 -> 5; matrix products, arithmetic and copies ran while one was open for 15% -> 4% of each run, Pallas kernels for 26% -> 10%
where the time goes in v2:
time: 745 us; the launch traced here: 735 us
  Pallas kernels  527 us (71%)
  local copies, waits for them, and re-layouts  81 us (11%)
  other arithmetic  65.4 us (9%)
  waiting for transfers between devices  31.7 us (4%)
  matrix products  19.1 us (3%)
  starting transfers between devices  8.96 us (1%)
    pallas_call x7, Pallas kernels, exchange(): pl.pallas_call(kernel, name=name, out_shape=[jax.ShapeDtypeStruct(s, d) f...  424 us
    pallas_call x1, Pallas kernels, feed_forward(): pl.pallas_call(mlp_kernel, name='feed_forward', out_shape=[jax.ShapeDtype...  85 us
    ppermute x7, waiting for transfers between devices, swap_fs(): return lax.ppermute(value, 'fsdp', [(s, s ^ mask) for s in range(N_FS)])  31.7 us
    convert_element_type x2, local copies, waits for them, and re-layouts, body(): all_gu[0].astype(F32)  15.2 us
  transfers between devices with their start and end apart: 9, of which 5 were waited for; matrix products, arithmetic and copies ran while one was open for 4% of the time, Pallas kernels for 10%

profile of v2, /device:TPU:35, one launch (start us, length us, event | category | flops | bytes accessed | tf_op | source)
XLA Modules:
  0.0 734.9 jit_solution(6409123242751718888)
XLA Ops:
  6.8 63.9 %gather_qkv.1 = (bf16[8,2,96,2048]{3,2,1,0:T(8,128)(2,1)}, bf16[8,16,128]{2,1,0:T(8,128)(2,1)}, bf16[2,8,4,48,1120]{4,3,2,1,0:T(8,128)(2,1)}) custom-call(bf16[2,96,2048]{2,1,0:T(8,128)(2,1)} %bitcast.210, bf16[16,128]{1,0:T(8,128)(2,1)} %pad.8.s_ref, bf16[8,48,1120]{2,1,0:T(8,128)(2,1)} %bitcast.208), custom_call_target="tpu_custom_call" | custom-call | tf_op jit(solution)/shard_map/gather_qkv/pallas_call | solution.py:89
  72.0 3.9 convolution_add_fusion.1
  79.8 80.6 %gather_kv_o.1 = (bf16[16,144,512]{2,1,0:T(8,128)(2,1)}, bf16[8,2,96,1536]{3,2,1,0:T(8,128)(2,1)}, bf16[8,128,1536]{2,1,0:T(8,128)(2,1)}) custom-call(bf16[144,512]{1,0:T(8,128)(2,1)} %pad_maximum_fusion.9.kv_ref, bf16[2,96,1536]{2,1,0:T(8,128)(2,1)} %bitcast.216, bf16[128,1536]{1,0:T(8,128)(2,1)} %fusion.28.t_ref), custom_call_target="tpu_custom_call" | custom-call | tf_op jit(solution)/shard_map/gather_kv_o/pallas_call | solution.py:89
  162.1 8.5 %attend.1 = (bf16[2,2048,768]{2,1,0:T(8,128)(2,1)}, f32[2,128,768]{2,1,0:T(8,128)S(1)}, f32[2,8,768]{2,1,0:T(8,128)S(1)}) custom-call(bf16[2,768,128]{2,1,0:T(8,128)(2,1)S(1)} %bitcast.183, bf16[16,144,512]{2,1,0:T(8,128)(2,1)S(1)} %copy-done, bf16[16,144,512]{2,1,0:T(8,128)(2,1)S(1)} %copy-done, f32[2,128]{1,0:T(2,128)S(1)} %pad_maximum_fusion.11.row_ref), custom_call_target="tpu_custom_call" | custom-call | flops 1610612736 | bytes 10485760 | tf_op jit(solution)/shard_map/attend/pallas_call | solution.py:349
  175.4 85.0 %feed_forward.1 = (f32[128,1536]{1,0:T(8,128)}, bf16[8,128,1536]{2,1,0:T(8,128)(2,1)}, bf16[1536,1120]{1,0:T(8,128)(2,1)}, bf16[560,1536]{1,0:T(8,128)(2,1)}) custom-call(bf16[128,1536]{1,0:T(8,128)(2,1)} %multiply_convert_fusion.nm_ref, bf16[8,128,1536]{2,1,0:T(8,128)(2,1)} %get-tuple-element.44.cot_ref, bf16[2,1536,1120]{2,1,0:T(8,128)(2,1)} %bitcast.199, ...), custom_call_target="tpu_custom_call" | custom-call | tf_op jit(solution)/shard_map/feed_forward/pallas_call | solution.py:647
  276.8 5.6 collective-permute-done.5
  282.4 9.8 %collective-permute-done.4 = bf16[128,1536]{1,0:T(8,128)(2,1)} collective-permute-done((bf16[128,1536]{1,0:T(8,128)(2,1)}, bf16[128,1536]{1,0:T(8,128)(2,1)}, u32[]{:S(2)}, u32[]{:S(2)}) %collective-permute-start.4) | collective-permute-done | bytes 393248 | tf_op jit(solution)/shard_map/ppermute | solution.py:291
  292.2 10.4 %collective-permute-done.3 = bf16[128,1536]{1,0:T(8,128)(2,1)} collective-permute-done((bf16[128,1536]{1,0:T(8,128)(2,1)}, bf16[128,1536]{1,0:T(8,128)(2,1)}, u32[]{:S(2)}, u32[]{:S(2)}) %collective-permute-start.3) | collective-permute-done | bytes 393248 | tf_op jit(solution)/shard_map/ppermute | solution.py:291
  306.6 4.0 convolution_convert_fusion.2
  311.0 9.4 %attend_back.1 = (f32[2,128,768]{2,1,0:T(8,128)S(1)}, bf16[16,128,256]{2,1,0:T(8,128)(2,1)S(1)}, bf16[16,128,256]{2,1,0:T(8,128)(2,1)S(1)}) custom-call(bf16[2,2048,768]{2,1,0:T(8,128)(2,1)} %get-tuple-element.48.e_ref, bf16[2,768,128]{2,1,0:T(8,128)(2,1)S(1)} %bitcast.184, bf16[16,144,512]{2,1,0:T(8,128)(2,1)} %get-tuple-element.41.k_ref.v_ref, ...), custom_call_target="tpu_custom_call" | custom-call | flops 3221225472 | bytes 12582912 | tf_op jit(solution)/shard_map/attend_back/pallas_call | solution.py:411
  330.3 19.4 %scatter_kv.1 = bf16[7,128,512]{2,1,0:T(8,128)(2,1)} custom-call(bf16[8,128,512]{2,1,0:T(8,128)(2,1)} %fusion.refs_0_), custom_call_target="tpu_custom_call" | custom-call | tf_op jit(solution)/shard_map/scatter_kv/pallas_call | solution.py:89
  372.4 76.3 %scatter_mlp.1 = (bf16[7,8,24,1120]{3,2,1,0:T(8,128)(2,1)}, bf16[7,70,1536]{2,1,0:T(8,128)(2,1)}) custom-call(bf16[8,8,24,1120]{3,2,1,0:T(8,128)(2,1)} %bitcast.205, bf16[8,70,1536]{2,1,0:T(8,128)(2,1)} %reshape.403.refs_1_), custom_call_target="tpu_custom_call" | custom-call | tf_op jit(solution)/shard_map/scatter_mlp/pallas_call | solution.py:89
  471.9 8.9 %add_convert_fusion = bf16[1536,1792]{0,1:T(8,128)(2,1)} fusion(bf16[1536,1792]{0,1:T(8,128)(2,1)} %collective-permute-done.8, pred[]{:T(512)S(6)} %eq.2, bf16[1536,256]{0,1:T(8,128)(2,1)} %copy-done.14, bf16[1536,768]{0,1:T(8,128)(2,1)} %copy-done.6, bf16[1536,768]{0,1:T(8,128)(2,1)} %get-tuple-element.75, bf16[1536,256]{0,1:T(8,128)(2,1)} %copy-done.13, ...), kind=kLoop, calls=%fused_computation | loop fusion | flops 46792704 | bytes 22020096 | tf_op jit(solution)/shard_map/convert_element_type | solution.py:881
  480.8 8.3 %copy.55 = bf16[1536,1792]{1,0:T(8,128)(2,1)} copy(bf16[1536,1792]{0,1:T(8,128)(2,1)} %add_convert_fusion) | data formatting | bytes 11010048 | tf_op jit(solution)/shard_map/convert_element_type | solution.py:881
  489.1 78.4 %scatter_attn.1 = bf16[7,8,24,1792]{3,2,1,0:T(8,128)(2,1)} custom-call(bf16[8,8,24,1792]{3,2,1,0:T(8,128)(2,1)} %bitcast.190), custom_call_target="tpu_custom_call" | custom-call | tf_op jit(solution)/shard_map/scatter_attn/pallas_call | solution.py:89
  572.7 16.8 %to_owner.1 = (bf16[8,24,1120]{2,1,0:T(8,128)(2,1)}, bf16[8,24,1792]{2,1,0:T(8,128)(2,1)}, f32[8,8,128]{2,1,0:T(8,128)}) custom-call(bf16[8,24,1120]{2,1,0:T(8,128)(2,1)} %fusion.8.refs_0_, bf16[8,24,1792]{2,1,0:T(8,128)(2,1)} %fusion.1.refs_1_, f32[8,8,128]{2,1,0:T(8,128)} %pad.9.refs_2_), custom_call_target="tpu_custom_call" | custom-call | tf_op jit(solution)/shard_map/to_owner/pallas_call | solution.py:89
  592.8 89.1 %gather_grads.1 = (bf16[16,8,24,1120]{3,2,1,0:T(8,128)(2,1)}, bf16[16,24,1792]{2,1,0:T(8,128)(2,1)}, bf16[16,70,1536]{2,1,0:T(8,128)(2,1)}, f32[16,8,128]{2,1,0:T(8,128)}) custom-call(bf16[8,24,1120]{2,1,0:T(8,128)(2,1)} %get-tuple-element.56.refs_0_, bf16[24,1792]{1,0:T(8,128)(2,1)} %reduce_sum.139.refs_1_, bf16[70,1536]{1,0:T(8,128)(2,1)} %fusion.30.refs_2_, ...), custom_call_target="tpu_custom_call" | custom-call | tf_op jit(solution)/shard_map/gather_grads/pallas_call | solution.py:89
  687.3 3.9 copy_bitcast_fusion
  691.2 6.4 reshape.430
  697.6 7.5 %slice_convert_fusion = (f32[1,8,24,8,1120]{4,2,3,0,1:T(8,128)S(1)}, f32[1,8,24,8,1120]{4,2,3,0,1:T(8,128)}) fusion(bf16[2,8,24,8,1120]{4,2,3,0,1:T(8,128)(2,1)} %bitcast.200), kind=kLoop, calls=%fused_computation.9 | loop fusion | flops 3440640 | bytes 20643840 | tf_op jit(solution)/shard_map/convert_element_type | solution.py:932
  705.1 4.1 copy.60
  709.2 7.9 %reshape.429 = f32[192,8960]{1,0:T(8,128)} reshape(f32[1,8,24,8,1120]{4,3,2,1,0:T(8,128)} %copy.60) | data formatting | bytes 13762560 | tf_op jit(solution)/shard_map/convert_element_type | solution.py:932
  717.2 7.1 copy.59
  724.3 8.0 %reshape.428 = f32[192,8960]{1,0:T(8,128)} reshape(f32[1,8,24,8,1120]{4,3,2,1,0:T(8,128)} %copy.59) | data formatting | bytes 13762560 | tf_op jit(solution)/shard_map/convert_element_type | solution.py:931
  (196 shorter events, 110.3 us)
Async XLA Ops:
  0.8 70.7 %copy-start.7 = (bf16[1,128,1536]{2,1,0:T(8,128)(2,1)S(1)}, bf16[1,128,1536]{2,1,0:T(8,128)(2,1)}, u32[]{:S(2)}) copy-start(bf16[1,128,1536]{2,1,0:T(8,128)(2,1)} %param.16) | copy-start | bytes 1179652
  171.1 89.3 %copy-start.15 = (bf16[128,2,6,128]{0,3,2,1:T(8,128)(2,1)}, bf16[128,2,6,128]{0,3,2,1:T(8,128)(2,1)S(1)}, u32[]{:S(2)}) copy-start(bf16[128,2,6,128]{0,3,2,1:T(8,128)(2,1)S(1)} %copy.44) | copy-start | bytes 1179652
  260.4 42.2 %copy-start.20 = (bf16[1,128,1536]{2,1,0:T(8,128)(2,1)S(1)}, bf16[1,128,1536]{2,1,0:T(8,128)(2,1)}, u32[]{:S(2)}) copy-start(bf16[1,128,1536]{2,1,0:T(8,128)(2,1)} %param.31) | copy-start | bytes 1179652
  260.4 16.1 %copy-start.18 = (f32[128,1536]{1,0:T(8,128)S(1)}, f32[128,1536]{1,0:T(8,128)}, u32[]{:S(2)}) copy-start(f32[128,1536]{1,0:T(8,128)} %get-tuple-element.47) | copy-start | bytes 2359300
  263.8 9.1 %collective-permute-start = (bf16[128,1536]{1,0:T(8,128)(2,1)}, bf16[128,1536]{1,0:T(8,128)(2,1)}, u32[]{:S(2)}, u32[]{:S(2)}) collective-permute-start(bf16[128,1536]{1,0:T(8,128)(2,1)} %get-tuple-element.76), channel_id=1, source_target_pairs={{0,1},{1,0},{2,3},{3,2},{4,5},{5,4},{6,7},{7,6},{8,9},{9,8},{10,11... | collective-permute-start | bytes 1179656 | tf_op jit(solution)/shard_map/ppermute | solution.py:291
  263.8 12.3 %collective-permute-start.6 = (bf16[128,1536]{1,0:T(8,128)(2,1)}, bf16[128,1536]{1,0:T(8,128)(2,1)}, u32[]{:S(2)}, u32[]{:S(2)}) collective-permute-start(bf16[128,1536]{1,0:T(8,128)(2,1)} %get-tuple-element.77), channel_id=1, source_target_pairs={{0,7},{1,6},{2,5},{3,4},{4,3},{5,2},{6,1},{7,0},{8,15},{9,14},{10,... | collective-permute-start | bytes 1179656 | tf_op jit(solution)/shard_map/ppermute | solution.py:291
  265.1 17.3 %collective-permute-start.5 = (bf16[128,1536]{1,0:T(8,128)(2,1)}, bf16[128,1536]{1,0:T(8,128)(2,1)}, u32[]{:S(2)}, u32[]{:S(2)}) collective-permute-start(bf16[128,1536]{1,0:T(8,128)(2,1)} %get-tuple-element.78), channel_id=1, source_target_pairs={{0,6},{1,7},{2,4},{3,5},{4,2},{5,3},{6,0},{7,1},{8,14},{9,15},{10,... | collective-permute-start | bytes 1179656 | tf_op jit(solution)/shard_map/ppermute | solution.py:291
  268.0 24.2 %collective-permute-start.4 = (bf16[128,1536]{1,0:T(8,128)(2,1)}, bf16[128,1536]{1,0:T(8,128)(2,1)}, u32[]{:S(2)}, u32[]{:S(2)}) collective-permute-start(bf16[128,1536]{1,0:T(8,128)(2,1)} %get-tuple-element.79), channel_id=1, source_target_pairs={{0,5},{1,4},{2,7},{3,6},{4,1},{5,0},{6,3},{7,2},{8,13},{9,12},{10,... | collective-permute-start | bytes 1179656 | tf_op jit(solution)/shard_map/ppermute | solution.py:291
  268.4 34.2 %collective-permute-start.3 = (bf16[128,1536]{1,0:T(8,128)(2,1)}, bf16[128,1536]{1,0:T(8,128)(2,1)}, u32[]{:S(2)}, u32[]{:S(2)}) collective-permute-start(bf16[128,1536]{1,0:T(8,128)(2,1)} %get-tuple-element.80), channel_id=1, source_target_pairs={{0,4},{1,5},{2,6},{3,7},{4,0},{5,1},{6,2},{7,3},{8,12},{9,13},{10,... | collective-permute-start | bytes 1179656 | tf_op jit(solution)/shard_map/ppermute | solution.py:291
  272.9 29.7 %collective-permute-start.2 = (bf16[128,1536]{1,0:T(8,128)(2,1)}, bf16[128,1536]{1,0:T(8,128)(2,1)S(1)}, u32[]{:S(2)}, u32[]{:S(2)}) collective-permute-start(bf16[128,1536]{1,0:T(8,128)(2,1)} %get-tuple-element.81), channel_id=1, source_target_pairs={{0,3},{1,2},{2,1},{3,0},{4,7},{5,6},{6,5},{7,4},{8,11},{9,10},{10,... | collective-permute-start | bytes 1179656 | tf_op jit(solution)/shard_map/ppermute | solution.py:291
  276.1 26.4 %collective-permute-start.1 = (bf16[128,1536]{1,0:T(8,128)(2,1)}, bf16[128,1536]{1,0:T(8,128)(2,1)S(1)}, u32[]{:S(2)}, u32[]{:S(2)}) collective-permute-start(bf16[128,1536]{1,0:T(8,128)(2,1)} %get-tuple-element.82), channel_id=1, source_target_pairs={{0,2},{1,3},{2,0},{3,1},{4,6},{5,7},{6,4},{7,5},{8,10},{9,11},{10,... | collective-permute-start | bytes 1179656 | tf_op jit(solution)/shard_map/ppermute | solution.py:291
  324.3 4.3 collective-permute-start.7
  328.6 32.8 %copy-start.2 = (bf16[1536,768]{0,1:T(8,128)(2,1)}, bf16[1536,768]{0,1:T(8,128)(2,1)S(1)}, u32[]{:S(2)}) copy-start(bf16[1536,768]{0,1:T(8,128)(2,1)S(1)} %get-tuple-element.74) | copy-start | bytes 7077892
  328.6 29.5 %copy-start.8 = (bf16[1,128,1536]{2,1,0:T(8,128)(2,1)S(1)}, bf16[1,128,1536]{2,1,0:T(8,128)(2,1)}, u32[]{:S(2)}) copy-start(bf16[1,128,1536]{2,1,0:T(8,128)(2,1)} %param.16) | copy-start | bytes 1179652
  368.0 103.9 %collective-permute-start.8 = (bf16[1536,1792]{0,1:T(8,128)(2,1)}, bf16[1536,1792]{0,1:T(8,128)(2,1)}, u32[]{:S(2)}, u32[]{:S(2)}) collective-permute-start(bf16[1536,1792]{0,1:T(8,128)(2,1)} %broadcast_select_fusion), channel_id=1, source_target_pairs={{0,8},{8,0},{16,24},{24,16},{32,40},{40,32},{48,56},{56,48},{64,72... | collective-permute-start | bytes 16515080 | tf_op jit(solution)/shard_map/ppermute | solution.py:295
  372.4 84.1 %slice-start = ((s8[6291456]{0:T(1024)(128)(4,1)}), s8[2097152]{0:T(1024)(128)(4,1)S(1)}, s32[]{:S(2)}) async-start(s8[6291456]{0:T(1024)(128)(4,1)} %bitcast.187), calls=%async_computation | async-start | bytes 4194304
  448.7 7.9 %copy-start.12 = (bf16[128,14,128]{0,2,1:T(8,128)(2,1)S(1)}, bf16[128,14,128]{0,2,1:T(8,128)(2,1)}, u32[]{:S(2)}) copy-start(bf16[128,14,128]{0,2,1:T(8,128)(2,1)} %copy-done.11) | copy-start | bytes 1376260
  448.7 7.8 %copy-start.25 = (bf16[128,256]{0,1:T(8,128)(2,1)S(1)}, bf16[128,256]{0,1:T(8,128)(2,1)}, u32[]{:S(2)}) copy-start(bf16[128,256]{0,1:T(8,128)(2,1)} %copy.52) | copy-start | bytes 196612
  448.7 7.8 %copy-start.31 = (f32[128]{0:T(128)S(1)}, f32[128]{0:T(128)}, u32[]{:S(2)}) copy-start(f32[128]{0:T(128)} %copy-done.30) | copy-start | bytes 1540
  460.2 11.7 %copy-start.3 = (bf16[1536,768]{0,1:T(8,128)(2,1)S(1)}, bf16[1536,768]{0,1:T(8,128)(2,1)}, u32[]{:S(2)}) copy-start(bf16[1536,768]{0,1:T(8,128)(2,1)} %copy-done.2) | copy-start | bytes 7077892
  724.3 8.1 %copy-start.23 = (bf16[192,768]{1,0:T(8,128)(2,1)S(1)}, bf16[192,768]{1,0:T(8,128)(2,1)}, u32[]{:S(2)}) copy-start(bf16[192,768]{1,0:T(8,128)(2,1)} %get-tuple-element.83) | copy-start | bytes 884740
  724.3 8.1 %copy-start.24 = (bf16[192,768]{1,0:T(8,128)(2,1)S(1)}, bf16[192,768]{1,0:T(8,128)(2,1)}, u32[]{:S(2)}) copy-start(bf16[192,768]{1,0:T(8,128)(2,1)} %get-tuple-element.84) | copy-start | bytes 884740
  724.3 9.2 %copy-start.21 = (bf16[192,768]{1,0:T(8,128)(2,1)S(1)}, bf16[192,768]{1,0:T(8,128)(2,1)}, u32[]{:S(2)}) copy-start(bf16[192,768]{1,0:T(8,128)(2,1)} %get-tuple-element.85) | copy-start | bytes 884740
  724.3 9.2 %copy-start.22 = (bf16[192,768]{1,0:T(8,128)(2,1)S(1)}, bf16[192,768]{1,0:T(8,128)(2,1)}, u32[]{:S(2)}) copy-start(bf16[192,768]{1,0:T(8,128)(2,1)} %get-tuple-element.86) | copy-start | bytes 884740
  (26 other events, 96.4 us)

commit v3 on v2

--- a/solution.py
+++ b/solution.py
@@ -180,119 +180,6 @@
         copy.wait_send()
     for copy in rest + own:
         copy.wait()
-
-
-def scatter_kernel(count, *refs):
-    ins, outs = refs[:count], refs[count : 2 * count]
-    send, recv, local = refs[2 * count :]
-    c, f = lax.axis_index("ctx"), lax.axis_index("fsdp")
-    ring = [(flip(c, 2 * i), f) for i in range(1, N_CTX // 2)]
-    greet(ring)
-    copies = Copies(send, recv)
-    for i, device in enumerate(ring):
-        for src, dst in zip(ins, outs):
-            piece = lax.div(device[0], 2)
-            if len(src.shape) == 4:
-                copies.start(src.at[:, piece], dst.at[i], device)
-            else:
-                copies.start(src.at[piece], dst.at[i], device)
-    for copy in copies.all:
-        copy.wait()
-
-
-def owner_kernel(count, *refs):
-    ins, outs = refs[:count], refs[count : 2 * count]
-    send, recv, local = refs[2 * count :]
-    c, f = lax.axis_index("ctx"), lax.axis_index("fsdp")
-    peers = [(c, flip(f, i)) for i in range(1, N_FS)]
-    greet(peers)
-    copies = Copies(send, recv)
-    own = [
-        pltpu.make_async_copy(src.at[f], dst.at[f], local.at[n])
-        for n, (src, dst) in enumerate(zip(ins, outs))
-    ]
-    for copy in own:
-        copy.start()
-    for peer in peers:
-        for src, dst in zip(ins, outs):
-            copies.start(src.at[peer[1]], dst.at[f], peer)
-    for copy in copies.all + own:
-        copy.wait()
-
-
-def gather_kernel(count, *refs):
-    ins, outs = refs[:count], refs[count : 2 * count]
-    send, recv, local = refs[2 * count :]
-    c, f = lax.axis_index("ctx"), lax.axis_index("fsdp")
-    sibling = (flip(c, 1), f)
-    ring = [(flip(c, 2 * i), f) for i in range(1, N_CTX // 2)]
-    greet(ring + [sibling])
-    copies = Copies(send, recv)
-    own = [
-        pltpu.make_async_copy(src, dst.at[c], local.at[n])
-        for n, (src, dst) in enumerate(zip(ins, outs))
-    ]
-    for copy in own:
-        copy.start()
-    near = [
-        [copies.start(src, dst.at[c], device) for src, dst in zip(ins, outs)] for device in ring
-    ]
-    rest = [copies.start(src, dst.at[c], sibling) for src, dst in zip(ins, outs)]
-    for group, device in zip(near, ring):
-        for copy, dst in zip(group, outs):
-            copy.wait_recv()
-            place = dst.at[device[0]]
-            rest.append(copies.start(place, place, sibling))
-    for group in near:
-        for copy in group:
-            copy.wait_send()
-    for copy in rest + own:
-        copy.wait()
-
-
-def gather_ctx(name, cid, arrays):
-    count = len(arrays)
-    return exchange(
-        functools.partial(gather_kernel, count),
-        name,
-        cid,
-        arrays,
-        [((N_CTX,) + a.shape, a.dtype) for a in arrays],
-        15 * count,
-        count,
-    )
-
-
-def scatter_ctx(name, cid, arrays):
-    count = len(arrays)
-    outs = [
-        ((7, a.shape[0]) + a.shape[2:] if a.ndim == 4 else (7,) + a.shape[1:], a.dtype)
-        for a in arrays
-    ]
-    return exchange(
-        functools.partial(scatter_kernel, count), name, cid, arrays, outs, 7 * count, 1
-    )
-
-
-def to_owner(name, cid, arrays):
-    count = len(arrays)
-    return exchange(
-        functools.partial(owner_kernel, count),
-        name,
-        cid,
-        arrays,
-        [(a.shape, a.dtype) for a in arrays],
-        7 * count,
-        count,
-    )
-
-
-def swap_fs(value, mask):
-    return lax.ppermute(value, "fsdp", [(s, s ^ mask) for s in range(N_FS)])
-
-
-def swap_ctx(value, mask):
-    return lax.ppermute(value, "ctx", [(s, s ^ mask) for s in range(N_CTX)])
 
 
 CHUNK = 256
@@ -376,70 +263,6 @@
     )(query, keys_values, keys_values, rows)
 
 
-def attend_back_kernel(
-    e_ref, q_ref, k_ref, v_ref, g_ref, o_ref, inv_ref, dq_ref, dk_ref, dv_ref
-):
-    tokens = k_ref.shape[1] - 16
-    length = N_CTX * tokens
-    scale = HD ** (-0.5)
-    query, grad = q_ref[0], g_ref[0]
-    inverse = inv_ref[0, 0:1, :]
-    grad_turned = grad.astype(F32).T
-    weighted = jnp.sum(grad_turned * o_ref[0], axis=0, keepdims=True)
-    factor = inverse * scale
-    shift = weighted * factor
-    grad_scaled = (grad_turned * inverse).T.astype(BF)
-    turned = jnp.zeros((HD, GROUP * tokens), F32)
-    for j in range(length // CHUNK):
-        part = e_ref[0, j * CHUNK : (j + 1) * CHUNK, :]
-        keys = k_ref[2 * j : 2 * j + 2, :tokens, :].reshape(CHUNK, HD)
-        values = v_ref[2 * j : 2 * j + 2, :tokens, :].reshape(CHUNK, HD)
-        prob_grad = contract_cols(values, grad)
-        score_grad = (part.astype(F32) * (prob_grad * factor - shift)).astype(BF)
-        dk = jnp.dot(score_grad, query, preferred_element_type=F32)
-        dv = jnp.dot(part, grad_scaled, preferred_element_type=F32)
-        dk_ref[2 * j : 2 * j + 2] = dk.reshape(2, tokens, HD).astype(dk_ref.dtype)
-        dv_ref[2 * j : 2 * j + 2] = dv.reshape(2, tokens, HD).astype(dv_ref.dtype)
-        turned = turned + contract_rows(keys, score_grad)
-    dq_ref[0] = turned
-
-
-def attend_back(expo, query, keys_values, grad, mixed, inverse):
-    wide = query.shape[1]
-    tokens = wide // GROUP
-    length = N_CTX * tokens
-    return pl.pallas_call(
-        attend_back_kernel,
-        name="attend_back",
-        grid=(KV_HEADS,),
-        in_specs=[
-            pl.BlockSpec((1, length, wide), lambda h: (h, 0, 0)),
-            pl.BlockSpec((1, wide, HD), lambda h: (h, 0, 0)),
-            pl.BlockSpec((N_CTX, tokens + 16, HD), lambda h: (0, 0, h)),
-            pl.BlockSpec((N_CTX, tokens + 16, HD), lambda h: (0, 0, KV_HEADS + h)),
-            pl.BlockSpec((1, wide, HD), lambda h: (h, 0, 0)),
-            pl.BlockSpec((1, HD, wide), lambda h: (h, 0, 0)),
-            pl.BlockSpec((1, 8, wide), lambda h: (h, 0, 0)),
-        ],
-        out_specs=[
-            pl.BlockSpec((1, HD, wide), lambda h: (h, 0, 0)),
-            pl.BlockSpec((N_CTX, tokens, HD), lambda h: (0, 0, h)),
-            pl.BlockSpec((N_CTX, tokens, HD), lambda h: (0, 0, h)),
-        ],
-        out_shape=[
-            jax.ShapeDtypeStruct((KV_HEADS, HD, wide), F32),
-            jax.ShapeDtypeStruct((N_CTX, tokens, KV_HEADS * HD), BF),
-            jax.ShapeDtypeStruct((N_CTX, tokens, KV_HEADS * HD), BF),
-        ],
-        compiler_params=pltpu.CompilerParams(vmem_limit_bytes=48 * 2**20),
-        cost_estimate=pl.CostEstimate(
-            flops=8 * KV_HEADS * length * wide * HD,
-            bytes_accessed=2 * KV_HEADS * length * wide + 6 * 2**20,
-            transcendentals=0,
-        ),
-    )(expo, query, keys_values, keys_values, grad, mixed, inverse)
-
-
 def apart(value, mask):
     out = 0
     for bit in (1, 2, 4):
@@ -683,6 +506,666 @@
     )(normed, cot_all, columns, down_weight)
 
 
+def turn_back(grad, cos_wide, sin_wide):
+    half = grad.shape[1] // 2
+    swapped = jnp.concatenate([grad[:, half:], grad[:, :half]], axis=1)
+    return grad * cos_wide + swapped * sin_wide
+
+
+def attention_back_kernel(
+    sum_gu,
+    sum_dn,
+    expo_hbm,
+    kv_hbm,
+    o_hbm,
+    mng_ref,
+    middle_ref,
+    cot_ref,
+    gain_ref,
+    query_ref,
+    mixed_ref,
+    inv_ref,
+    attended_ref,
+    normed_ref,
+    cos_ref,
+    sin_ref,
+    done_gu,
+    done_dn,
+    own_kv,
+    o_red,
+    q_red,
+    q_grad,
+    mid_ref,
+    gain_grad,
+    expo,
+    kv,
+    full_o,
+    branch,
+    back,
+    gu_mine,
+    gu_z,
+    gu_x,
+    dn_mine,
+    dn_x,
+    dn_z,
+    dkv,
+    kv_in,
+    kv_far,
+    out_half,
+    keep_half,
+    o_in,
+    q_in,
+    o_far,
+    q_far,
+    send,
+    recv,
+    local,
+):
+    c, f = lax.axis_index("ctx"), lax.axis_index("fsdp")
+    core, pair = lax.rem(c, 2), lax.div(c, 2)
+    x_at, z_at = lax.rem(pair, 4), lax.div(pair, 4)
+    sibling = (flip(c, 1), f)
+    partner = (flip(c, 8), f)
+    along = [(flip(c, 2 * i), f) for i in range(1, 4)]
+    ring = [(flip(c, 2 * i), f) for i in range(1, N_CTX // 2)]
+    peers = [(c, flip(f, i)) for i in range(1, N_FS)]
+    greet(ring + peers + [sibling])
+    copies = Copies(send, recv)
+    tokens, width = mng_ref.shape
+    strip = dn_mine.shape[1]
+    window = dn_z.shape[0]
+    shift = dn_mine.shape[0] - window
+    side = width // 2
+    scale = HD ** (-0.5)
+
+    def x_of(device):
+        return lax.rem(lax.div(device[0], 2), 4)
+
+    def strip_of(ref, x):
+        return ref.at[:, pl.ds(pl.multiple_of(x * strip, strip), strip)]
+
+    def local_copy(src, dst, n):
+        copy = pltpu.make_async_copy(src, dst, local.at[n])
+        copy.start()
+        return copy
+
+    z_gu = copies.start(sum_gu.at[:, pl.ds(4 * (1 - z_at), 4)], gu_z, partner)
+    x_dn = [
+        copies.start(strip_of(sum_dn, x_of(device)), dn_x.at[i], device)
+        for i, device in enumerate(along)
+    ]
+    loads_o = local_copy(o_hbm, full_o, 0)
+    loads = [
+        local_copy(kv_hbm, kv, 1),
+        local_copy(expo_hbm, expo, 2),
+    ]
+    loads_own = [
+        local_copy(sum_gu.at[:, pl.ds(4 * z_at, 4)], gu_mine, 3),
+        local_copy(strip_of(sum_dn, x_at), dn_mine, 4),
+    ]
+
+    middle = middle_ref[...]
+    scale_two = lax.rsqrt(jnp.mean(middle * middle, axis=-1, keepdims=True) + EPSILON)
+    norm = middle * scale_two
+    grad = mng_ref[...]
+    gain_grad[...] = jnp.sum(grad * norm, axis=0, keepdims=True)
+    scaled = grad * gain_ref[...]
+    mid = cot_ref[...].astype(F32) + scale_two * (
+        scaled - norm * jnp.mean(scaled * norm, axis=-1, keepdims=True)
+    )
+    mid_ref[...] = mid
+    branch[...] = mid.astype(BF)
+    loads_o.wait()
+    back[...] = contract_cols(branch[...], full_o[...]).astype(BF)
+
+    def columns_of(which):
+        return pl.ds(pl.multiple_of(which * side, side), side)
+
+    out_half[...] = contract_rows(attended_ref[...], branch[:, columns_of(1 - core)]).astype(BF)
+    swap_o = copies.start(out_half, o_in, sibling)
+    keep_half[...] = contract_rows(attended_ref[...], branch[:, columns_of(core)]).astype(BF)
+    for load in loads:
+        load.wait()
+
+    length = N_CTX * tokens
+    for h in range(KV_HEADS):
+        query = query_ref[h]
+        heads = back[:, h * GROUP * HD : (h + 1) * GROUP * HD]
+        rows = jnp.concatenate([heads[:, i * HD : (i + 1) * HD] for i in range(GROUP)], axis=0)
+        inverse = inv_ref[h, 0:1, :]
+        turned = rows.astype(F32).T
+        weighted = jnp.sum(turned * mixed_ref[h], axis=0, keepdims=True)
+        factor = inverse * scale
+        offset = weighted * factor
+        rows_scaled = (turned * inverse).T.astype(BF)
+        dq = jnp.zeros((HD, GROUP * tokens), F32)
+        for j in range(length // CHUNK):
+            part = expo[h, j * CHUNK : (j + 1) * CHUNK, :]
+            keys = kv[2 * j : 2 * j + 2, :tokens, h * HD : (h + 1) * HD].reshape(CHUNK, HD)
+            values = kv[
+                2 * j : 2 * j + 2, :tokens, (KV_HEADS + h) * HD : (KV_HEADS + h + 1) * HD
+            ].reshape(CHUNK, HD)
+            prob_grad = contract_cols(values, rows)
+            score_grad = (part.astype(F32) * (prob_grad * factor - offset)).astype(BF)
+            dk = jnp.dot(score_grad, query, preferred_element_type=F32).astype(BF)
+            dv = jnp.dot(part, rows_scaled, preferred_element_type=F32).astype(BF)
+            for side_core in range(2):
+                cut = slice(side_core * tokens, (side_core + 1) * tokens)
+                dkv[side_core, j, :, h * HD : (h + 1) * HD] = dk[cut]
+                dkv[side_core, j, :, (KV_HEADS + h) * HD : (KV_HEADS + h + 1) * HD] = dv[cut]
+            dq = dq + contract_rows(keys, score_grad)
+        for i in range(GROUP):
+            at = (h * GROUP + i) * HD
+            q_grad[:, at : at + HD] = turn_back(
+                dq[:, i * tokens : (i + 1) * tokens].T, cos_ref[...], sin_ref[...]
+            ).astype(BF)
+    swap_kv = copies.start(dkv.at[1 - core], kv_in, sibling)
+
+    def add_half(ref):
+        def step(m, carry):
+            at = pl.multiple_of(m * 192, 192)
+            ref[pl.ds(at, 192), :] = (
+                ref[pl.ds(at, 192), :].astype(F32) + keep_half[pl.ds(at, 192), :].astype(F32)
+            ).astype(BF)
+            return carry
+
+        lax.fori_loop(0, width // 192, step, 0)
+
+    def owner_rows(ref, owner):
+        return ref.at[pl.ds(pl.multiple_of(owner * 192, 192), 192)]
+
+    swap_o.wait_recv()
+    add_half(o_in)
+    o_sends = [
+        copies.start(owner_rows(o_in, peer[1]), o_far.at[i], peer) for i, peer in enumerate(peers)
+    ]
+
+    swap_kv.wait_recv()
+    kv_in[...] = (dkv[core].astype(F32) + kv_in[...].astype(F32)).astype(BF)
+    kv_sends = [
+        copies.start(kv_in.at[lax.div(device[0], 2)], kv_far.at[i], device)
+        for i, device in enumerate(ring)
+    ]
+
+    swap_o.wait_send()
+    out_half[...] = contract_rows(normed_ref[...], q_grad[:, columns_of(1 - core)]).astype(BF)
+    swap_q = copies.start(out_half, q_in, sibling)
+    keep_half[...] = contract_rows(normed_ref[...], q_grad[:, columns_of(core)]).astype(BF)
+    for load in loads_own:
+        load.wait()
+    for copy in x_dn:
+        copy.wait_recv()
+    dn_mine[...] = (
+        dn_mine[...].astype(F32)
+        + dn_x[0].astype(F32)
+        + dn_x[1].astype(F32)
+        + dn_x[2].astype(F32)
+    ).astype(BF)
+
+    def window_of(z):
+        return pl.ds(pl.multiple_of(z * shift, 16), window)
+
+    z_dn = copies.start(dn_mine.at[window_of(1 - z_at)], dn_z, partner)
+    swap_q.wait_recv()
+    add_half(q_in)
+    q_sends = [
+        copies.start(owner_rows(q_in, peer[1]), q_far.at[i], peer) for i, peer in enumerate(peers)
+    ]
+    z_gu.wait_recv()
+
+    def add_gu(g, carry):
+        gu_z[g] = (gu_z[g].astype(F32) + gu_mine[g].astype(F32)).astype(BF)
+        return carry
+
+    lax.fori_loop(0, N_FS, add_gu, 0)
+    x_gu = [
+        copies.start(gu_z.at[:, x_of(device)], gu_x.at[i], device)
+        for i, device in enumerate(along)
+    ]
+    for copy in kv_sends:
+        copy.wait_recv()
+    total = kv_in[pair].astype(F32)
+    for i in range(N_CTX // 2 - 1):
+        total = total + kv_far[i].astype(F32)
+    own_kv[...] = total
+    for ref, sends, far, out in ((o_in, o_sends, o_far, o_red), (q_in, q_sends, q_far, q_red)):
+        for copy in sends:
+            copy.wait_recv()
+        total = ref[pl.ds(pl.multiple_of(f * 192, 192), 192), :].astype(F32)
+        for i in range(N_FS - 1):
+            total = total + far[i].astype(F32)
+        out[...] = total.astype(BF)
+    z_dn.wait_recv()
+    done_dn[...] = (dn_mine[window_of(z_at), :].astype(F32) + dn_z[...].astype(F32)).astype(BF)
+    for copy in x_gu:
+        copy.wait_recv()
+
+    def sum_gu_x(g, carry):
+        done_gu[g] = (
+            gu_z[g, x_at].astype(F32)
+            + gu_x[0, g].astype(F32)
+            + gu_x[1, g].astype(F32)
+            + gu_x[2, g].astype(F32)
+        ).astype(BF)
+        return carry
+
+    lax.fori_loop(0, N_FS, sum_gu_x, 0)
+    for copy in [z_gu, z_dn, swap_kv, swap_q] + x_dn + x_gu + kv_sends + o_sends + q_sends:
+        copy.wait_send()
+
+
+def attention_back(cid, arrays, vmem_arrays):
+    sum_gu, sum_dn, expo, kv_all, full_o = arrays
+    tokens, width = vmem_arrays[0].shape
+    piece, units = sum_gu.shape[2:]
+    half = sum_dn.shape[0]
+    strip = width // 4
+    window = half // 2 + 8
+    side = width // 2
+    kv_width = KV_HEADS * HD
+    rows = width // N_FS
+    anywhere = pl.BlockSpec(memory_space=pl.ANY)
+    vmem = pl.BlockSpec(memory_space=pltpu.VMEM)
+    outs = [
+        jax.ShapeDtypeStruct((N_FS, piece, units), BF),
+        jax.ShapeDtypeStruct((window, strip), BF),
+        jax.ShapeDtypeStruct((tokens, 2 * kv_width), F32),
+        jax.ShapeDtypeStruct((rows, side), BF),
+        jax.ShapeDtypeStruct((rows, side), BF),
+        jax.ShapeDtypeStruct((tokens, width), BF),
+        jax.ShapeDtypeStruct((tokens, width), F32),
+        jax.ShapeDtypeStruct((1, width), F32),
+    ]
+    return pl.pallas_call(
+        attention_back_kernel,
+        name="attention_back",
+        out_shape=outs,
+        in_specs=[anywhere] * len(arrays) + [vmem] * len(vmem_arrays),
+        out_specs=[vmem] * len(outs),
+        scratch_shapes=[
+            pltpu.VMEM(expo.shape, BF),
+            pltpu.VMEM(kv_all.shape, BF),
+            pltpu.VMEM(full_o.shape, BF),
+            pltpu.VMEM((tokens, width), BF),
+            pltpu.VMEM((tokens, width), BF),
+            pltpu.VMEM((N_FS, 4, piece, units), BF),
+            pltpu.VMEM((N_FS, 4, piece, units), BF),
+            pltpu.VMEM((3, N_FS, piece, units), BF),
+            pltpu.VMEM((half, strip), BF),
+            pltpu.VMEM((3, half, strip), BF),
+            pltpu.VMEM((window, strip), BF),
+            pltpu.VMEM((2, N_CTX // 2, tokens, 2 * kv_width), BF),
+            pltpu.VMEM((N_CTX // 2, tokens, 2 * kv_width), BF),
+            pltpu.VMEM((N_CTX // 2 - 1, tokens, 2 * kv_width), BF),
+            pltpu.VMEM((width, side), BF),
+            pltpu.VMEM((width, side), BF),
+            pltpu.VMEM((width, side), BF),
+            pltpu.VMEM((width, side), BF),
+            pltpu.VMEM((N_FS - 1, rows, side), BF),
+            pltpu.VMEM((N_FS - 1, rows, side), BF),
+            pltpu.SemaphoreType.DMA((32,)),
+            pltpu.SemaphoreType.DMA((32,)),
+            pltpu.SemaphoreType.DMA((5,)),
+        ],
+        compiler_params=pltpu.CompilerParams(
+            collective_id=cid, has_side_effects=True, vmem_limit_bytes=62 * 2**20
+        ),
+    )(*arrays, *vmem_arrays)
+
+
+def last_kernel(
+    done_gu,
+    done_dn,
+    parts,
+    qkv_hbm,
+    own_kv,
+    q_grad,
+    o_red,
+    q_red,
+    normed_ref,
+    input_ref,
+    gain_ref,
+    mid_ref,
+    middle_ref,
+    gain_two_grad,
+    cos_ref,
+    sin_ref,
+    all_gu,
+    all_dn,
+    all_at,
+    vec_sum,
+    out_rows,
+    in_rows,
+    full_qkv,
+    proj,
+    own_gu,
+    kv_out,
+    kv_keep,
+    kv_in,
+    kv_far,
+    at_all,
+    at_far,
+    at_own,
+    vec,
+    vec_fs,
+    vec_mid,
+    vec_ctx,
+    out_in,
+    send,
+    recv,
+    local,
+):
+    c, f = lax.axis_index("ctx"), lax.axis_index("fsdp")
+    core, pair = lax.rem(c, 2), lax.div(c, 2)
+    x_at, z_at = lax.rem(pair, 4), lax.div(pair, 4)
+    sibling = (flip(c, 1), f)
+    partner = (flip(c, 8), f)
+    along = [(flip(c, 2 * i), f) for i in range(1, 4)]
+    ring = [(flip(c, 2 * i), f) for i in range(1, N_CTX // 2)]
+    peers = [(c, flip(f, i)) for i in range(1, N_FS)]
+    greet(ring + peers + [sibling])
+    copies = Copies(send, recv)
+    tokens, width = normed_ref.shape
+    kv_width = KV_HEADS * HD
+    strip = done_dn.shape[1]
+    at_rows, at_cols = at_own.shape
+    rest, own = [], []
+
+    def local_copy(src, dst, n):
+        copy = pltpu.make_async_copy(src, dst, local.at[n])
+        copy.start()
+        own.append(copy)
+        return copy
+
+    def x_of(device):
+        return lax.rem(lax.div(device[0], 2), 4)
+
+    def z_of(device):
+        return lax.div(device[0], 8)
+
+    def gu_place(device):
+        return all_gu.at[lax.rem(device[0], 2), lax.div(device[0], 2)]
+
+    def dn_place(device):
+        columns = pl.ds(pl.multiple_of(x_of(device) * strip, strip), strip)
+        return all_dn.at[lax.rem(device[0], 2), z_of(device), :, columns]
+
+    def at_piece(ref, device):
+        return ref.at[
+            pl.ds(pl.multiple_of(x_of(device) * at_rows, at_rows), at_rows),
+            pl.ds(pl.multiple_of(z_of(device) * at_cols, at_cols), at_cols),
+        ]
+
+    def at_place(device):
+        return at_piece(all_at.at[lax.rem(device[0], 2)], device)
+
+    here = (c, f)
+    far = (partner[0], f)
+    gu_own = local_copy(done_gu.at[f], own_gu.at[f], 0)
+    gu_sends = [copies.start(done_gu.at[peer[1]], own_gu.at[f], peer) for peer in peers]
+    local_copy(done_dn, dn_place(here), 1)
+    dn_z = copies.start(done_dn, dn_place(here), partner)
+    dn_x = [copies.start(done_dn, dn_place(here), device) for device in along]
+    rest.append(copies.start(done_dn, dn_place(here), sibling))
+    load_qkv = local_copy(qkv_hbm, full_qkv, 2)
+
+    for h in range(KV_HEADS):
+        at = width + h * HD
+        proj[:, at : at + HD] = turn_back(
+            own_kv[:, h * HD : (h + 1) * HD], cos_ref[...], sin_ref[...]
+        ).astype(BF)
+    proj[:, width + kv_width :] = own_kv[:, kv_width:].astype(BF)
+    proj[:, :width] = q_grad[...]
+
+    def side_of(which):
+        return pl.ds(pl.multiple_of(width + which * kv_width, kv_width), kv_width)
+
+    kv_out[...] = contract_rows(normed_ref[...], proj[:, side_of(1 - core)]).astype(BF)
+    swap_kv = copies.start(kv_out, kv_in, sibling)
+    kv_keep[...] = contract_rows(normed_ref[...], proj[:, side_of(core)]).astype(BF)
+
+    gu_own.wait()
+    for copy in gu_sends:
+        copy.wait_recv()
+    gu_x = [copies.start(own_gu, gu_place(here), device) for device in along]
+    gu_z = [copies.start(own_gu, gu_place(here), partner)]
+    rest.append(copies.start(own_gu, gu_place(here), sibling))
+    local_copy(own_gu, gu_place(here), 3)
+
+    swap_kv.wait_recv()
+    kv_in[...] = (kv_in[...].astype(F32) + kv_keep[...].astype(F32)).astype(BF)
+
+    def owner_rows(owner):
+        return pl.ds(pl.multiple_of(owner * 192, 192), 192)
+
+    kv_sends = [
+        copies.start(kv_in.at[owner_rows(peer[1])], kv_far.at[i], peer)
+        for i, peer in enumerate(peers)
+    ]
+    out_sends = [
+        copies.start(parts.at[i + 1], out_in.at[i], peer) for i, peer in enumerate(peers)
+    ]
+    out_own = local_copy(parts.at[0], out_in.at[N_FS - 1], 4)
+
+    load_qkv.wait()
+    in_norm_grad = contract_cols(proj[...], full_qkv[...])
+    inputs = input_ref[...].astype(F32)
+    scale_one = lax.rsqrt(jnp.mean(inputs * inputs, axis=-1, keepdims=True) + EPSILON)
+    norm = inputs * scale_one
+    gain_one_grad = jnp.sum(in_norm_grad * norm, axis=0, keepdims=True)
+    scaled = in_norm_grad * gain_ref[...]
+    in_rows[...] = mid_ref[...] + scale_one * (
+        scaled - norm * jnp.mean(scaled * norm, axis=-1, keepdims=True)
+    )
+    bias_grad = jnp.sum(proj[...].astype(F32), axis=0, keepdims=True)
+    row = 0
+    for vector in (gain_one_grad, gain_two_grad[...], bias_grad):
+        for n in range(vector.shape[1] // 128):
+            vec[row : row + 1, :] = vector[:, n * 128 : (n + 1) * 128]
+            row += 1
+    vec_sends = [copies.start(vec, vec_fs.at[i], peer) for i, peer in enumerate(peers)]
+
+    dn_z.wait_recv()
+    dn_x2 = [copies.start(dn_place(far), dn_place(far), device) for device in along]
+    rest.append(copies.start(dn_place(far), dn_place(far), sibling))
+
+    for copy in kv_sends:
+        copy.wait_recv()
+    total = kv_in[owner_rows(f), :].astype(F32)
+    for i in range(N_FS - 1):
+        total = total + kv_far[i].astype(F32)
+    side = width // 2
+    at_all[:, :side] = o_red[...]
+    at_all[:, side : 2 * side] = q_red[...]
+    at_all[:, 2 * side :] = total.astype(BF)
+    at_sends = [
+        copies.start(at_piece(at_all, device), at_far.at[i], device)
+        for i, device in enumerate(ring)
+    ]
+    for copy in vec_sends:
+        copy.wait_recv()
+    total = vec[...]
+    for i in range(N_FS - 1):
+        total = total + vec_fs[i]
+    vec_mid[...] = total
+    vec_near = [copies.start(vec_mid, vec_ctx.at[c], device) for device in ring]
+    rest.append(copies.start(vec_mid, vec_ctx.at[c], sibling))
+    vec_ctx[pl.ds(c, 1)] = total[None]
+
+    for copy, device in zip(gu_x, along):
+        copy.wait_recv()
+        gu_z.append(copies.start(gu_place(device), gu_place(device), partner))
+        rest.append(copies.start(gu_place(device), gu_place(device), sibling))
+
+    for copy in at_sends:
+        copy.wait_recv()
+    total = at_all[
+        pl.ds(pl.multiple_of(x_at * at_rows, at_rows), at_rows),
+        pl.ds(pl.multiple_of(z_at * at_cols, at_cols), at_cols),
+    ].astype(F32)
+    for i in range(N_CTX // 2 - 1):
+        total = total + at_far[i].astype(F32)
+    at_own[...] = total.astype(BF)
+    at_near = [copies.start(at_own, at_place(here), device) for device in ring]
+    rest.append(copies.start(at_own, at_place(here), sibling))
+    local_copy(at_own, at_place(here), 5)
+
+    for copy, device in zip(vec_near, ring):
+        copy.wait_recv()
+        place = vec_ctx.at[device[0]]
+        rest.append(copies.start(place, place, sibling))
+    for one, two, device in zip(dn_x, dn_x2, along):
+        one.wait_recv()
+        rest.append(copies.start(dn_place(device), dn_place(device), sibling))
+        two.wait_recv()
+        other = (flip(device[0], 8), f)
+        rest.append(copies.start(dn_place(other), dn_place(other), sibling))
+    for copy in out_sends:
+        copy.wait_recv()
+    out_own.wait()
+    total = middle_ref[...]
+    for i in range(N_FS):
+        total = total + out_in[i].astype(F32)
+    out_rows[...] = total.astype(BF)
+    for copy, device in zip(at_near, ring):
+        copy.wait_recv()
+        rest.append(copies.start(at_place(device), at_place(device), sibling))
+    for copy, device in zip(gu_z, [here] + along):
+        copy.wait_recv()
+        other = (flip(device[0], 8), f)
+        rest.append(copies.start(gu_place(other), gu_place(other), sibling))
+    for copy in (
+        gu_sends + [dn_z] + dn_x + dn_x2 + gu_x + gu_z + [swap_kv] + kv_sends + out_sends
+        + vec_sends + vec_near + at_sends + at_near
+    ):
+        copy.wait_send()
+    for copy in rest:
+        copy.wait()
+    total = vec_ctx[0]
+    for i in range(1, N_CTX):
+        total = total + vec_ctx[i]
+    vec_sum[...] = total
+    for copy in own:
+        if copy is not gu_own and copy is not load_qkv and copy is not out_own:
+            copy.wait()
+
+
+def last_exchange(cid, arrays, vmem_arrays):
+    done_gu, done_dn, parts, full_qkv = arrays
+    tokens, width = parts.shape[1:]
+    piece, units = done_gu.shape[1:]
+    window, strip = done_dn.shape
+    rows = width // N_FS
+    kv_width = KV_HEADS * HD
+    at_width = width + kv_width
+    anywhere = pl.BlockSpec(memory_space=pl.ANY)
+    vmem = pl.BlockSpec(memory_space=pltpu.VMEM)
+    outs = [
+        jax.ShapeDtypeStruct((2, N_CTX // 2, N_FS, piece, units), BF),
+        jax.ShapeDtypeStruct((2, 2, window, width), BF),
+        jax.ShapeDtypeStruct((2, rows, at_width), BF),
+        jax.ShapeDtypeStruct((40, 128), F32),
+        jax.ShapeDtypeStruct((tokens, width), BF),
+        jax.ShapeDtypeStruct((tokens, width), F32),
+    ]
+    return pl.pallas_call(
+        last_kernel,
+        name="last_exchange",
+        out_shape=outs,
+        in_specs=[anywhere] * len(arrays) + [vmem] * len(vmem_arrays),
+        out_specs=[anywhere] * 3 + [vmem] * 3,
+        scratch_shapes=[
+            pltpu.VMEM(full_qkv.shape, BF),
+            pltpu.VMEM((tokens, width + 2 * kv_width), BF),
+            pltpu.VMEM((N_FS, piece, units), BF),
+            pltpu.VMEM((width, kv_width), BF),
+            pltpu.VMEM((width, kv_width), BF),
+            pltpu.VMEM((width, kv_width), BF),
+            pltpu.VMEM((N_FS - 1, rows, kv_width), BF),
+            pltpu.VMEM((rows, at_width), BF),
+            pltpu.VMEM((N_CTX // 2 - 1, rows // 4, at_width // 2), BF),
+            pltpu.VMEM((rows // 4, at_width // 2), BF),
+            pltpu.VMEM((40, 128), F32),
+            pltpu.VMEM((N_FS - 1, 40, 128), F32),
+            pltpu.VMEM((40, 128), F32),
+            pltpu.VMEM((N_CTX, 40, 128), F32),
+            pltpu.VMEM((N_FS, tokens, width), BF),
+            pltpu.SemaphoreType.DMA((100,)),
+            pltpu.SemaphoreType.DMA((100,)),
+            pltpu.SemaphoreType.DMA((6,)),
+        ],
+        compiler_params=pltpu.CompilerParams(
+            collective_id=cid, has_side_effects=True, vmem_limit_bytes=48 * 2**20
+        ),
+    )(*arrays, *vmem_arrays)
+
+
+def wide_kernel(gu_ref, gate_ref, up_ref):
+    for which, out in enumerate((gate_ref, up_ref)):
+        out[...] = jnp.concatenate(
+            [gu_ref[which, 0, source].astype(F32) for source in range(N_FS)], axis=1
+        )
+
+
+def wide_results(all_gu):
+    piece, units = all_gu.shape[3:]
+    parts = all_gu.shape[1]
+    shape = jax.ShapeDtypeStruct((parts * piece, N_FS * units), F32)
+    return pl.pallas_call(
+        wide_kernel,
+        name="wide_results",
+        grid=(parts,),
+        in_specs=[pl.BlockSpec((2, 1, N_FS, piece, units), lambda p: (0, p, 0, 0, 0))],
+        out_specs=[pl.BlockSpec((piece, N_FS * units), lambda p: (p, 0))] * 2,
+        out_shape=[shape, shape],
+        compiler_params=pltpu.CompilerParams(vmem_limit_bytes=32 * 2**20),
+    )(all_gu)
+
+
+def rest_kernel(dn_ref, at_ref, down_ref, o_ref, q_ref, k_ref, v_ref):
+    z = lax.rem(pl.program_id(0), 2)
+    rows = down_ref.shape[0]
+    block = dn_ref[0, 0].astype(F32)
+    down_ref[...] = jnp.where(z == 0, block[:rows], block[8 : 8 + rows])
+    side = o_ref.shape[1] // 2
+    for n in range(2):
+        part = at_ref[n].astype(F32)
+        o_ref[:, n * side : (n + 1) * side] = part[:, :side]
+        q_ref[:, n * side : (n + 1) * side] = part[:, side : 2 * side]
+        (k_ref, v_ref)[n][...] = part[:, 2 * side :]
+
+
+def rest_results(all_dn, all_at):
+    window, width = all_dn.shape[2:]
+    rows = window - 8
+    own, at_width = all_at.shape[1:]
+    kv_width = KV_HEADS * HD
+    return pl.pallas_call(
+        rest_kernel,
+        name="rest_results",
+        grid=(4,),
+        in_specs=[
+            pl.BlockSpec((1, 1, window, width), lambda n: (n // 2, n % 2, 0, 0)),
+            pl.BlockSpec((2, own // 4, at_width), lambda n: (0, n, 0)),
+        ],
+        out_specs=[
+            pl.BlockSpec((rows, width), lambda n: (n, 0)),
+            pl.BlockSpec((own // 4, width), lambda n: (n, 0)),
+            pl.BlockSpec((own // 4, width), lambda n: (n, 0)),
+            pl.BlockSpec((own // 4, kv_width), lambda n: (n, 0)),
+            pl.BlockSpec((own // 4, kv_width), lambda n: (n, 0)),
+        ],
+        out_shape=[
+            jax.ShapeDtypeStruct((4 * rows, width), F32),
+            jax.ShapeDtypeStruct((own, width), F32),
+            jax.ShapeDtypeStruct((own, width), F32),
+            jax.ShapeDtypeStruct((own, kv_width), F32),
+            jax.ShapeDtypeStruct((own, kv_width), F32),
+        ],
+        compiler_params=pltpu.CompilerParams(vmem_limit_bytes=32 * 2**20),
+    )(all_dn, all_at)
+
+
 def body(
     layer_input,
     segments,
@@ -806,131 +1289,68 @@
     mid_norm_grad, out_part, sum_gu, sum_down = feed_forward(
         8, normed_mid, cot_all, columns, down_weight
     )
-    output_rows = middle + out_part[0].astype(F32)
-    for i in range(1, N_FS):
-        output_rows = output_rows + swap_fs(out_part[i], i).astype(F32)
-    output_rows = output_rows.astype(BF)
-    sum_gu = sum_gu.reshape(N_FS, 8, piece, units)
-    sum_down = sum_down.reshape(8, units // 16, width)
-    far_gu, far_down = scatter_ctx("scatter_mlp", 3, (sum_gu, sum_down))
-    done_gu = (
-        lax.dynamic_index_in_dim(sum_gu, pair, 1, False).astype(F32)
-        + jnp.sum(far_gu.astype(F32), axis=0)
-    ).astype(BF)
-    done_down = (
-        lax.dynamic_index_in_dim(sum_down, pair, 0, False).astype(F32)
-        + jnp.sum(far_down.astype(F32), axis=0)
-    ).astype(BF)
-
-    gain_two_grad = jnp.sum(mid_norm_grad * norm_second, axis=0)
-    scaled_two = mid_norm_grad * gain_two
-    mid_grad = cotangent + scale_two * (
-        scaled_two - norm_second * jnp.mean(scaled_two * norm_second, axis=-1, keepdims=True)
-    )
-    branch_low = mid_grad.astype(BF)
-    attended_grad = contract_cols(branch_low, full_o).astype(BF)
-    grad_rows = (
-        attended_grad.reshape(tokens, KV_HEADS, GROUP, HD)
-        .transpose(1, 2, 0, 3)
-        .reshape(KV_HEADS, GROUP * tokens, HD)
-    )
-    turned_grad, key_part, value_part = attend_back(
-        expo, query, kv_all, grad_rows, mixed, inverse
-    )
-    kv_part = jnp.concatenate([key_part, value_part], axis=2)
-    kv_part = kv_part.reshape(N_CTX // 2, 2, tokens, 2 * kv_width)
-    keep_kv = jnp.where(core == 0, kv_part[:, 0], kv_part[:, 1])
-    send_kv = jnp.where(core == 0, kv_part[:, 1], kv_part[:, 0])
-    sum_kv = (keep_kv.astype(F32) + swap_ctx(send_kv, 1).astype(F32)).astype(BF)
-    (far_kv,) = scatter_ctx("scatter_kv", 4, (sum_kv,))
-    own_kv = lax.dynamic_index_in_dim(sum_kv, pair, 0, False).astype(F32) + jnp.sum(
-        far_kv.astype(F32), axis=0
-    )
-    query_rot_grad = (
-        turned_grad.reshape(KV_HEADS, HD, GROUP, tokens)
-        .transpose(3, 0, 2, 1)
-        .reshape(tokens, HEADS, HD)
-    )
-    turned_back = rotate(
-        jnp.concatenate(
-            [query_rot_grad, own_kv[:, :kv_width].reshape(tokens, KV_HEADS, HD)], axis=1
+    cos_wide = jnp.concatenate([cosine, cosine], axis=1)
+    sin_wide = jnp.concatenate([sine, -sine], axis=1)
+    done_gu, done_dn, own_kv, o_red, q_red, q_grad, mid_grad, gain_two_grad = attention_back(
+        3,
+        (sum_gu.reshape(N_FS, 8, piece, units), sum_down, expo, kv_all, full_o),
+        (
+            mid_norm_grad,
+            middle,
+            cot_low,
+            gain_two[None],
+            query,
+            mixed,
+            inverse,
+            attended,
+            normed_in,
+            cos_wide,
+            sin_wide,
         ),
-        cosine,
-        -sine,
-    ).reshape(tokens, q_width + kv_width)
-    proj_grad = jnp.concatenate([turned_back, own_kv[:, kv_width:]], axis=1).astype(BF)
-    bias_grads = jnp.sum(proj_grad.astype(F32), axis=0)
-    in_norm_grad = contract_cols(proj_grad, full_qkv)
-    gain_one_grad = jnp.sum(in_norm_grad * norm_first, axis=0)
-    scaled_one = in_norm_grad * gain_one
-    input_rows = mid_grad + scale_one * (
-        scaled_one - norm_first * jnp.mean(scaled_one * norm_first, axis=-1, keepdims=True)
-    )
-
-    q_part = contract_rows(normed_in, proj_grad).astype(BF)
-    o_part = contract_rows(attended, branch_low).astype(BF)
-    side = q_width // 2
-    low_side = jnp.concatenate(
-        [o_part[:, :side], q_part[:, :side], q_part[:, q_width : q_width + kv_width]], axis=1
-    )
-    high_side = jnp.concatenate(
-        [o_part[:, side:], q_part[:, side:q_width], q_part[:, q_width + kv_width :]], axis=1
-    )
-    keep_at = jnp.where(core == 0, low_side, high_side)
-    send_at = jnp.where(core == 0, high_side, low_side)
-    sum_at = (keep_at.astype(F32) + swap_ctx(send_at, 1).astype(F32)).astype(BF)
-    sum_at = sum_at.reshape(N_FS, 8, piece, -1)
-    (far_at,) = scatter_ctx("scatter_attn", 5, (sum_at,))
-    done_at = (
-        lax.dynamic_index_in_dim(sum_at, pair, 1, False).astype(F32)
-        + jnp.sum(far_at.astype(F32), axis=0)
-    ).astype(BF)
-
-    vectors = jnp.concatenate(
-        [
-            v.reshape(N_FS, -1)
-            for v in (
-                gain_one_grad,
-                gain_two_grad,
-                bias_grads[:q_width],
-                bias_grads[q_width : q_width + kv_width],
-                bias_grads[q_width + kv_width :],
-            )
-        ],
-        axis=1,
-    ).reshape(N_FS, 5, 128)
-    vectors = jnp.pad(vectors, ((0, 0), (0, 3), (0, 0)))
-    own_gu, own_at, own_vec = to_owner("to_owner", 6, (done_gu, done_at, vectors))
-    own_at = jnp.sum(own_at.astype(F32), axis=0).astype(BF)
-    own_vec = jnp.sum(own_vec, axis=0)
-    all_gu, all_at, all_down, all_vec = gather_ctx(
-        "gather_grads", 7, (own_gu, own_at, done_down, own_vec)
-    )
-    all_vec = jnp.sum(all_vec, axis=0)[:5].reshape(-1)
-    sum_vec = [all_vec[lo:hi] for lo, hi in zip(marks[:-1], marks[1:])]
-    all_gu = all_gu.reshape(8, 2, N_FS, piece, units).transpose(1, 0, 3, 2, 4)
-    all_gu = all_gu.reshape(2, rows, N_FS * units)
-    all_at = all_at.reshape(8, 2, piece, -1).transpose(1, 0, 2, 3).reshape(2, rows, -1)
-    all_down = all_down.reshape(8, 2, units // 16, width).transpose(1, 0, 2, 3)
-    o_grad = jnp.concatenate([all_at[0, :, :side], all_at[1, :, :side]], axis=1).astype(F32)
-    q_grad = jnp.concatenate(
-        [all_at[0, :, side:q_width], all_at[1, :, side:q_width]], axis=1
-    ).astype(F32)
+    )
+    all_gu, all_dn, all_at, all_vec, output_rows, input_rows = last_exchange(
+        4,
+        (done_gu, done_dn, out_part, full_qkv),
+        (
+            own_kv,
+            q_grad,
+            o_red,
+            q_red,
+            normed_in,
+            layer_input[0],
+            gain_one[None],
+            mid_grad,
+            middle,
+            gain_two_grad,
+            cos_wide,
+            sin_wide,
+        ),
+    )
+    gate_grad, up_grad = wide_results(all_gu)
+    down_grad, o_grad, q_weight_grad, k_grad, v_grad = rest_results(all_dn, all_at)
+    flat_vec = all_vec.reshape(-1)
+    mine = lax.axis_index("fsdp")
+    vectors = []
+    start = 0
+    for whole in (width, width, q_width, kv_width, kv_width):
+        part = whole // N_FS
+        vectors.append(lax.dynamic_slice_in_dim(flat_vec, start + mine * part, part, 0))
+        start += whole
     return (
         output_rows[None],
         input_rows[None],
-        sum_vec[0],
-        q_grad,
-        sum_vec[2],
-        all_at[0, :, q_width:].astype(F32),
-        sum_vec[3],
-        all_at[1, :, q_width:].astype(F32),
-        sum_vec[4],
+        vectors[0],
+        q_weight_grad,
+        vectors[2],
+        k_grad,
+        vectors[3],
+        v_grad,
+        vectors[4],
         o_grad,
-        sum_vec[1],
-        all_gu[0].astype(F32),
-        all_gu[1].astype(F32),
-        all_down.reshape(units, width).astype(F32),
+        vectors[1],
+        gate_grad,
+        up_grad,
+        down_grad,
     )
 
 

time: 745 us -> 539 us (0.72)
  other arithmetic: 65.4 us -> 11.2 us
  local copies, waits for them, and re-layouts: 81 us -> 30.8 us
  Pallas kernels: 527 us -> 480 us
  waiting for transfers between devices: 31.7 us -> 0 us
  matrix products: 19.1 us -> 7.06 us
  starting transfers between devices: 8.96 us -> 0 us
    pallas_call x7 -> x2, Pallas kernels: 424 us -> 144 us  [exchange(): pl.pallas_call(kernel, name=name, out_shape=[jax.ShapeDtypeStruct(s, d) f...]
    pallas_call x1 -> x4, Pallas kernels: 9.36 us -> 242 us  [the longest x1 120 us: last_exchange(): pl.pallas_call(last_kernel, name='last_exchange', out_shape=outs, in_spec...]
    convert_element_type x7 -> x0, local copies, waits for them, and re-layouts: 42.1 us -> none  [the longest x2 15.2 us: body(): all_gu[0].astype(F32)]
    ppermute x9 -> x0, waiting for transfers between devices: 31.7 us -> none  [the longest x7 31.7 us: swap_fs(): return lax.ppermute(value, 'fsdp', [(s, s ^ mask) for s in range(N_FS)])]
    convert_element_type x11 -> x1, other arithmetic: 31.6 us -> 1.04 us  [body(): normed_in = (norm_first * gain_one).astype(BF)]
    reduce_sum x9 -> x0, other arithmetic: 14.6 us -> none  [the longest x1 3.19 us: body(): jnp.sum(far_at.astype(F32), axis=0)]
    dot_general x4 -> x0, matrix products: 11.9 us -> none  [the longest x2 7.65 us: contract_cols(): lax.dot_general(left, right, (((1,), (1,)), ((), ())), preferred_element_...]
    unnamed x84 -> x48, local copies, waits for them, and re-layouts: 7.94 us -> 19.5 us
  transfers between devices with their start and end apart: 9 -> 0, of which waited for: 5 -> 0; matrix products, arithmetic and copies ran while one was open for 4% -> 0% of each run, Pallas kernels for 10% -> 0%
where the time goes in v3:
time: 539 us; the launch traced here: 531 us
  Pallas kernels  480 us (89%)
  local copies, waits for them, and re-layouts  30.8 us (6%)
  other arithmetic  11.2 us (2%)
  matrix products  7.06 us (1%)
    pallas_call x2, Pallas kernels, exchange(): pl.pallas_call(kernel, name=name, out_shape=[jax.ShapeDtypeStruct(s, d) f...  144 us
    pallas_call x1, Pallas kernels, last_exchange(): pl.pallas_call(last_kernel, name='last_exchange', out_shape=outs, in_spec...  120 us
    pallas_call x1, Pallas kernels, attention_back(): pl.pallas_call(attention_back_kernel, name='attention_back', out_shape=ou...  112 us
    pallas_call x1, Pallas kernels, feed_forward(): pl.pallas_call(mlp_kernel, name='feed_forward', out_shape=[jax.ShapeDtype...  85 us
    unnamed x48, local copies, waits for them, and re-layouts  19.5 us

profile of v3, /device:TPU:35, one launch (start us, length us, event | category | flops | bytes accessed | tf_op | source)
XLA Modules:
  0.0 530.7 jit_solution(64972308292920310)
XLA Ops:
  2.0 1.2 fusion
  3.9 3.4 concatenate.29
  9.2 2.2 pad_maximum_fusion
  11.3 1.7 dynamic-slice_select_fusion
  13.0 1.5 reshape.262
  14.6 1.0 copy.55
  15.6 63.9 %gather_qkv.1 = (bf16[8,2,96,2048]{3,2,1,0:T(8,128)(2,1)}, bf16[8,16,128]{2,1,0:T(8,128)(2,1)}, bf16[2,8,4,48,1120]{4,3,2,1,0:T(8,128)(2,1)}) custom-call(bf16[2,96,2048]{2,1,0:T(8,128)(2,1)} %bitcast.66, bf16[16,128]{1,0:T(8,128)(2,1)} %pad.4.s_ref, bf16[8,48,1120]{2,1,0:T(8,128)(2,1)} %bitcast.63), custom_call_target="tpu_custom_call" | custom-call | tf_op jit(solution)/shard_map/gather_qkv/pallas_call | solution.py:89
  81.5 1.0 fusion.2
  82.5 3.8 convolution_add_fusion.1
  88.1 80.6 %gather_kv_o.1 = (bf16[16,144,512]{2,1,0:T(8,128)(2,1)}, bf16[8,2,96,1536]{3,2,1,0:T(8,128)(2,1)}, bf16[8,128,1536]{2,1,0:T(8,128)(2,1)}) custom-call(bf16[144,512]{1,0:T(8,128)(2,1)} %pad_maximum_fusion.1.kv_ref, bf16[2,96,1536]{2,1,0:T(8,128)(2,1)} %bitcast.69, bf16[128,1536]{1,0:T(8,128)(2,1)} %get-tuple-element.105.t_ref.cot_ref), custom_call_target="tpu_custom_call" | custom-call | tf_op jit(solution)/shard_map/gather_kv_o/pallas_call | solution.py:89
  168.6 1.7 copy-done.7
  170.3 8.5 %attend.1 = (bf16[2,2048,768]{2,1,0:T(8,128)(2,1)}, f32[2,128,768]{2,1,0:T(8,128)S(1)}, f32[2,8,768]{2,1,0:T(8,128)S(1)}) custom-call(bf16[2,768,128]{2,1,0:T(8,128)(2,1)S(1)} %bitcast.50, bf16[16,144,512]{2,1,0:T(8,128)(2,1)S(1)} %copy-done.7, bf16[16,144,512]{2,1,0:T(8,128)(2,1)S(1)} %copy-done.7, f32[2,128]{1,0:T(2,128)S(1)} %pad_maximum_fusion.5.row_ref), custom_call_target="tpu_custom_call" | custom-call | flops 1610612736 | bytes 10485760 | tf_op jit(solution)/shard_map/attend/pallas_call | solution.py:236
  181.8 3.2 multiply_reduce_fusion
  186.0 85.0 %feed_forward.1 = (f32[128,1536]{1,0:T(8,128)}, bf16[8,128,1536]{2,1,0:T(8,128)(2,1)}, bf16[1536,1120]{1,0:T(8,128)(2,1)}, bf16[560,1536]{1,0:T(8,128)(2,1)}) custom-call(bf16[128,1536]{1,0:T(8,128)(2,1)} %multiply_convert_fusion.nm_ref, bf16[8,128,1536]{2,1,0:T(8,128)(2,1)} %get-tuple-element.53.cot_ref, bf16[2,1536,1120]{2,1,0:T(8,128)(2,1)} %bitcast.60, ...), custom_call_target="tpu_custom_call" | custom-call | tf_op jit(solution)/shard_map/feed_forward/pallas_call | solution.py:470
  271.1 112.0 %attention_back.1 = (bf16[8,24,1120]{2,1,0:T(8,128)(2,1)}, bf16[288,384]{1,0:T(8,128)(2,1)}, f32[128,512]{1,0:T(8,128)}, bf16[192,768]{1,0:T(8,128)(2,1)}, bf16[...) custom-call(bf16[8,8,24,1120]{3,2,1,0:T(8,128)(2,1)} %bitcast.62, ...), custom_call_target="tpu_custom_call" | custom-call | tf_op jit(solution)/shard_map/attention_back/pallas_call | solution.py:779
  383.2 1.1 copy-done.10
  384.3 1.0 copy-done.13
  385.3 1.0 copy-done.14
  390.8 120.1 %last_exchange.1 = (bf16[2,8,8,24,1120]{4,3,2,1,0:T(8,128)(2,1)}, bf16[2,2,288,1536]{3,2,1,0:T(8,128)(2,1)}, bf16[2,192,1792]{2,1,0:T(8,128)(2,1)}, f32[40,128]{...) custom-call(bf16[8,24,1120]{2,1,0:T(8,128)(2,1)S(1)} %copy-done.13, ...), custom_call_target="tpu_custom_call" | custom-call | tf_op jit(solution)/shard_map/last_exchange/pallas_call | solution.py:1071
  512.2 2.0 copy-done.4
  514.2 1.3 copy-done.9
  515.5 3.8 rest_results.1
  519.3 3.0 copy-done.3
  522.3 6.3 %wide_results.1 = (f32[192,8960]{1,0:T(8,128)}, f32[192,8960]{1,0:T(8,128)}) custom-call(bf16[2,8,8,24,1120]{4,3,2,1,0:T(8,128)(2,1)S(1)} %copy-done.3), custom_call_target="tpu_custom_call" | custom-call | tf_op jit(solution)/shard_map/wide_results/pallas_call | solution.py:1114
  (81 shorter events, 18.9 us)
Async XLA Ops:
  11.3 70.2 %copy-start.2 = (bf16[1,128,1536]{2,1,0:T(8,128)(2,1)S(1)}, bf16[1,128,1536]{2,1,0:T(8,128)(2,1)}, u32[]{:S(2)}) copy-start(bf16[1,128,1536]{2,1,0:T(8,128)(2,1)} %param.16) | copy-start | bytes 1179652
  11.3 70.2 %copy-start.21 = (bf16[1,128,1536]{2,1,0:T(8,128)(2,1)S(1)}, bf16[1,128,1536]{2,1,0:T(8,128)(2,1)}, u32[]{:S(2)}) copy-start(bf16[1,128,1536]{2,1,0:T(8,128)(2,1)} %param.31) | copy-start | bytes 1179652
  87.2 91.6 %copy-start.8 = (bf16[128,2,6,128]{3,0,2,1:T(8,128)(2,1)}, bf16[128,2,6,128]{3,0,2,1:T(8,128)(2,1)S(1)}, u32[]{:S(2)}) copy-start(bf16[128,2,6,128]{3,0,2,1:T(8,128)(2,1)S(1)} %copy.46) | copy-start | bytes 1179652
  168.6 1.7 copy-start.7
  178.8 0.6 copy-start.19
  179.4 0.9 copy-start.6
  185.0 86.0 %copy-start = (f32[128,1536]{1,0:T(8,128)}, f32[128,1536]{1,0:T(8,128)S(1)}, u32[]{:S(2)}) copy-start(f32[128,1536]{1,0:T(8,128)S(1)} %get-tuple-element.100.middle_ref) | copy-start | bytes 2359300
  271.1 112.0 %copy-start.1 = (f32[128,1536]{1,0:T(8,128)S(1)}, f32[128,1536]{1,0:T(8,128)}, u32[]{:S(2)}) copy-start(f32[128,1536]{1,0:T(8,128)} %copy-done) | copy-start | bytes 2359300
  271.1 112.0 %copy-start.5 = (bf16[128,1536]{1,0:T(8,128)(2,1)S(1)}, bf16[128,1536]{1,0:T(8,128)(2,1)}, u32[]{:S(2)}) copy-start(bf16[128,1536]{1,0:T(8,128)(2,1)} %get-tuple-element.104.normed_ref) | copy-start | bytes 1179652
  271.1 112.0 %copy-start.11 = (f32[128,128]{1,0:T(8,128)S(1)}, f32[128,128]{1,0:T(8,128)}, u32[]{:S(2)}) copy-start(f32[128,128]{1,0:T(8,128)} %get-tuple-element.101.cos_ref) | copy-start | bytes 196612
  271.1 112.0 %copy-start.12 = (f32[128,128]{1,0:T(8,128)S(1)}, f32[128,128]{1,0:T(8,128)}, u32[]{:S(2)}) copy-start(f32[128,128]{1,0:T(8,128)} %get-tuple-element.102.sin_ref) | copy-start | bytes 196612
  383.1 1.1 copy-start.10
  384.3 1.0 copy-start.13
  385.3 1.0 copy-start.14
  386.3 1.0 copy-start.15
  387.2 1.0 copy-start.16
  388.2 0.9 copy-start.17
  389.2 0.9 copy-start.18
  390.1 0.7 copy-start.20
  512.2 2.0 copy-start.4
  514.2 1.3 copy-start.9
  519.3 3.0 copy-start.3

commit v4 on v3

--- a/solution.py
+++ b/solution.py
@@ -24,17 +24,6 @@
     freqs = THETA ** (-jnp.arange(0, head_dim, 2).astype(F32) / head_dim)
     angles = position.astype(F32)[:, None] * freqs[None, :]
     return (jnp.cos(angles), jnp.sin(angles))
-
-
-def rotate(values, cosine, sine):
-    middle = values.shape[-1] // 2
-    front = values[..., :middle]
-    behind = values[..., middle:]
-    cos_head = cosine[:, None, :]
-    sin_head = sine[:, None, :]
-    return jnp.concatenate(
-        [front * cos_head - behind * sin_head, behind * cos_head + front * sin_head], axis=-1
-    )
 
 
 def contract_rows(left, right):
@@ -85,182 +74,387 @@
     pl.semaphore_wait(barrier, len(devices))
 
 
-def exchange(kernel, name, cid, ins, outs, copies, locals_):
-    return pl.pallas_call(
-        kernel,
-        name=name,
-        out_shape=[jax.ShapeDtypeStruct(s, d) for s, d in outs],
-        in_specs=[pl.BlockSpec(memory_space=pl.ANY)] * len(ins),
-        out_specs=[pl.BlockSpec(memory_space=pl.ANY)] * len(outs),
-        scratch_shapes=[
-            pltpu.SemaphoreType.DMA((copies,)),
-            pltpu.SemaphoreType.DMA((copies,)),
-            pltpu.SemaphoreType.DMA((locals_,)),
-        ],
-        compiler_params=pltpu.CompilerParams(collective_id=cid, has_side_effects=True),
-    )(*ins)
-
-
-def first_kernel(w_ref, s_ref, g_ref, w_out, s_out, g_out, send, recv, local):
+def cross_peers(c, f):
+    away = c + lax.rem(c, 2) * (flip(c, 8) - c)
+    return [(c if i < 4 else away, flip(f, i)) for i in range(1, N_FS)]
+
+
+class SharedRows:
+    def __init__(self, copies, ref, c, f, columns=None):
+        core = lax.rem(c, 2)
+        self.copies, self.f = copies, f
+        self.sibling = (flip(c, 1), f)
+        self.over = (c + core * (flip(c, 8) - c), flip(f, 4))
+        self.one, self.three = (c, flip(f, 1)), (c, flip(f, 3))
+        rows = ref.shape[1] // 2
+
+        def place(owner, part=None):
+            if part is None:
+                span = pl.ds(pl.multiple_of(core * rows, 16), rows)
+            else:
+                span = pl.ds(pl.multiple_of(core * rows + part * (rows // 2), 16), rows // 2)
+            if columns is None:
+                return ref.at[owner, span]
+            return ref.at[owner, span, columns]
+
+        self.place = place
+        mine = place(f)
+        self.from_one = copies.start(mine, mine, self.one)
+        self.from_three = copies.start(mine, mine, self.three)
+        self.z_copies = [copies.start(mine, mine, self.over)]
+        self.sent = [self.from_one, self.from_three]
+        self.rest = []
+
+    def send(self, here, device):
+        return self.copies.start(here, here, device)
+
+    def pass_y(self):
+        one, three = flip(self.f, 1), flip(self.f, 3)
+        self.from_one.wait_recv()
+        self.far = [self.send(self.place(one, 0), self.three)]
+        self.z_copies.append(self.send(self.place(one), self.over))
+        self.from_three.wait_recv()
+        self.far.append(self.send(self.place(three, 1), self.one))
+        self.z_copies.append(self.send(self.place(three), self.over))
+        self.rest.append(self.send(self.place(one), self.sibling))
+        self.rest.append(self.send(self.place(three), self.sibling))
+        for copy in self.far:
+            copy.wait_recv()
+        two = self.place(flip(self.f, 2))
+        self.z_copies.append(self.send(two, self.over))
+        self.rest.append(self.send(two, self.sibling))
+
+    def pass_z(self):
+        for copy, mask in zip(self.z_copies, (4, 5, 7, 6)):
+            copy.wait_recv()
+            self.rest.append(self.send(self.place(flip(self.f, mask)), self.sibling))
+
+    def wait(self):
+        for copy in self.rest:
+            copy.wait_recv()
+
+    def finish(self):
+        for copy in self.sent + self.far + self.z_copies + self.rest:
+            copy.wait_send()
+
+
+CHUNK = 256
+
+
+def turn_back(grad, cos_wide, sin_wide):
+    half = grad.shape[1] // 2
+    swapped = jnp.concatenate([grad[:, half:], grad[:, :half]], axis=1)
+    return grad * cos_wide + swapped * sin_wide
+
+
+def front_kernel(
+    q_hbm,
+    k_hbm,
+    v_hbm,
+    o_hbm,
+    gate_hbm,
+    up_hbm,
+    cot_ref,
+    small_ref,
+    input_ref,
+    row_ref,
+    cos_ref,
+    sin_ref,
+    w_out,
+    o_out,
+    kv_out,
+    g_out,
+    t_out,
+    e_out,
+    gains_ref,
+    normed_ref,
+    query_ref,
+    mixed_ref,
+    inv_ref,
+    attended_ref,
+    middle_ref,
+    normed_mid_ref,
+    weights,
+    full_o,
+    small_all,
+    strip,
+    stage,
+    kv_own,
+    kv,
+    s_ref,
+    expo,
+    send,
+    recv,
+    local,
+):
     c, f = lax.axis_index("ctx"), lax.axis_index("fsdp")
     core = lax.rem(c, 2)
     sibling = (flip(c, 1), f)
+    here = (c, f)
     peers = [(c, flip(f, i)) for i in range(1, N_FS)]
-    along = [(flip(c, 2 * i), f) for i in range(1, 4)]
-    greet(peers + along + [sibling])
+    ring = [(flip(c, 2 * i), f) for i in range(1, N_CTX // 2)]
+    along = ring[:3]
+    near, turn = peers[:3], peers[3]
+    greet(peers + ring + [sibling, (flip(c, 8), flip(f, 4))])
     copies = Copies(send, recv)
-
-    def columns(device):
-        part = lax.rem(device[0], N_FS)
-        return g_out.at[lax.div(part, 4), :, lax.rem(part, 4)]
+    tokens, width = input_ref.shape
+    rows = q_hbm.shape[0]
+    kv_width = KV_HEADS * HD
+    cut, units = stage.shape[1:]
+    x_part = lax.rem(c, N_FS)
+
+    def local_copy(src, dst, n):
+        copy = pltpu.make_async_copy(src, dst, local.at[n])
+        copy.start()
+        return copy
+
+    mine = weights.at[f]
+    q_columns, kv_columns = pl.ds(0, width), pl.ds(width, 2 * kv_width)
+    load_k = local_copy(k_hbm, mine.at[:, pl.ds(width, kv_width)], 1)
+    load_v = local_copy(v_hbm, mine.at[:, pl.ds(width + kv_width, kv_width)], 2)
+    block_rows = pl.ds(pl.multiple_of(lax.rem(x_part, 4) * cut, cut), cut)
+    load_gate = local_copy(gate_hbm.at[block_rows], strip.at[0], 3)
+    load_up = local_copy(up_hbm.at[block_rows], strip.at[1], 4)
+    load_q = local_copy(q_hbm, mine.at[:, q_columns], 0)
+    load_o = local_copy(o_hbm, full_o.at[f], 5)
+    load_t = local_copy(cot_ref, t_out.at[0], 6)
+    small_own = local_copy(small_ref, small_all.at[f], 7)
+    small_sends = [copies.start(small_ref, small_all.at[f], peer) for peer in peers]
+    load_k.wait()
+    load_v.wait()
+    share_kv = SharedRows(copies, weights, c, f, kv_columns)
+
+    def columns(device, part=None):
+        where = lax.rem(device[0], N_FS)
+        if part is None:
+            return g_out.at[lax.div(where, 4), :, lax.rem(where, 4)]
+        half = N_FS // 2
+        return g_out.at[lax.div(where, 4), pl.ds(part * half, half), lax.rem(where, 4)]
 
     def block(device, source):
-        part = lax.rem(device[0], N_FS)
-        return g_out.at[lax.div(part, 4), source, lax.rem(part, 4)]
-
-    here = (c, f)
-    own = [
-        pltpu.make_async_copy(g_ref.at[f], block(here, f), local.at[2]),
-        pltpu.make_async_copy(w_ref, w_out.at[f], local.at[0]),
-        pltpu.make_async_copy(s_ref, s_out.at[f], local.at[1]),
-    ]
-    for copy in own:
-        copy.start()
-    rest = [copies.start(s_ref, s_out.at[f], peer) for peer in peers]
-    blocks = [copies.start(g_ref.at[peer[1]], block(here, f), peer) for peer in peers]
-    halves = [copies.start(w_ref.at[core], w_out.at[f, core], peer) for peer in peers]
-    own[0].wait()
+        where = lax.rem(device[0], N_FS)
+        return g_out.at[lax.div(where, 4), source, lax.rem(where, 4)]
+
+    load_gate.wait()
+    load_up.wait()
+    which = lax.div(x_part, 4)
+    for owner in range(N_FS):
+        stage[owner] = strip[which, :, owner * units : (owner + 1) * units]
+    block_own = local_copy(stage.at[f], block(here, f), 8)
+    blocks = [copies.start(stage.at[peer[1]], block(here, f), peer) for peer in peers]
+    load_q.wait()
+    share_q = SharedRows(copies, weights, c, f, q_columns)
+
+    inputs = input_ref[...].astype(F32)
+    norm = inputs * lax.rsqrt(jnp.mean(inputs * inputs, axis=-1, keepdims=True) + EPSILON)
+    small_own.wait()
+    for copy in small_sends:
+        copy.wait_recv()
+
+    def vector(n, part):
+        pieces = [small_all[owner, n : n + 1, :part] for owner in range(N_FS)]
+        return jnp.concatenate(pieces, axis=1)
+
+    gain_one, gain_two, bias_q = vector(0, rows), vector(1, rows), vector(2, rows)
+    bias_k, bias_v = vector(3, kv_width // N_FS), vector(4, kv_width // N_FS)
+    gains_ref[0:1, :] = gain_one
+    gains_ref[1:2, :] = gain_two
+    normed_ref[...] = (norm * gain_one).astype(BF)
+
+    share_kv.pass_y()
+    share_kv.pass_z()
+    share_kv.wait()
+    cos_wide, sin_wide = cos_ref[...], -sin_ref[...]
+    full = weights[:, :, width:].reshape(width, 2 * kv_width)
+    projected = jnp.dot(normed_ref[...], full, preferred_element_type=F32)
+    projected = projected + jnp.concatenate([bias_k, bias_v], axis=1)
+    for h in range(KV_HEADS):
+        cols = slice(h * HD, (h + 1) * HD)
+        kv_own[:tokens, cols] = turn_back(projected[:, cols], cos_wide, sin_wide).astype(BF)
+    kv_own[:tokens, kv_width:] = projected[:, kv_width:].astype(BF)
+    marks = jnp.concatenate([row_ref[1:2, :]] * (2 * KV_HEADS), axis=1)
+    kv_own[tokens:, :] = jnp.broadcast_to(marks, (16, 2 * kv_width)).astype(BF)
+    keep_kv = local_copy(kv_own, kv.at[c], 9)
+    keys = [copies.start(kv_own, kv.at[c], device) for device in ring]
+    kv_rest = [copies.start(kv_own, kv.at[c], sibling)]
+
+    block_own.wait()
     for copy in blocks:
         copy.wait_recv()
-    mine = columns(here)
-    near = [copies.start(mine, mine, device) for device in along]
-    rest.append(copies.start(mine, mine, sibling))
-    for half, peer in zip(halves, peers):
-        half.wait_recv()
-        place = w_out.at[peer[1], core]
-        rest.append(copies.start(place, place, sibling))
-    for copy, device in zip(near, along):
-        copy.wait_recv()
-        place = columns(device)
-        rest.append(copies.start(place, place, sibling))
-    for copy in halves + blocks + near:
-        copy.wait_send()
-    for copy in rest + own[1:]:
-        copy.wait()
-
-
-def second_kernel(kv_ref, w_ref, t_ref, kv_out, w_out, t_out, send, recv, local):
-    c, f = lax.axis_index("ctx"), lax.axis_index("fsdp")
-    core = lax.rem(c, 2)
-    sibling = (flip(c, 1), f)
-    ring = [(flip(c, 2 * i), f) for i in range(1, N_CTX // 2)]
-    peers = [(c, flip(f, i)) for i in range(1, N_FS)]
-    greet(ring + peers + [sibling])
-    copies = Copies(send, recv)
-    own = [
-        pltpu.make_async_copy(kv_ref, kv_out.at[c], local.at[0]),
-        pltpu.make_async_copy(w_ref, w_out.at[f], local.at[1]),
-        pltpu.make_async_copy(t_ref, t_out.at[0], local.at[2]),
+    x_one, x_two, x_three = along
+    from_one = copies.start(columns(here), columns(here), x_one)
+    from_three = copies.start(columns(here), columns(here), x_three)
+    g_rest = [copies.start(columns(here), columns(here), sibling)]
+
+    share_q.pass_y()
+    load_o.wait()
+    share_o = SharedRows(copies, full_o, c, f)
+    half = tokens // 2
+    upper, lower = pl.ds(0, half), pl.ds(half, half)
+    low_z = copies.start(cot_ref.at[lower], t_out.at[4, lower], turn)
+    up_y = [
+        copies.start(cot_ref.at[upper], t_out.at[i + 1, upper], device)
+        for i, device in enumerate(near)
     ]
-    for copy in own:
-        copy.start()
-    keys = [copies.start(kv_ref, kv_out.at[c], device) for device in ring]
-    rest = [copies.start(kv_ref, kv_out.at[c], sibling)]
-    halves = [copies.start(w_ref.at[core], w_out.at[f, core], peer) for peer in peers]
-    rest += [copies.start(t_ref, t_out.at[i + 1], peer) for i, peer in enumerate(peers)]
+    up_z = [copies.start(cot_ref.at[upper], t_out.at[4, upper], turn)]
+    low_y = [
+        copies.start(cot_ref.at[lower], t_out.at[i + 1, lower], device)
+        for i, device in enumerate(near)
+    ]
     for key, device in zip(keys, ring):
         key.wait_recv()
-        place = kv_out.at[device[0]]
-        rest.append(copies.start(place, place, sibling))
-    for half, peer in zip(halves, peers):
-        half.wait_recv()
-        place = w_out.at[peer[1], core]
-        rest.append(copies.start(place, place, sibling))
-    for copy in keys + halves:
+        place = kv.at[device[0]]
+        kv_rest.append(copies.start(place, place, sibling))
+    share_q.pass_z()
+    share_q.wait()
+
+    full = weights[:, :, :width].reshape(width, width)
+    projected = jnp.dot(normed_ref[...], full, preferred_element_type=F32) + bias_q
+    for n in range(HEADS):
+        at = (n % GROUP) * tokens
+        query_ref[n // GROUP, at : at + tokens, :] = turn_back(
+            projected[:, n * HD : (n + 1) * HD], cos_wide, sin_wide
+        ).astype(BF)
+    save_w = local_copy(weights, w_out, 0)
+
+    from_one.wait_recv()
+    far = [copies.start(columns(x_one, 0), columns(x_one, 0), x_three)]
+    from_three.wait_recv()
+    far.append(copies.start(columns(x_three, 1), columns(x_three, 1), x_one))
+    for device in (x_one, x_three):
+        g_rest.append(copies.start(columns(device), columns(device), sibling))
+    share_o.pass_y()
+    keep_kv.wait()
+    for copy in kv_rest:
+        copy.wait_recv()
+    save_kv = local_copy(kv, kv_out, 1)
+
+    length = N_CTX * tokens
+    scale = HD ** (-0.5)
+    row_place, row_seg = row_ref[0:1, :], row_ref[1:2, :]
+    key_seg = kv[:, tokens : tokens + 16, :HD][:, 0, :].astype(F32).T
+    within = lax.broadcasted_iota(jnp.int32, (tokens, tokens), 0)
+    saves = []
+    for h in range(KV_HEADS):
+        query = query_ref[h]
+        top = jnp.full((8, GROUP * tokens), -1e30, F32)
+        for b in range(N_CTX):
+            place = jnp.where(
+                within < half, b * half + within, (2 * N_CTX - 1 - b) * half + within - half
+            ).astype(F32)
+            allowed = (place <= row_place) & (key_seg[:, b : b + 1] == row_seg) & (row_seg > 0.5)
+            bias = jnp.where(allowed, 0.0, -1e30).astype(F32)
+            scores = contract_cols(kv[b, :tokens, h * HD : (h + 1) * HD], query) * scale
+            scores = scores + jnp.concatenate([bias] * GROUP, axis=1)
+            s_ref[b * tokens : (b + 1) * tokens, :] = scores
+            top = jnp.maximum(top, jnp.max(scores.reshape(tokens // 8, 8, -1), axis=0))
+        highest = jnp.maximum(jnp.max(top, axis=0, keepdims=True), -1e29)
+        total = jnp.zeros((8, GROUP * tokens), F32)
+        mixed = jnp.zeros((HD, GROUP * tokens), F32)
+        for j in range(length // CHUNK):
+            part = jnp.exp(s_ref[j * CHUNK : (j + 1) * CHUNK, :] - highest)
+            total = total + jnp.sum(part.reshape(CHUNK // 8, 8, -1), axis=0)
+            low = part.astype(BF)
+            expo[h, j * CHUNK : (j + 1) * CHUNK, :] = low
+            at = (KV_HEADS + h) * HD
+            values = kv[2 * j : 2 * j + 2, :tokens, at : at + HD].reshape(CHUNK, HD)
+            mixed = mixed + contract_rows(values, low)
+        total = jnp.sum(total, axis=0, keepdims=True)
+        inverse = 1.0 / jnp.where(total > 0.5, total, 1.0)
+        mixed = mixed * inverse
+        mixed_ref[h] = mixed
+        inv_ref[h] = jnp.broadcast_to(inverse, (8, GROUP * tokens))
+        for i in range(GROUP):
+            at = (h * GROUP + i) * HD
+            attended_ref[:, at : at + HD] = mixed[:, i * tokens : (i + 1) * tokens].T.astype(BF)
+        saves.append(local_copy(expo.at[h], e_out.at[h], 2 + h))
+        if h == 0:
+            low_z.wait_recv()
+            for i, device in enumerate(near):
+                low_y.append(copies.start(t_out.at[4, lower], t_out.at[5 + i, lower], device))
+            for i, copy in enumerate(up_y):
+                copy.wait_recv()
+                up_z.append(copies.start(t_out.at[i + 1, upper], t_out.at[5 + i, upper], turn))
+            for copy in far:
+                copy.wait_recv()
+            g_rest.append(copies.start(columns(x_two), columns(x_two), sibling))
+            share_o.pass_z()
+
+    share_o.wait()
+    product = jnp.dot(
+        attended_ref[...], full_o[...].reshape(width, width), preferred_element_type=F32
+    )
+    middle = input_ref[...].astype(F32) + product
+    middle_ref[...] = middle
+    scale_two = lax.rsqrt(jnp.mean(middle * middle, axis=-1, keepdims=True) + EPSILON)
+    normed_mid_ref[...] = (middle * scale_two * gains_ref[1:2, :]).astype(BF)
+    save_o = local_copy(full_o, o_out, 4)
+    for copy in low_y + up_z + g_rest:
+        copy.wait_recv()
+    for share in (share_kv, share_q, share_o):
+        share.finish()
+    for copy in (
+        small_sends + blocks + [from_one, from_three] + far + g_rest + low_y + up_z + up_y
+        + [low_z] + keys + kv_rest
+    ):
         copy.wait_send()
-    for copy in rest + own:
+    for copy in saves + [save_w, save_kv, save_o, load_t]:
         copy.wait()
 
 
-CHUNK = 256
-
-
-def attend_kernel(q_ref, k_ref, v_ref, row_ref, e_ref, o_ref, inv_ref, s_ref):
-    tokens = k_ref.shape[1] - 16
-    length = N_CTX * tokens
-    half = tokens // 2
-    scale = HD ** (-0.5)
-    query = q_ref[0]
-    row_place, row_seg = row_ref[0:1, :], row_ref[1:2, :]
-    key_seg = k_ref[:, tokens : tokens + 16, :][:, 0, :].astype(F32).T
-    within = lax.broadcasted_iota(jnp.int32, (tokens, tokens), 0)
-    top = jnp.full((8, GROUP * tokens), -1e30, F32)
-    for b in range(N_CTX):
-        place = jnp.where(
-            within < half, b * half + within, (2 * N_CTX - 1 - b) * half + within - half
-        ).astype(F32)
-        allowed = (place <= row_place) & (key_seg[:, b : b + 1] == row_seg) & (row_seg > 0.5)
-        bias = jnp.where(allowed, 0.0, -1e30).astype(F32)
-        scores = (
-            lax.dot_general(
-                k_ref[b, :tokens, :],
-                query,
-                (((1,), (1,)), ((), ())),
-                preferred_element_type=F32,
-            )
-            * scale
-            + jnp.concatenate([bias] * GROUP, axis=1)
-        )
-        s_ref[b * tokens : (b + 1) * tokens, :] = scores
-        top = jnp.maximum(top, jnp.max(scores.reshape(tokens // 8, 8, -1), axis=0))
-    highest = jnp.maximum(jnp.max(top, axis=0, keepdims=True), -1e29)
-    total = jnp.zeros((8, GROUP * tokens), F32)
-    mixed = jnp.zeros((HD, GROUP * tokens), F32)
-    for j in range(length // CHUNK):
-        part = jnp.exp(s_ref[j * CHUNK : (j + 1) * CHUNK, :] - highest)
-        total = total + jnp.sum(part.reshape(CHUNK // 8, 8, -1), axis=0)
-        low = part.astype(BF)
-        e_ref[0, j * CHUNK : (j + 1) * CHUNK, :] = low
-        values = v_ref[2 * j : 2 * j + 2, :tokens, :].reshape(CHUNK, HD)
-        mixed = mixed + contract_rows(values, low)
-    total = jnp.sum(total, axis=0, keepdims=True)
-    inverse = 1.0 / jnp.where(total > 0.5, total, 1.0)
-    o_ref[0] = mixed * inverse
-    inv_ref[0] = jnp.broadcast_to(inverse, (8, GROUP * tokens))
-
-
-def attend(query, keys_values, rows):
-    tokens = rows.shape[1]
+def front(cid, arrays, vmem_arrays):
+    tokens, width = vmem_arrays[1].shape
+    rows, all_units = arrays[4].shape
+    units = all_units // N_FS
+    cut = rows // 4
+    kv_width = KV_HEADS * HD
     wide = GROUP * tokens
     length = N_CTX * tokens
+    anywhere = pl.BlockSpec(memory_space=pl.ANY)
+    vmem = pl.BlockSpec(memory_space=pltpu.VMEM)
+    weights = (N_FS, rows, width + 2 * kv_width)
+    full_o = (N_FS, rows, width)
+    kv = (N_CTX, tokens + 16, 2 * kv_width)
+    expo = (KV_HEADS, length, wide)
     return pl.pallas_call(
-        attend_kernel,
-        name="attend",
-        grid=(KV_HEADS,),
-        in_specs=[
-            pl.BlockSpec((1, wide, HD), lambda h: (h, 0, 0)),
-            pl.BlockSpec((N_CTX, tokens + 16, HD), lambda h: (0, 0, h)),
-            pl.BlockSpec((N_CTX, tokens + 16, HD), lambda h: (0, 0, KV_HEADS + h)),
-            pl.BlockSpec((2, tokens), lambda h: (0, 0)),
-        ],
-        out_specs=[
-            pl.BlockSpec((1, length, wide), lambda h: (h, 0, 0)),
-            pl.BlockSpec((1, HD, wide), lambda h: (h, 0, 0)),
-            pl.BlockSpec((1, 8, wide), lambda h: (h, 0, 0)),
-        ],
+        front_kernel,
+        name="front",
         out_shape=[
-            jax.ShapeDtypeStruct((KV_HEADS, length, wide), BF),
+            jax.ShapeDtypeStruct(weights, BF),
+            jax.ShapeDtypeStruct(full_o, BF),
+            jax.ShapeDtypeStruct(kv, BF),
+            jax.ShapeDtypeStruct((2, N_FS, 4, cut, units), BF),
+            jax.ShapeDtypeStruct((N_FS, tokens, width), BF),
+            jax.ShapeDtypeStruct(expo, BF),
+            jax.ShapeDtypeStruct((2, width), F32),
+            jax.ShapeDtypeStruct((tokens, width), BF),
+            jax.ShapeDtypeStruct((KV_HEADS, wide, HD), BF),
             jax.ShapeDtypeStruct((KV_HEADS, HD, wide), F32),
             jax.ShapeDtypeStruct((KV_HEADS, 8, wide), F32),
+            jax.ShapeDtypeStruct((tokens, width), BF),
+            jax.ShapeDtypeStruct((tokens, width), F32),
+            jax.ShapeDtypeStruct((tokens, width), BF),
         ],
-        scratch_shapes=[pltpu.VMEM((length, wide), F32)],
-        compiler_params=pltpu.CompilerParams(vmem_limit_bytes=48 * 2**20),
-        cost_estimate=pl.CostEstimate(
-            flops=4 * KV_HEADS * length * wide * HD,
-            bytes_accessed=2 * KV_HEADS * length * wide + 4 * 2**20,
-            transcendentals=KV_HEADS * length * wide,
+        in_specs=[anywhere] * len(arrays) + [vmem] * len(vmem_arrays),
+        out_specs=[anywhere] * 6 + [vmem] * 8,
+        scratch_shapes=[
+            pltpu.VMEM(weights, BF),
+            pltpu.VMEM(full_o, BF),
+            pltpu.VMEM((N_FS,) + vmem_arrays[0].shape, F32),
+            pltpu.VMEM((2, cut, all_units), BF),
+            pltpu.VMEM((N_FS, cut, units), BF),
+            pltpu.VMEM(kv[1:], BF),
+            pltpu.VMEM(kv, BF),
+            pltpu.VMEM((length, wide), F32),
+            pltpu.VMEM(expo, BF),
+            pltpu.SemaphoreType.DMA((104,)),
+            pltpu.SemaphoreType.DMA((104,)),
+            pltpu.SemaphoreType.DMA((10,)),
+        ],
+        compiler_params=pltpu.CompilerParams(
+            collective_id=cid, has_side_effects=True, vmem_limit_bytes=60 * 2**20
         ),
-    )(query, keys_values, keys_values, rows)
+    )(*arrays, *vmem_arrays)
 
 
 def apart(value, mask):
@@ -504,12 +698,6 @@
             collective_id=cid, has_side_effects=True, vmem_limit_bytes=60 * 2**20
         ),
     )(normed, cot_all, columns, down_weight)
-
-
-def turn_back(grad, cos_wide, sin_wide):
-    half = grad.shape[1] // 2
-    swapped = jnp.concatenate([grad[:, half:], grad[:, :half]], axis=1)
-    return grad * cos_wide + swapped * sin_wide
 
 
 def attention_back_kernel(
@@ -568,7 +756,7 @@
     partner = (flip(c, 8), f)
     along = [(flip(c, 2 * i), f) for i in range(1, 4)]
     ring = [(flip(c, 2 * i), f) for i in range(1, N_CTX // 2)]
-    peers = [(c, flip(f, i)) for i in range(1, N_FS)]
+    peers = cross_peers(c, f)
     greet(ring + peers + [sibling])
     copies = Copies(send, recv)
     tokens, width = mng_ref.shape
@@ -589,7 +777,10 @@
         copy.start()
         return copy
 
-    z_gu = copies.start(sum_gu.at[:, pl.ds(4 * (1 - z_at), 4)], gu_z, partner)
+    x_gu = [
+        copies.start(sum_gu.at[:, :, x_of(device)], gu_x.at[i], device)
+        for i, device in enumerate(along)
+    ]
     x_dn = [
         copies.start(strip_of(sum_dn, x_of(device)), dn_x.at[i], device)
         for i, device in enumerate(along)
@@ -600,7 +791,7 @@
         local_copy(expo_hbm, expo, 2),
     ]
     loads_own = [
-        local_copy(sum_gu.at[:, pl.ds(4 * z_at, 4)], gu_mine, 3),
+        local_copy(sum_gu.at[:, :, x_at], gu_mine, 3),
         local_copy(strip_of(sum_dn, x_at), dn_mine, 4),
     ]
 
@@ -711,17 +902,20 @@
     q_sends = [
         copies.start(owner_rows(q_in, peer[1]), q_far.at[i], peer) for i, peer in enumerate(peers)
     ]
-    z_gu.wait_recv()
-
-    def add_gu(g, carry):
-        gu_z[g] = (gu_z[g].astype(F32) + gu_mine[g].astype(F32)).astype(BF)
+    for copy in x_gu:
+        copy.wait_recv()
+
+    def sum_gu_x(g, carry):
+        gu_mine[g] = (
+            gu_mine[g].astype(F32)
+            + gu_x[0, g].astype(F32)
+            + gu_x[1, g].astype(F32)
+            + gu_x[2, g].astype(F32)
+        ).astype(BF)
         return carry
 
-    lax.fori_loop(0, N_FS, add_gu, 0)
-    x_gu = [
-        copies.start(gu_z.at[:, x_of(device)], gu_x.at[i], device)
-        for i, device in enumerate(along)
-    ]
+    lax.fori_loop(0, N_FS, sum_gu_x, 0)
+    z_gu = copies.start(gu_mine.at[:, 1 - z_at], gu_z, partner)
     for copy in kv_sends:
         copy.wait_recv()
     total = kv_in[pair].astype(F32)
@@ -737,19 +931,13 @@
         out[...] = total.astype(BF)
     z_dn.wait_recv()
     done_dn[...] = (dn_mine[window_of(z_at), :].astype(F32) + dn_z[...].astype(F32)).astype(BF)
-    for copy in x_gu:
-        copy.wait_recv()
-
-    def sum_gu_x(g, carry):
-        done_gu[g] = (
-            gu_z[g, x_at].astype(F32)
-            + gu_x[0, g].astype(F32)
-            + gu_x[1, g].astype(F32)
-            + gu_x[2, g].astype(F32)
-        ).astype(BF)
+    z_gu.wait_recv()
+
+    def add_gu(g, carry):
+        done_gu[g] = (gu_mine[g, z_at].astype(F32) + gu_z[g].astype(F32)).astype(BF)
         return carry
 
-    lax.fori_loop(0, N_FS, sum_gu_x, 0)
+    lax.fori_loop(0, N_FS, add_gu, 0)
     for copy in [z_gu, z_dn, swap_kv, swap_q] + x_dn + x_gu + kv_sends + o_sends + q_sends:
         copy.wait_send()
 
@@ -757,7 +945,7 @@
 def attention_back(cid, arrays, vmem_arrays):
     sum_gu, sum_dn, expo, kv_all, full_o = arrays
     tokens, width = vmem_arrays[0].shape
-    piece, units = sum_gu.shape[2:]
+    piece, units = sum_gu.shape[3:]
     half = sum_dn.shape[0]
     strip = width // 4
     window = half // 2 + 8
@@ -788,9 +976,9 @@
             pltpu.VMEM(full_o.shape, BF),
             pltpu.VMEM((tokens, width), BF),
             pltpu.VMEM((tokens, width), BF),
-            pltpu.VMEM((N_FS, 4, piece, units), BF),
-            pltpu.VMEM((N_FS, 4, piece, units), BF),
-            pltpu.VMEM((3, N_FS, piece, units), BF),
+            pltpu.VMEM((N_FS, 2, piece, units), BF),
+            pltpu.VMEM((N_FS, piece, units), BF),
+            pltpu.VMEM((3, N_FS, 2, piece, units), BF),
             pltpu.VMEM((half, strip), BF),
             pltpu.VMEM((3, half, strip), BF),
             pltpu.VMEM((window, strip), BF),
@@ -863,7 +1051,8 @@
     along = [(flip(c, 2 * i), f) for i in range(1, 4)]
     ring = [(flip(c, 2 * i), f) for i in range(1, N_CTX // 2)]
     peers = [(c, flip(f, i)) for i in range(1, N_FS)]
-    greet(ring + peers + [sibling])
+    cross = cross_peers(c, f)
+    greet(ring + peers + [(flip(c, 8), flip(f, i)) for i in range(4, N_FS)] + [sibling])
     copies = Copies(send, recv)
     tokens, width = normed_ref.shape
     kv_width = KV_HEADS * HD
@@ -927,8 +1116,8 @@
     gu_own.wait()
     for copy in gu_sends:
         copy.wait_recv()
+    gu_z = copies.start(own_gu, gu_place(here), partner)
     gu_x = [copies.start(own_gu, gu_place(here), device) for device in along]
-    gu_z = [copies.start(own_gu, gu_place(here), partner)]
     rest.append(copies.start(own_gu, gu_place(here), sibling))
     local_copy(own_gu, gu_place(here), 3)
 
@@ -940,7 +1129,7 @@
 
     kv_sends = [
         copies.start(kv_in.at[owner_rows(peer[1])], kv_far.at[i], peer)
-        for i, peer in enumerate(peers)
+        for i, peer in enumerate(cross)
     ]
     out_sends = [
         copies.start(parts.at[i + 1], out_in.at[i], peer) for i, peer in enumerate(peers)
@@ -992,10 +1181,9 @@
     rest.append(copies.start(vec_mid, vec_ctx.at[c], sibling))
     vec_ctx[pl.ds(c, 1)] = total[None]
 
-    for copy, device in zip(gu_x, along):
-        copy.wait_recv()
-        gu_z.append(copies.start(gu_place(device), gu_place(device), partner))
-        rest.append(copies.start(gu_place(device), gu_place(device), sibling))
+    gu_z.wait_recv()
+    gu_x2 = [copies.start(gu_place(far), gu_place(far), device) for device in along]
+    rest.append(copies.start(gu_place(far), gu_place(far), sibling))
 
     for copy in at_sends:
         copy.wait_recv()
@@ -1030,12 +1218,14 @@
     for copy, device in zip(at_near, ring):
         copy.wait_recv()
         rest.append(copies.start(at_place(device), at_place(device), sibling))
-    for copy, device in zip(gu_z, [here] + along):
-        copy.wait_recv()
+    for one, two, device in zip(gu_x, gu_x2, along):
+        one.wait_recv()
+        rest.append(copies.start(gu_place(device), gu_place(device), sibling))
+        two.wait_recv()
         other = (flip(device[0], 8), f)
         rest.append(copies.start(gu_place(other), gu_place(other), sibling))
     for copy in (
-        gu_sends + [dn_z] + dn_x + dn_x2 + gu_x + gu_z + [swap_kv] + kv_sends + out_sends
+        gu_sends + [dn_z] + dn_x + dn_x2 + gu_x + [gu_z] + gu_x2 + [swap_kv] + kv_sends + out_sends
         + vec_sends + vec_near + at_sends + at_near
     ):
         copy.wait_send()
@@ -1191,84 +1381,18 @@
     kv_width = KV_HEADS * HD
     half_block = tokens // 2
     ctx = lax.axis_index("ctx")
-    core = lax.rem(ctx, 2)
-    pair = lax.div(ctx, 2)
-    x_part = lax.rem(ctx, N_FS)
-    inputs = layer_input[0].astype(F32)
     segment = segments[0]
-    position = positions[0]
-    keep = (segment > 0).astype(F32)[:, None]
-    cotangent = out_cotangent[0].astype(F32) * keep
-    cot_low = cotangent.astype(BF)
-
-    qkv = jnp.concatenate([q_weight, k_weight, v_weight], axis=1).reshape(2, rows // 2, -1)
-    small = jnp.concatenate([attn_norm, mlp_norm, q_bias, k_bias, v_bias]).reshape(-1, 128)
-    small = jnp.pad(small, ((0, 16 - small.shape[0]), (0, 0)))
-    cut = rows // 4
-    start = lax.rem(x_part, 4) * cut
-    gate_cut = lax.dynamic_slice_in_dim(gate_weight, start, cut, 0)
-    up_cut = lax.dynamic_slice_in_dim(up_weight, start, cut, 0)
-    blocks = (
-        jnp.where(x_part < 4, gate_cut, up_cut).reshape(cut, N_FS, units).transpose(1, 0, 2)
+    cot_low = jnp.where((segment > 0)[:, None], out_cotangent[0], 0)
+    small = jnp.stack(
+        [
+            jnp.pad(v.astype(F32), (0, 256 - v.shape[0]))
+            for v in (attn_norm, mlp_norm, q_bias, k_bias, v_bias)
+        ]
+        + [jnp.zeros((256,), F32)] * 3
     )
-    full_qkv, small_all, columns = exchange(
-        first_kernel,
-        "gather_qkv",
-        1,
-        (qkv, small, blocks),
-        [
-            ((N_FS,) + qkv.shape, BF),
-            ((N_FS,) + small.shape, BF),
-            ((2, N_FS, 4, cut, units), BF),
-        ],
-        35,
-        3,
-    )
-    columns = columns.reshape(2, width, units)
-
-    flat = small_all[:, :5].reshape(N_FS, -1)
-    marks = [0, rows, 2 * rows, 2 * rows + q_width // N_FS]
-    marks += [marks[-1] + kv_width // N_FS, marks[-1] + 2 * kv_width // N_FS]
-    gain_one, gain_two, bias_q, bias_k, bias_v = (
-        flat[:, lo:hi].reshape(-1).astype(F32) for lo, hi in zip(marks[:-1], marks[1:])
-    )
-    bias_all = jnp.concatenate([bias_q, bias_k, bias_v])
-    full_qkv = full_qkv.reshape(width, q_width + 2 * kv_width)
-
-    scale_one = lax.rsqrt(jnp.mean(inputs * inputs, axis=-1, keepdims=True) + EPSILON)
-    norm_first = inputs * scale_one
-    normed_in = (norm_first * gain_one).astype(BF)
-    projected = jnp.dot(normed_in, full_qkv, preferred_element_type=F32) + bias_all
-    cosine, sine = rope_tables(position, HD)
-    turned = rotate(
-        projected[:, : q_width + kv_width].reshape(tokens, HEADS + KV_HEADS, HD), cosine, sine
-    ).astype(BF)
-    value_low = projected[:, q_width + kv_width :].astype(BF)
-    query = (
-        turned[:, :HEADS]
-        .reshape(tokens, KV_HEADS, GROUP, HD)
-        .transpose(1, 2, 0, 3)
-        .reshape(KV_HEADS, GROUP * tokens, HD)
-    )
-    keys_values = jnp.concatenate([turned[:, HEADS:].reshape(tokens, kv_width), value_low], axis=1)
-    segment_rows = jnp.broadcast_to(
-        jnp.tile(segment.astype(BF)[None, :], (1, 2 * KV_HEADS)), (16, 2 * kv_width)
-    )
-    keys_values = jnp.concatenate([keys_values, segment_rows], axis=0)
-    kv_all, full_o, cot_all = exchange(
-        second_kernel,
-        "gather_kv_o",
-        2,
-        (keys_values, o_weight.reshape(2, rows // 2, width), cot_low),
-        [
-            ((N_CTX,) + keys_values.shape, BF),
-            ((N_FS, 2, rows // 2, width), BF),
-            ((N_FS, tokens, width), BF),
-        ],
-        36,
-        3,
-    )
-    full_o = full_o.reshape(q_width, width)
+    cosine, sine = rope_tables(positions[0], HD)
+    cos_wide = jnp.concatenate([cosine, cosine], axis=1)
+    sin_wide = jnp.concatenate([sine, -sine], axis=1)
     within = jnp.arange(tokens, dtype=jnp.int32)
     row_place = jnp.where(
         within < half_block,
@@ -1276,29 +1400,43 @@
         (2 * N_CTX - 1 - ctx) * half_block + within - half_block,
     )
     row_info = jnp.stack([row_place.astype(F32), segment.astype(F32)])
-    expo, mixed, inverse = attend(query, kv_all, row_info)
-    attended = (
-        mixed.reshape(KV_HEADS, HD, GROUP, tokens).transpose(3, 0, 2, 1).reshape(tokens, q_width)
-    ).astype(BF)
-    middle = inputs + jnp.dot(attended, full_o, preferred_element_type=F32)
-    scale_two = lax.rsqrt(jnp.mean(middle * middle, axis=-1, keepdims=True) + EPSILON)
-    norm_second = middle * scale_two
-    normed_mid = (norm_second * gain_two).astype(BF)
+    (
+        full_qkv,
+        full_o,
+        kv_all,
+        columns,
+        cot_all,
+        expo,
+        gains,
+        normed_in,
+        query,
+        mixed,
+        inverse,
+        attended,
+        middle,
+        normed_mid,
+    ) = front(
+        1,
+        (q_weight, k_weight, v_weight, o_weight, gate_weight, up_weight, cot_low),
+        (small, layer_input[0], row_info, cos_wide, sin_wide),
+    )
+    full_qkv = full_qkv.reshape(width, q_width + 2 * kv_width)
+    full_o = full_o.reshape(q_width, width)
+    columns = columns.reshape(2, width, units)
+    gain_one, gain_two = gains[0:1], gains[1:2]
 
     piece = rows // 8
     mid_norm_grad, out_part, sum_gu, sum_down = feed_forward(
         8, normed_mid, cot_all, columns, down_weight
     )
-    cos_wide = jnp.concatenate([cosine, cosine], axis=1)
-    sin_wide = jnp.concatenate([sine, -sine], axis=1)
     done_gu, done_dn, own_kv, o_red, q_red, q_grad, mid_grad, gain_two_grad = attention_back(
         3,
-        (sum_gu.reshape(N_FS, 8, piece, units), sum_down, expo, kv_all, full_o),
+        (sum_gu.reshape(N_FS, 2, 4, piece, units), sum_down, expo, kv_all, full_o),
         (
             mid_norm_grad,
             middle,
             cot_low,
-            gain_two[None],
+            gain_two,
             query,
             mixed,
             inverse,
@@ -1318,7 +1456,7 @@
             q_red,
             normed_in,
             layer_input[0],
-            gain_one[None],
+            gain_one,
             mid_grad,
             middle,
             gain_two_grad,

time: 539 us -> 443 us (0.82)
  Pallas kernels: 480 us -> 409 us
  local copies, waits for them, and re-layouts: 30.8 us -> 14.9 us
  matrix products: 7.06 us -> 0 us
    pallas_call x3 -> x1, Pallas kernels: 153 us -> 97 us  [front(): pl.pallas_call(front_kernel, name='front', out_shape=[jax.ShapeDtypeStruc...]
    pallas_call x1, Pallas kernels: 112 us -> 101 us  [attention_back(): pl.pallas_call(attention_back_kernel, name='attention_back', out_shape=ou...]
    unnamed x48 -> x40, local copies, waits for them, and re-layouts: 19.5 us -> 12.4 us
    dot_general x2 -> x0, matrix products: 7.06 us -> none  [the longest x1 3.84 us: body(): jnp.dot(normed_in, full_qkv, preferred_element_type=F32) + bias_all]
where the time goes in v4:
time: 443 us; the launch traced here: 434 us
  Pallas kernels  409 us (92%)
  local copies, waits for them, and re-layouts  14.9 us (3%)
  other arithmetic  8.76 us (2%)
    pallas_call x1, Pallas kernels, last_exchange(): pl.pallas_call(last_kernel, name='last_exchange', out_shape=outs, in_spec...  117 us
    pallas_call x1, Pallas kernels, attention_back(): pl.pallas_call(attention_back_kernel, name='attention_back', out_shape=ou...  101 us
    pallas_call x1, Pallas kernels, front(): pl.pallas_call(front_kernel, name='front', out_shape=[jax.ShapeDtypeStruc...  97 us
    pallas_call x1, Pallas kernels, feed_forward(): pl.pallas_call(mlp_kernel, name='feed_forward', out_shape=[jax.ShapeDtype...  84.4 us
    unnamed x40, local copies, waits for them, and re-layouts  12.4 us

profile of v4, /device:TPU:35, one launch (start us, length us, event | category | flops | bytes accessed | tf_op | source)
XLA Modules:
  0.0 434.3 jit_solution(5571546338744344258)
XLA Ops:
  0.6 0.7 convert_bitcast_fusion
  1.6 0.8 pad_maximum_fusion
  3.6 0.7 compare_bitcast_fusion
  4.3 1.8 bitcast_select_fusion.cot_ref
  6.1 0.7 pad_convert_fusion.4
  6.8 0.7 pad_convert_fusion.3
  7.4 0.7 pad_convert_fusion.2
  10.0 97.0 %front.1 = (bf16[8,192,2048]{2,1,0:T(8,128)(2,1)}, bf16[8,192,1536]{2,1,0:T(8,128)(2,1)}, bf16[16,144,512]{2,1,0:T(8,128)(2,1)}, bf16[2,8,4,48,1120]{4,3,2,1,0:T...) custom-call(bf16[192,1536]{1,0:T(8,128)(2,1)} %q_hbm.1, ...), custom_call_target="tpu_custom_call" | custom-call | tf_op jit(solution)/shard_map/front/pallas_call | solution.py:419
  107.1 84.4 %feed_forward.1 = (f32[128,1536]{1,0:T(8,128)}, bf16[8,128,1536]{2,1,0:T(8,128)(2,1)}, bf16[1536,1120]{1,0:T(8,128)(2,1)}, bf16[560,1536]{1,0:T(8,128)(2,1)}) custom-call(bf16[128,1536]{1,0:T(8,128)(2,1)} %get-tuple-element.53.nm_ref, bf16[8,128,1536]{2,1,0:T(8,128)(2,1)} %get-tuple-element.54.cot_ref, bf16[2,1536,1120]{2,1,0:T(8,128)(2,1)} %bitcast.25, ...), custom_call_target="tpu_custom_call" | custom-call | tf_op jit(solution)/shard_map/feed_forward/pallas_call | solution.py:664
  192.2 101.0 %attention_back.1 = (bf16[8,24,1120]{2,1,0:T(8,128)(2,1)}, bf16[288,384]{1,0:T(8,128)(2,1)}, f32[128,512]{1,0:T(8,128)}, bf16[192,768]{1,0:T(8,128)(2,1)}, bf16[...) custom-call(bf16[8,2,4,24,1120]{4,3,2,1,0:T(8,128)(2,1)} %bitcast.28, ...), custom_call_target="tpu_custom_call" | custom-call | tf_op jit(solution)/shard_map/attention_back/pallas_call | solution.py:967
  293.3 1.1 copy-done.8
  294.4 1.0 copy-done.9
  295.4 1.0 copy-done.10
  296.4 1.0 copy-done.13
  297.4 1.0 copy-done.14
  298.3 0.9 copy-done.15
  299.3 0.9 copy-done.16
  300.2 0.7 copy-done.17
  300.9 116.6 %last_exchange.1 = (bf16[2,8,8,24,1120]{4,3,2,1,0:T(8,128)(2,1)}, bf16[2,2,288,1536]{3,2,1,0:T(8,128)(2,1)}, bf16[2,192,1792]{2,1,0:T(8,128)(2,1)}, f32[40,128]{...) custom-call(bf16[8,24,1120]{2,1,0:T(8,128)(2,1)S(1)} %copy-done.9, ...), custom_call_target="tpu_custom_call" | custom-call | tf_op jit(solution)/shard_map/last_exchange/pallas_call | solution.py:1261
  417.5 3.1 copy-done
  420.7 6.5 %wide_results.1 = (f32[192,8960]{1,0:T(8,128)}, f32[192,8960]{1,0:T(8,128)}) custom-call(bf16[2,8,8,24,1120]{4,3,2,1,0:T(8,128)(2,1)S(1)} %copy-done), custom_call_target="tpu_custom_call" | custom-call | tf_op jit(solution)/shard_map/wide_results/pallas_call | solution.py:1304
  427.2 3.8 rest_results.1
  432.3 0.7 copy.32
  433.0 0.9 copy.33
  (42 shorter events, 5.4 us)
Async XLA Ops:
  107.1 84.5 %copy-start.18 = (f32[2,1536]{1,0:T(2,128)S(1)}, f32[2,1536]{1,0:T(2,128)}, u32[]{:S(2)}) copy-start(f32[2,1536]{1,0:T(2,128)} %get-tuple-element.63) | copy-start | bytes 36868
  192.2 101.1 %copy-start.2 = (f32[128,1536]{1,0:T(8,128)S(1)}, f32[128,1536]{1,0:T(8,128)}, u32[]{:S(2)}) copy-start(f32[128,1536]{1,0:T(8,128)} %get-tuple-element.62.middle_ref) | copy-start | bytes 2359300
  192.2 101.1 %copy-start.3 = (bf16[1,128,1536]{2,1,0:T(8,128)(2,1)S(1)}, bf16[1,128,1536]{2,1,0:T(8,128)(2,1)}, u32[]{:S(2)}) copy-start(bf16[1,128,1536]{2,1,0:T(8,128)(2,1)} %param.16) | copy-start | bytes 1179652
  192.2 101.1 %copy-start.4 = (bf16[128,1536]{1,0:T(8,128)(2,1)S(1)}, bf16[128,1536]{1,0:T(8,128)(2,1)}, u32[]{:S(2)}) copy-start(bf16[128,1536]{1,0:T(8,128)(2,1)} %get-tuple-element.68.normed_ref) | copy-start | bytes 1179652
  192.2 101.1 %copy-start.6 = (f32[128,128]{1,0:T(8,128)S(1)}, f32[128,128]{1,0:T(8,128)}, u32[]{:S(2)}) copy-start(f32[128,128]{1,0:T(8,128)} %get-tuple-element.102.cos_ref) | copy-start | bytes 196612
  192.2 101.1 %copy-start.7 = (f32[128,128]{1,0:T(8,128)S(1)}, f32[128,128]{1,0:T(8,128)}, u32[]{:S(2)}) copy-start(f32[128,128]{1,0:T(8,128)} %get-tuple-element.103.sin_ref) | copy-start | bytes 196612
  293.3 1.1 copy-start.8
  294.4 1.0 copy-start.9
  295.4 1.0 copy-start.10
  296.4 1.0 copy-start.13
  297.4 1.0 copy-start.14
  298.3 0.9 copy-start.15
  299.3 0.9 copy-start.16
  300.2 0.7 copy-start.17
  417.5 9.7 %copy-start.11 = (bf16[128,1536]{1,0:T(8,128)(2,1)}, bf16[128,1536]{1,0:T(8,128)(2,1)S(1)}, u32[]{:S(2)}) copy-start(bf16[128,1536]{1,0:T(8,128)(2,1)S(1)} %get-tuple-element.79) | copy-start | bytes 1179652
  417.5 3.2 copy-start
  420.7 6.5 %copy-start.1 = (bf16[2,2,288,1536]{3,2,1,0:T(8,128)(2,1)S(1)}, bf16[2,2,288,1536]{3,2,1,0:T(8,128)(2,1)}, u32[]{:S(2)}) copy-start(bf16[2,2,288,1536]{3,2,1,0:T(8,128)(2,1)} %get-tuple-element.82.dn_ref) | copy-start | bytes 10616836
  420.7 6.6 %copy-start.5 = (bf16[2,192,1792]{2,1,0:T(8,128)(2,1)S(1)}, bf16[2,192,1792]{2,1,0:T(8,128)(2,1)}, u32[]{:S(2)}) copy-start(bf16[2,192,1792]{2,1,0:T(8,128)(2,1)} %get-tuple-element.83.at_ref) | copy-start | bytes 4128772
  427.2 5.1 %copy-start.12 = (bf16[128,1536]{1,0:T(8,128)(2,1)S(1)}, bf16[128,1536]{1,0:T(8,128)(2,1)}, u32[]{:S(2)}) copy-start(bf16[128,1536]{1,0:T(8,128)(2,1)} %copy-done.11) | copy-start | bytes 1179652
